TPU v7x, 512 devices: a whole 4x8x8 slice. The times are simulated.
512 devices in a mesh: member: 16 (over x_lo, y), tile: 32 (over z, x_hi, core).
Axes of the slice: x: 4 (x_hi: 2, x_lo: 2; x = x_hi * 2 + x_lo), y: 8, z: 8, core: 2. Of those that a mesh axis runs over, the one named last changes fastest.
Arguments:
- density: float32 [16, 6, 512, 512], P('member', None, 'tile'), may hold values from 0.05 to 5
- scaling: float32 [16, 6, 512, 512], P('member', None, 'tile'), may hold values from 0.2 to 5
- member_weights: float32 [16], P('member'), may hold values from 0.5 to 11
- seams: int32 [3, 4, 6], replicated, may hold values from 0 to 5, as said below
Outputs:
- new_scaling: float32 [16, 6, 512, 512], P('member', None, 'tile')
- dual_scaling: float32 [16, 6, 512, 512], P('member', None, 'tile')
- barycenter: float32 [6, 512, 512], P(None, 'tile')
Inputs may be any that keep to these rules, and one draw needn't show every extreme that they name: Edges are numbered 0 first row, 1 last row, 2 first column, 3 last column. The table describes the six faces of a cube, each face's frame turned or mirrored: seams[0, e, f] is the face across edge e of face f, seams[1, e, f] the edge of that face which meets it, and the relation is symmetric; seams[2, e, f] is 1 where positions along the seam run opposite ways on the two faces, and the same from both sides.
All inputs are finite; a program needn't handle non-finite values.
Results may differ from a plain program's by a relative error of at most 0.00007.
Values sent between devices are 32-bit elements; how exact they have to be, the bound alone decides.
No kernel may reach another device: no remote copies, remote signals or barrier semaphores. Data moves between devices by JAX's collectives and lax.ppermute only.
A program may use at most 64 MiB of HBM per device.

v0:
```python
import jax
import jax.numpy as jnp
from jax import lax
from jax.sharding import PartitionSpec as P

STEPS = 4


KAPPA = 0.24


def with_halo(block, sides, width):
    for axis, dim in sides:
        count = lax.axis_size(axis)
        forward = [(i, i + 1) for i in range(count - 1)]
        backward = [(target, source) for source, target in forward]
        low = lax.ppermute(
            lax.slice_in_dim(block, block.shape[dim] - width, None, axis=dim), axis, forward
        )
        high = lax.ppermute(lax.slice_in_dim(block, 0, width, axis=dim), axis, backward)
        block = jnp.concatenate([low, block, high], axis=dim)
    return block


def body(density, scaling, member_weights, seams):
    tiles = lax.axis_size("tile")
    position = lax.axis_index("tile")
    members = scaling.shape[0]
    faces = scaling.shape[1]
    rows = scaling.shape[2]
    side = scaling.shape[3]
    is_first = (position == 0).astype(jnp.float32)
    is_last = (position == tiles - 1).astype(jnp.float32)
    slots = jnp.arange(4 * faces, dtype=jnp.int32)
    selectors = []
    for edge_id in range(4):
        wanted = seams[0, edge_id] * 4 + seams[1, edge_id]
        selectors.append((wanted[:, None] == slots[None, :]).astype(jnp.float32))

    def edge_table(field):
        first_row = field[:, :, 0, :] * is_first
        last_row = field[:, :, -1, :] * is_last
        empty = jnp.zeros((members, faces, 2, side), jnp.float32)
        column_pieces = jnp.stack([field[:, :, :, 0], field[:, :, :, -1]], axis=2)
        placed = lax.dynamic_update_slice_in_dim(empty, column_pieces, position * rows, 3)
        local = jnp.concatenate([jnp.stack([first_row, last_row], axis=2), placed], axis=2)
        return lax.psum(local, "tile")

    def ghost(table, edge_id):
        flat = table.reshape(members, faces * 4, side)
        taken = jnp.einsum("fq,mqn->mfn", selectors[edge_id], flat, precision=lax.Precision.HIGHEST)
        return jnp.where((seams[2, edge_id] == 1)[None, :, None], taken[..., ::-1], taken)

    def diffuse(field):
        widened = with_halo(field, (("tile", 2),), 1)
        table = edge_table(field)
        upper = ghost(table, 0)
        lower = ghost(table, 1)
        start = position * rows
        left = lax.dynamic_slice_in_dim(ghost(table, 2), start, rows, 2)
        right = lax.dynamic_slice_in_dim(ghost(table, 3), start, rows, 2)
        top_row = jnp.where(position == 0, upper, widened[:, :, 0, :])
        bottom_row = jnp.where(position == tiles - 1, lower, widened[:, :, -1, :])
        widened = jnp.concatenate(
            [top_row[:, :, None, :], field, bottom_row[:, :, None, :]], axis=2
        )
        vertical = widened[:, :, :-2, :] + widened[:, :, 2:, :]
        lateral = jnp.concatenate([left[..., None], field[..., :-1]], axis=3) + jnp.concatenate(
            [field[..., 1:], right[..., None]], axis=3
        )
        return field + KAPPA * (vertical + lateral - 4.0 * field)

    def kernel(field):
        for counter in range(STEPS):
            field = diffuse(field)
        return field

    dual_scaling = density / kernel(scaling)
    marginal = scaling * kernel(dual_scaling)
    log_marginal = jnp.log(marginal)
    weighted = jnp.einsum(
        "k,kfrc->frc", member_weights, log_marginal, precision=lax.Precision.HIGHEST
    )
    weight_local = jnp.sum(member_weights)
    summed, weight_sum = lax.psum((weighted, weight_local), "member")
    barycenter = jnp.exp(summed / weight_sum)
    new_scaling = scaling * barycenter[None] / marginal
    return (new_scaling, dual_scaling, barycenter)


def solution(mesh):
    return jax.shard_map(
        body,
        mesh=mesh,
        in_specs=(
            P("member", None, "tile", None),
            P("member", None, "tile", None),
            P("member"),
            P(),
        ),
        out_specs=(
            P("member", None, "tile", None),
            P("member", None, "tile", None),
            P(None, "tile", None),
        ),
        check_vma=False,
    )
```

profile of v0, /device:TPU:4, one launch (start us, length us, event | category | flops | bytes accessed | tf_op | source)
XLA Modules:
  0.0 1329.6 jit_solution(210642740823785259)
XLA Ops:
  8.4 1.9 collective-permute-start
  10.3 5.1 collective-permute-start.1
  17.0 131.4 %psum.70 = f32[24,512]{1,0:T(8,128)S(1)} all-reduce(f32[24,512]{1,0:T(8,128)S(1)} %reshape.773), channel_id=1, replica_groups=mesh['member'=16,'tile'=32] {'tile'}, use_global_device_ids=true, to_apply=%region_0.0 | all-reduce | flops 12288 | bytes 98304 | tf_op jit(solution)/shard_map/psum | solution.py:47
  153.3 127.9 %psum.71 = f32[24,512]{1,0:T(8,128)S(1)} all-reduce(f32[24,512]{1,0:T(8,128)S(1)} %reshape.774), channel_id=1, replica_groups=mesh['member'=16,'tile'=32] {'tile'}, use_global_device_ids=true, to_apply=%region_1.2 | all-reduce | flops 12288 | bytes 98304 | tf_op jit(solution)/shard_map/psum | solution.py:47
  283.8 5.1 collective-permute-start.3
  292.6 125.8 %psum.72 = f32[24,512]{1,0:T(8,128)S(1)} all-reduce(f32[24,512]{1,0:T(8,128)S(1)} %reshape.775), channel_id=1, replica_groups=mesh['member'=16,'tile'=32] {'tile'}, use_global_device_ids=true, to_apply=%region_2.3 | all-reduce | flops 12288 | bytes 98304 | tf_op jit(solution)/shard_map/psum | solution.py:47
  421.0 5.1 collective-permute-start.5
  429.8 125.8 %psum.73 = f32[24,512]{1,0:T(8,128)S(1)} all-reduce(f32[24,512]{1,0:T(8,128)S(1)} %reshape.776), channel_id=1, replica_groups=mesh['member'=16,'tile'=32] {'tile'}, use_global_device_ids=true, to_apply=%region_3.4 | all-reduce | flops 12288 | bytes 98304 | tf_op jit(solution)/shard_map/psum | solution.py:47
  558.2 5.1 collective-permute-start.7
  567.1 130.9 %psum.74 = f32[24,512]{1,0:T(8,128)S(1)} all-reduce(f32[24,512]{1,0:T(8,128)S(1)} %reshape.777), channel_id=1, replica_groups=mesh['member'=16,'tile'=32] {'tile'}, use_global_device_ids=true, to_apply=%region_4.5 | all-reduce | flops 12288 | bytes 98304 | tf_op jit(solution)/shard_map/psum | solution.py:47
  698.8 3.8 collective-permute-start.8
  702.6 3.3 collective-permute-start.9
  707.7 2.1 collective-permute-done.9
  711.6 133.7 %psum.75 = f32[24,512]{1,0:T(8,128)S(1)} all-reduce(f32[24,512]{1,0:T(8,128)S(1)} %reshape.778), channel_id=1, replica_groups=mesh['member'=16,'tile'=32] {'tile'}, use_global_device_ids=true, to_apply=%region_5.6 | all-reduce | flops 12288 | bytes 98304 | tf_op jit(solution)/shard_map/psum | solution.py:47
  846.0 3.5 collective-permute-start.10
  849.5 3.6 collective-permute-start.11
  858.6 133.7 %psum.76 = f32[24,512]{1,0:T(8,128)S(1)} all-reduce(f32[24,512]{1,0:T(8,128)S(1)} %reshape.779), channel_id=1, replica_groups=mesh['member'=16,'tile'=32] {'tile'}, use_global_device_ids=true, to_apply=%region_6.7 | all-reduce | flops 12288 | bytes 98304 | tf_op jit(solution)/shard_map/psum | solution.py:47
  993.0 3.5 collective-permute-start.12
  996.5 3.7 collective-permute-start.13
  1005.5 133.7 %psum.77 = f32[24,512]{1,0:T(8,128)S(1)} all-reduce(f32[24,512]{1,0:T(8,128)S(1)} %reshape.780), channel_id=1, replica_groups=mesh['member'=16,'tile'=32] {'tile'}, use_global_device_ids=true, to_apply=%region_7.8 | all-reduce | flops 12288 | bytes 98304 | tf_op jit(solution)/shard_map/psum | solution.py:47
  1139.9 3.5 collective-permute-start.14
  1143.5 3.6 collective-permute-start.15
  1151.8 36.2 %psum.79 = f32[]{:T(128)} all-reduce(f32[]{:T(128)} %bitcast.118), channel_id=1, replica_groups=mesh['member'=16,'tile'=32] {'member'}, use_global_device_ids=true, to_apply=%region_9.10 | all-reduce | flops 1 | bytes 8 | tf_op jit(solution)/shard_map/psum | solution.py:85
  1188.8 130.6 %all-reduce.2.cloned.1.call-done = f32[6,16,512]{2,0,1:T(8,128)} async-done(((f32[6,16,512]{2,0,1:T(8,128)}), f32[6,16,512]{2,0,1:T(8,128)}) %all-reduce.2.cloned.1.call-update) | async-done | bytes 196624 | tf_op jit(solution)/shard_map/psum | solution.py:85
  (264 shorter events, 51.1 us)
Async XLA Ops:
  7.2 1312.2 %all-reduce.2.cloned.1.call-start = ((), (), s32[]{:S(2)}) async-start(), calls=%async_computation | async-start | bytes 524288 | tf_op jit(solution)/shard_map/psum | solution.py:85
  7.2 8.3 copy-start
  8.3 7.1 copy-start.2
  8.4 143.0 %collective-permute-start = (f32[1,6,1,512]{3,1,2,0:T(8,128)S(1)}, f32[1,6,1,512]{3,1,2,0:T(8,128)S(1)}, u32[]{:S(2)}, u32[]{:S(2)}) collective-permute-start(f32[1,6,1,512]{3,1,2,0:T(8,128)S(1)} %get-tuple-element.73), channel_id=1, source_target_pairs={{0,1},{1,2},{2,3},{3,4},{4,5},{5,6},{6,7},{7,8},{8,9},{9,10},{10,1... | collective-permute-start | bytes 36872 | tf_op jit(solution)/shard_map/ppermute | solution.py:17
  10.3 141.2 %collective-permute-start.1 = (f32[1,6,1,512]{3,1,2,0:T(8,128)S(1)}, f32[1,6,1,512]{3,1,2,0:T(8,128)S(1)}, u32[]{:S(2)}, u32[]{:S(2)}) collective-permute-start(f32[1,6,1,512]{3,1,2,0:T(8,128)S(1)} %get-tuple-element.76), channel_id=1, source_target_pairs={{1,0},{2,1},{3,2},{4,3},{5,4},{6,5},{7,6},{8,7},{9,8},{10,9},{11,1... | collective-permute-start | bytes 36872 | tf_op jit(solution)/shard_map/ppermute | solution.py:20
  281.9 8.8 collective-permute-start.2
  283.8 7.0 collective-permute-start.3
  419.1 8.8 collective-permute-start.4
  421.0 7.0 collective-permute-start.5
  556.3 8.9 collective-permute-start.6
  558.2 7.0 collective-permute-start.7
  564.1 1.2 copy-start.1
  698.8 8.8 collective-permute-start.8
  702.6 7.3 collective-permute-start.9
  846.0 8.8 collective-permute-start.10
  849.5 7.3 collective-permute-start.11
  993.0 9.0 collective-permute-start.12
  996.5 7.3 collective-permute-start.13
  1139.9 8.8 collective-permute-start.14
  1143.5 7.3 collective-permute-start.15
Sparse Core Ops, SparseCore 0:
  1151.9 167.4 all-reduce.1
where the time goes:
time: 1330 us
  blocking collectives  1080 us (81%)
  waiting for transfers between devices  138 us (10%)
  starting transfers between devices  56.8 us (4%)
  local copies, waits for them, and re-layouts  27 us (2%)
  between operations  15.7 us (1%)
    psum x8, blocking collectives, edge_table(): return lax.psum(local, 'tile')  1040 us
    psum x1, waiting for transfers between devices, body(): summed, weight_sum = lax.psum((weighted, weight_local), 'member')  131 us
    psum x1, blocking collectives, body(): summed, weight_sum = lax.psum((weighted, weight_local), 'member')  36.2 us
    ppermute x8, starting transfers between devices, with_halo(): lax.ppermute(lax.slice_in_dim(block, 0, width, axis=dim), axis, backward)  34.7 us
  transfers between devices with their start and end apart: 17, of which 5 were waited for; matrix products, arithmetic and copies ran while one was open for 1% of the time, Pallas kernels for 0%

commit v1 on v0

v1 whole, which is shorter than its diff:
```python
import jax
import jax.numpy as jnp
from jax import lax
from jax.experimental import pallas as pl
from jax.experimental.pallas import tpu as pltpu
from jax.sharding import PartitionSpec as P

KAPPA = 0.24
STEPS = 4
FACES = 6
ROWS = 16
SIDE = 512
HALO = 8
TALL = ROWS + 2 * HALO
WIDE = SIDE + 128
HIGH = lax.Precision.HIGHEST


def iota(shape, dim):
    return lax.broadcasted_iota(jnp.int32, shape, dim)


def reverse_lanes(x):
    index = 127 - iota((8, 128), 1)
    tiles = [
        jnp.take_along_axis(x[:, at : at + 128], index, axis=1)
        for at in range(0, x.shape[1], 128)
    ]
    return jnp.concatenate(tiles[::-1], axis=1) if len(tiles) > 1 else tiles[0]


def column_strips(first, last):
    strips = None
    for g in range(FACES):
        a, b = first(g), last(g)
        lane = iota(a.shape, 1)
        moved = pltpu.roll(jnp.where(lane >= 64, b, a), 16 * g + 8, 1)
        strips = moved if strips is None else jnp.where(lane >= 16 * g, moved, strips)
    return strips


def spread(block):
    return [pltpu.roll(block, 96 - 32 * b, 1) for b in range(3)]


def unspread(b0, b1, b2):
    lane = iota((8, 128), 1)
    return jnp.where(
        lane < 32, pltpu.roll(b0, 32, 1), jnp.where(lane < 64, pltpu.roll(b1, 64, 1), pltpu.roll(b2, 96, 1))
    )


def pack_kernel(place, seams, scaling, density, up, down, message):
    p = place[0]
    count = message.shape[0]
    lane = iota((8, 128), 1)
    sub = iota((8, 128), 0)
    for g in range(FACES):
        up[g] = scaling[g, HALO:]
        up[FACES + g] = density[g, HALO:]
        down[g] = scaling[g, :HALO]
        down[FACES + g] = density[g, :HALO]
    vs = column_strips(lambda g: scaling[g, :, :128], lambda g: scaling[g, :, SIDE - 128 :])
    vd = column_strips(lambda g: density[g, :, :128], lambda g: density[g, :, SIDE - 128 :])
    tail = spread(vd[8:])
    head = (vs[:8], vs[8:], vd[:8])
    block = jnp.concatenate([jnp.where(lane < 96, head[b], tail[b]) for b in range(3)], axis=0)
    is_last = p == count - 1
    is_edge = (p == 0) | is_last

    @pl.when(jnp.logical_not(is_edge))
    def _():
        for q in range(count):
            message[q] = block

    @pl.when(is_edge)
    def _():
        message[0] = block
        message[count - 1] = block
        e = is_last.astype(jnp.int32)
        base = pl.multiple_of(e * 8, 8)
        own_s = jnp.where(is_last, vs[:8], vs[8:])
        own_d = jnp.where(is_last, vd[:8], vd[8:])
        far = jnp.where(is_last, pltpu.roll(own_d, 5, 0), pltpu.roll(own_d, 3, 0))
        free = jnp.where(is_last, (sub >= 5).astype(jnp.int32), (sub <= 2).astype(jnp.int32)) == 1
        lane16 = lane % 16
        coded = jnp.where(
            free & (lane16 < 4),
            pltpu.roll(far, 124, 1),
            jnp.where(free & (lane16 >= 12), pltpu.roll(far, 4, 1), own_s),
        )
        extra = spread(coded)
        pieces = []
        for g in range(FACES):
            turned = seams[2, e, g] == 1
            s = scaling[g, pl.ds(base, 8), :]
            d = density[g, pl.ds(base, 8), :]
            pieces.append((jnp.where(turned, reverse_lanes(s), s), jnp.where(turned, reverse_lanes(d), d)))
        sub_wide = iota((8, SIDE), 0)
        lane_wide = iota((8, SIDE), 1) % 128
        blocks = []
        for b in range(3):
            (s0, d0), (s1, d1) = pieces[2 * b], pieces[2 * b + 1]
            low = jnp.where(is_last, pltpu.roll(d0, 4, 0), d0)
            high = jnp.where(is_last, d1, pltpu.roll(d1, 4, 0))
            blocks.append((s0, s1, jnp.where(sub_wide < 4, low, high)))
        for t in range(3):
            tail_t = jnp.concatenate([extra[t]] * 4, axis=1)
            for r in range(8):
                moved = [pltpu.roll(blocks[b][t], (32 * b - 16 * r + 8) % SIDE, 1) for b in range(3)]
                full = jnp.where(
                    lane_wide < 32,
                    moved[0],
                    jnp.where(lane_wide < 64, moved[1], jnp.where(lane_wide < 96, moved[2], tail_t)),
                )
                for a in range(4):
                    q = 8 * a + r
                    if 0 < q < count - 1:
                        message[q, 8 * t : 8 * t + 8, :] = full[:, 128 * a : 128 * a + 128]


def step(x, where):
    above = pltpu.roll(x, 1, 0)
    below = pltpu.roll(x, TALL - 1, 0)
    left = pltpu.roll(x, 1, 1)
    right = pltpu.roll(x, WIDE - 1, 1)
    if where is not None:
        lane = iota((8, 128), 1)
        sub = iota((8, 128), 0)
        if where == "first":
            at, edge, depth = 0, 8, 7 - sub
        else:
            at, edge, depth = 24, 23, sub
        rows = x[at : at + 8]
        line = jnp.broadcast_to(x[edge : edge + 1, SIDE:], (8, 128))
        on_left = lane == 127 - depth
        on_right = lane == depth
        from_left = jnp.sum(jnp.where(on_left, line, 0.0), axis=1, keepdims=True)
        from_right = jnp.sum(jnp.where(on_right, line, 0.0), axis=1, keepdims=True)
        columns = jnp.where(
            on_left, rows[:, :1], jnp.where(on_right, rows[:, SIDE - 1 : SIDE], 0.0)
        )
        across = jnp.sum(columns, axis=0, keepdims=True)
        fixed_left = jnp.concatenate(
            [jnp.where(lane == 0, from_left, left[at : at + 8, :128]), left[at : at + 8, 128:]], axis=1
        )
        fixed_right = jnp.concatenate(
            [
                right[at : at + 8, : SIDE - 128],
                jnp.where(lane == 127, from_right, right[at : at + 8, SIDE - 128 : SIDE]),
                right[at : at + 8, SIDE:],
            ],
            axis=1,
        )
        ghost = (lane < 8) | (lane >= 120)
        if where == "first":
            left = jnp.concatenate([fixed_left, left[8:]], axis=0)
            right = jnp.concatenate([fixed_right, right[8:]], axis=0)
            tile = jnp.where(ghost & (sub == 0), across, above[8:16, SIDE:])
            tile = jnp.concatenate([above[:8, SIDE:], tile, above[16:, SIDE:]], axis=0)
            above = jnp.concatenate([above[:, :SIDE], tile], axis=1)
        else:
            left = jnp.concatenate([left[:24], fixed_left], axis=0)
            right = jnp.concatenate([right[:24], fixed_right], axis=0)
            tile = jnp.where(ghost & (sub == 7), across, below[16:24, SIDE:])
            tile = jnp.concatenate([below[:16, SIDE:], tile, below[24:, SIDE:]], axis=0)
            below = jnp.concatenate([below[:, :SIDE], tile], axis=1)
    return x + KAPPA * (((above + below) + (left + right)) - 4.0 * x)


def heat_kernel(
    place, seams, weight, scaling, density, up, down, message, dual, marginal, weighted,
    xs, xd, mixed, chunk, all_s, all_d, lines_s, lines_d,
):
    q = place[0]
    count = message.shape[0]
    last = count - 1
    members = weighted.shape[0]
    per = 48 // members
    lane = iota((8, 128), 1)
    sub = iota((8, 128), 0)
    for g in range(FACES):
        for x, field, at in ((xs, scaling, 0), (xd, density, FACES)):
            x[g, :HALO, :SIDE] = up[at + g]
            x[g, HALO : HALO + ROWS, :SIDE] = field[g]
            x[g, HALO + ROWS :, :SIDE] = down[at + g]

    def far_rows(p):
        return unspread(
            message[p, :8, :], message[p, 8:16, :], message[p, 16:24, :]
        )

    mixed[:TALL, :128] = column_strips(lambda g: xs[g, :, :128], lambda g: xs[g, :, SIDE - 128 : SIDE])
    mixed[TALL:, :128] = column_strips(lambda g: xd[g, :, :128], lambda g: xd[g, :, SIDE - 128 : SIDE])

    main, upper, lower = last - q, jnp.minimum(last + 1 - q, last), jnp.maximum(last - 1 - q, 0)
    source = jnp.where(q == 1, last, 0)
    coded = far_rows(source)
    near = jnp.where(q == 1, pltpu.roll(coded, 3, 0), pltpu.roll(coded, 5, 0))
    coded_d = jnp.where(lane % 16 < 8, pltpu.roll(near, 4, 1), pltpu.roll(near, 124, 1))
    parts_s = (
        jnp.where(q == last - 1, coded, message[lower, 8:16, :]),
        message[main, :8, :],
        message[main, 8:16, :],
        jnp.where(q == 1, coded, message[upper, :8, :]),
    )
    parts_d = (
        jnp.where(q == last - 1, coded_d, far_rows(lower)),
        message[main, 16:24, :],
        far_rows(main),
        jnp.where(q == 1, coded_d, message[upper, 16:24, :]),
    )
    for base, parts in ((0, parts_s), (TALL, parts_d)):
        for block in range(4):
            for i in range(8):
                at = base + TALL - 1 - 8 * block - i
                mixed[at : at + 1, 128:256] = parts[block][i : i + 1]

    chunk[...] = jnp.zeros_like(chunk)
    is_edge = (q == 0) | (q == last)

    @pl.when(jnp.logical_not(is_edge))
    def _():
        for e in range(2):
            p = e * last
            for g in range(FACES):
                b, h = g // 2, g % 2
                turn = (128 - 32 * b) % 128
                s = message[p, 8 * h : 8 * h + 8, :]
                d = message[p, 16:24, :]
                if turn:
                    s, d = pltpu.roll(s, turn, 1), pltpu.roll(d, turn, 1)
                if h != e:
                    d = pltpu.roll(d, 4, 0)
                at = 48 * e + 8 * g
                chunk[0, at : at + 8, :] = s
                chunk[1, at : at + 8, :] = d

    for is_first in (True, False):

        @pl.when(q == (0 if is_first else last))
        def _():
            for k, (lines, field) in enumerate(((lines_s, scaling), (lines_d, density))):
                for e in range(2):
                    for g in range(FACES):
                        if is_first:
                            rows = field[g, :HALO] if e == 0 else up[FACES * k + g]
                        else:
                            rows = down[FACES * k + g] if e == 0 else field[g, HALO:]
                        at = 48 * e + 8 * g
                        lines[at : at + 8, :] = rows
                        turned = seams[2, e, g] == 1
                        a, b = rows[:, :128], rows[:, SIDE - 128 :]
                        if is_first:
                            piece = pltpu.roll(jnp.where(turned, reverse_lanes(b), a), 8, 1)
                        else:
                            piece = pltpu.roll(jnp.where(turned, reverse_lanes(a), b), 24, 1)
                        chunk[k, at : at + 8, :] = piece

    for k in range(2):
        mixed[k * TALL : (k + 1) * TALL, 256:] = jnp.transpose(chunk[k])[:TALL]

    target = iota((1, 128), 1)
    wanted = jnp.full((1, 128), -1, jnp.int32)
    for f in range(FACES):
        for e in (2, 3):
            g, meets, turned = seams[0, e, f], seams[1, e, f], seams[2, e, f]
            start = jnp.where(
                meets >= 2,
                128 * turned + 16 * g + jnp.where(meets == 2, 8, 0),
                256 + 48 * meets + 8 * g,
            )
            at = 16 * f + (0 if e == 2 else 8)
            depth = at + 7 - target if e == 2 else target - at
            rising = (meets % 2) == 0
            index = start + jnp.where(rising, depth, 7 - depth)
            wanted = jnp.where((target >= at) & (target < at + 8), index, wanted)
    choice = (iota((384, 128), 0) == wanted).astype(jnp.float32)
    ghosts = jnp.dot(mixed[...], choice, precision=HIGH, preferred_element_type=jnp.float32)
    for f in range(FACES):
        turn = 120 - 16 * f
        xs[f, :, SIDE:] = pltpu.roll(ghosts[:TALL], turn, 1)
        xd[f, :, SIDE:] = pltpu.roll(ghosts[TALL:], turn, 1)

    for is_first in (True, False):

        @pl.when(q == (0 if is_first else last))
        def _():
            def gather(p, carry):
                at = pl.multiple_of(16 * p, 16)
                all_s[pl.ds(at, 16), :] = message[p, :16, :]
                all_d[pl.ds(at, 8), :] = message[p, 16:24, :]
                all_d[pl.ds(at + 8, 8), :] = far_rows(p)
                return carry

            lax.fori_loop(0, count, gather, 0)
            e = 0 if is_first else 1
            of_columns, of_lines = [], []
            for f in range(FACES):
                g, meets = seams[0, e, f], seams[1, e, f]
                depth = 7 - sub if is_first else sub
                rising = (meets % 2) == 0
                index = jnp.where(rising, depth, 7 - depth)
                column_at = jnp.where(meets >= 2, 16 * g + jnp.where(meets == 2, 8, 0), -1000)
                line_at = jnp.where(meets < 2, 48 * meets + 8 * g, -1000)
                of_columns.append((lane == column_at + index).astype(jnp.float32))
                of_lines.append((lane == line_at + index).astype(jnp.float32))
            of_columns = jnp.concatenate(of_columns, axis=0)
            of_lines = jnp.concatenate(of_lines, axis=0)[:, :96]
            for x, columns, lines in ((xs, all_s, lines_s), (xd, all_d, lines_d)):
                taken = lax.dot_general(
                    of_columns, columns[...], (((1,), (1,)), ((), ())),
                    precision=HIGH, preferred_element_type=jnp.float32,
                ) + jnp.dot(of_lines, lines[...], precision=HIGH, preferred_element_type=jnp.float32)
                for f in range(FACES):
                    piece = taken[8 * f : 8 * f + 8]
                    piece = jnp.where(seams[2, e, f] == 1, reverse_lanes(piece), piece)
                    at = 0 if is_first else HALO + ROWS
                    x[f, at : at + 8, :SIDE] = piece

    share = weight[0]
    for k in range(members):
        weighted[k, 8 * per :, :] = jnp.full((8, 128), share, jnp.float32)

    def run(where):
        def face(f, carry):
            x = xs[f]
            for _ in range(STEPS):
                x = step(x, where)
            y = xd[f] / x
            dual[f] = y[HALO : HALO + ROWS, :SIDE]
            for _ in range(STEPS):
                y = step(y, where)
            m = scaling[f] * y[HALO : HALO + ROWS, :SIDE]
            marginal[f] = m
            scaled = share * jnp.log(m)
            for i in range(2):
                for j in range(4):
                    t = 8 * f + 4 * i + j
                    at = pl.multiple_of(8 * lax.rem(t, per), 8)
                    weighted[lax.div(t, per), pl.ds(at, 8), :] = scaled[8 * i : 8 * i + 8, 128 * j : 128 * j + 128]
            return carry

        lax.fori_loop(0, FACES, face, 0)

    @pl.when(q == 0)
    def _():
        run("first")

    @pl.when(q == last)
    def _():
        run("last")

    @pl.when(jnp.logical_not(is_edge))
    def _():
        run(None)


def mean_kernel(parts, result):
    members, rows = result.shape[0], result.shape[1]
    total = parts[0]
    for k in range(1, members):
        total = total + parts[k]
    mean = total[:rows] / total[rows : rows + 1]
    value = jnp.exp(mean)
    for k in range(members):
        result[k] = value


def update_kernel(parts, scaling, marginal, fresh, barycenter):
    members = parts.shape[0]
    per = 48 // members
    for f in range(FACES):
        for i in range(2):
            for j in range(4):
                t = 8 * f + 4 * i + j
                at = 8 * (t % per)
                value = parts[t // per, at : at + 8, :]
                rows, columns = slice(8 * i, 8 * i + 8), slice(128 * j, 128 * j + 128)
                barycenter[f, rows, columns] = value
                fresh[f, rows, columns] = scaling[f, rows, columns] * value / marginal[f, rows, columns]


def body(density, scaling, member_weights, seams):
    tiles = lax.axis_size("tile")
    members = lax.axis_size("member")
    scaling = scaling[0]
    density = density[0]
    place = lax.axis_index("tile").astype(jnp.int32).reshape(1)
    f32 = jnp.float32
    vmem = pl.BlockSpec(memory_space=pltpu.VMEM)
    smem = pl.BlockSpec(memory_space=pltpu.SMEM)
    field = jax.ShapeDtypeStruct((FACES, ROWS, SIDE), f32)
    edge_rows = jax.ShapeDtypeStruct((2 * FACES, HALO, SIDE), f32)
    params = pltpu.CompilerParams(vmem_limit_bytes=24 * 1024 * 1024)
    up, down, message = pl.pallas_call(
        pack_kernel,
        out_shape=(edge_rows, edge_rows, jax.ShapeDtypeStruct((tiles, 24, 128), f32)),
        in_specs=[smem, smem, vmem, vmem],
        out_specs=(vmem, vmem, vmem),
        compiler_params=params,
        name="pack",
    )(place, seams, scaling, density)
    onward = [(i, (i + 1) % tiles) for i in range(tiles)]
    back = [(b, a) for a, b in onward]
    up = lax.ppermute(up, "tile", onward)
    down = lax.ppermute(down, "tile", back)
    message = lax.all_to_all(message, "tile", 0, 0)
    rows = 384 // members
    dual, marginal, weighted = pl.pallas_call(
        heat_kernel,
        out_shape=(field, field, jax.ShapeDtypeStruct((members, rows + 8, 128), f32)),
        in_specs=[smem, smem, smem] + [vmem] * 5,
        out_specs=(vmem, vmem, vmem),
        scratch_shapes=[
            pltpu.VMEM((FACES, TALL, WIDE), f32),
            pltpu.VMEM((FACES, TALL, WIDE), f32),
            pltpu.VMEM((2 * TALL, 384), f32),
            pltpu.VMEM((2, 128, 128), f32),
            pltpu.VMEM((SIDE, 128), f32),
            pltpu.VMEM((SIDE, 128), f32),
            pltpu.VMEM((96, SIDE), f32),
            pltpu.VMEM((96, SIDE), f32),
        ],
        compiler_params=params,
        name="heat",
    )(place, seams, member_weights, scaling, density, up, down, message)
    weighted = lax.all_to_all(weighted, "member", 0, 0)
    means = pl.pallas_call(
        mean_kernel,
        out_shape=jax.ShapeDtypeStruct((members, rows, 128), f32),
        in_specs=[vmem],
        out_specs=vmem,
        compiler_params=params,
        name="mean",
    )(weighted)
    means = lax.all_to_all(means, "member", 0, 0)
    fresh, barycenter = pl.pallas_call(
        update_kernel,
        out_shape=(field, field),
        in_specs=[vmem] * 3,
        out_specs=(vmem, vmem),
        compiler_params=params,
        name="update",
    )(means, scaling, marginal)
    return (fresh[None], dual[None], barycenter)


def solution(mesh):
    return jax.shard_map(
        body,
        mesh=mesh,
        in_specs=(
            P("member", None, "tile", None),
            P("member", None, "tile", None),
            P("member"),
            P(),
        ),
        out_specs=(
            P("member", None, "tile", None),
            P("member", None, "tile", None),
            P(None, "tile", None),
        ),
        check_vma=False,
    )
```

time: 1330 us -> 76.6 us (0.06)
  the two profiles are of different devices: /device:TPU:4 before, /device:TPU:8 now
where the time goes in v1:
time: 76.6 us; the launch traced here: 76.2 us
  blocking collectives  28.9 us (38%)
  starting transfers between devices  22 us (29%)
  Pallas kernels  14.2 us (19%)
  waiting for transfers between devices  7.11 us (9%)
  local copies, waits for them, and re-layouts  2.54 us (3%)
  between operations  1.34 us (2%)
    all_to_all x1, blocking collectives, body(): weighted = lax.all_to_all(weighted, 'member', 0, 0)  16.4 us
    all_to_all x1, starting transfers between devices, body(): message = lax.all_to_all(message, 'tile', 0, 0)  12.9 us
    all_to_all x1, blocking collectives, body(): means = lax.all_to_all(means, 'member', 0, 0)  12.5 us
    pallas_call x1, Pallas kernels, body(): pl.pallas_call(heat_kernel, out_shape=(field, field, jax.ShapeDtypeStruct...  11.4 us
    ppermute x1, waiting for transfers between devices, body(): up = lax.ppermute(up, 'tile', onward)  7.1 us
    ppermute x1, starting transfers between devices, body(): down = lax.ppermute(down, 'tile', back)  6.99 us
    unnamed x10, local copies, waits for them, and re-layouts  2.54 us
    ppermute x1, starting transfers between devices, body(): up = lax.ppermute(up, 'tile', onward)  2.18 us
  transfers between devices with their start and end apart: 3, of which 1 were waited for; matrix products, arithmetic and copies ran while one was open for 0% of the time, Pallas kernels for 0%

profile of v1, /device:TPU:8, one launch (start us, length us, event | category | flops | bytes accessed | tf_op | source)
XLA Modules:
  0.0 76.2 jit_solution(18166394647033338423)
XLA Ops:
  0.6 0.0 copy-start.4
  0.6 0.7 copy-done.4
  1.3 0.0 copy-start
  1.3 0.9 %copy-done = f32[1,6,16,512]{3,2,1,0:T(8,128)S(1)} copy-done((f32[1,6,16,512]{3,2,1,0:T(8,128)S(1)}, f32[1,6,16,512]{3,2,1,0:T(8,128)}, u32[]{:S(2)}) %copy-start) | copy-done | bytes 196632
  2.2 0.0 copy-start.2
  2.3 0.9 %copy-done.2 = f32[1,6,16,512]{3,2,1,0:T(8,128)S(1)} copy-done((f32[1,6,16,512]{3,2,1,0:T(8,128)S(1)}, f32[1,6,16,512]{3,2,1,0:T(8,128)}, u32[]{:S(2)}) %copy-start.2) | copy-done | bytes 196632
  3.2 2.0 %pack.1 = (f32[12,8,512]{2,1,0:T(8,128)S(1)}, f32[12,8,512]{2,1,0:T(8,128)S(1)}, f32[32,24,128]{2,1,0:T(8,128)}) custom-call(s32[1]{0:T(128)} %bitcast.place, s32[3,4,6]{2,1,0:T(4,128)S(1)} %copy-done.4, f32[6,16,512]{2,1,0:T(8,128)S(1)} %bitcast.5, f32[6,16,512]{2,1,0:T(8,128)S(1)} %bitcast.8), custom_call_target="tpu_custom_call" | custom-call | tf_op jit(solution)/shard_map/pack/pallas_call | solution.py:396
  5.2 0.0 copy-start.1
  5.2 0.0 copy-start.3
  5.2 12.9 %all-to-all-start = ((f32[32,24,128]{2,1,0:T(8,128)}), f32[32,24,128]{2,1,0:T(8,128)S(1)}, u32[]{:S(2)}, u32[]{:S(2)}) async-start(f32[32,24,128]{2,1,0:T(8,128)} %get-tuple-element.13), calls=%async_computation | async-start | bytes 786432 | tf_op jit(solution)/shard_map/all_to_all | solution.py:408
  18.0 2.2 %collective-permute-start = (f32[12,8,512]{2,1,0:T(8,128)S(1)}, f32[12,8,512]{2,1,0:T(8,128)S(1)}, u32[]{:S(2)}, u32[]{:S(2)}) collective-permute-start(f32[12,8,512]{2,1,0:T(8,128)S(1)} %get-tuple-element.11), channel_id=1, source_target_pairs={{0,1},{1,2},{2,3},{3,4},{4,5},{5,6},{6,7},{7,8},{8,9},{9,10},{10,1... | collective-permute-start | bytes 589832 | tf_op jit(solution)/shard_map/ppermute | solution.py:406
  20.2 7.0 %collective-permute-start.1 = (f32[12,8,512]{2,1,0:T(8,128)S(1)}, f32[12,8,512]{2,1,0:T(8,128)S(1)}, u32[]{:S(2)}, u32[]{:S(2)}) collective-permute-start(f32[12,8,512]{2,1,0:T(8,128)S(1)} %get-tuple-element.12), channel_id=1, source_target_pairs={{1,0},{2,1},{3,2},{4,3},{5,4},{6,5},{7,6},{8,7},{9,8},{10,9},{11,1... | collective-permute-start | bytes 589832 | tf_op jit(solution)/shard_map/ppermute | solution.py:407
  27.9 7.1 %collective-permute-done.up = f32[12,8,512]{2,1,0:T(8,128)S(1)} collective-permute-done((f32[12,8,512]{2,1,0:T(8,128)S(1)}, f32[12,8,512]{2,1,0:T(8,128)S(1)}, u32[]{:S(2)}, u32[]{:S(2)}) %collective-permute-start) | collective-permute-done | bytes 196640 | tf_op jit(solution)/shard_map/ppermute | solution.py:406
  35.0 0.0 collective-permute-done.1.down
  35.0 0.0 all-to-all-done.message
  35.0 0.0 copy-done.1
  35.0 0.0 copy-done.3
  35.0 11.4 %heat.1 = (f32[6,16,512]{2,1,0:T(8,128)}, f32[6,16,512]{2,1,0:T(8,128)S(1)}, f32[16,32,128]{2,1,0:T(8,128)S(1)}) custom-call(s32[1]{0:T(128)} %bitcast.place, s32[3,4,6]{2,1,0:T(4,128)S(1)} %copy-done.4, f32[1]{0:T(128)S(6)} %copy.7.weight, f32[6,16,512]{2,1,0:T(8,128)S(1)} %bitcast.6, f32[6,16,512]{2,1,0:T(8,128)S(1)} %bitcast.9, ...), custom_call_target="tpu_custom_call" | custom-call | tf_op jit(solution)/shard_map/heat/pallas_call | solution.py:410
  46.4 16.4 %all_to_all.15.parts = f32[16,32,128]{2,1,0:T(8,128)S(1)} all-to-all(f32[16,32,128]{2,1,0:T(8,128)S(1)} %get-tuple-element.14), channel_id=1, replica_groups=mesh['member'=16,'tile'=32] {'member'}, dimensions={0} | all-to-all | bytes 524288 | tf_op jit(solution)/shard_map/all_to_all | solution.py:428
  62.9 12.5 %all_to_all.16.parts = f32[16,24,128]{2,1,0:T(8,128)S(1)} all-to-all(f32[16,24,128]{2,1,0:T(8,128)S(1)} %mean.1), channel_id=1, replica_groups=mesh['member'=16,'tile'=32] {'member'}, dimensions={0} | all-to-all | bytes 393216 | tf_op jit(solution)/shard_map/all_to_all | solution.py:437
  75.4 0.8 %update.1 = (f32[6,16,512]{2,1,0:T(8,128)}, f32[6,16,512]{2,1,0:T(8,128)}) custom-call(f32[16,24,128]{2,1,0:T(8,128)S(1)} %all_to_all.16.parts, f32[6,16,512]{2,1,0:T(8,128)S(1)} %bitcast.7, f32[6,16,512]{2,1,0:T(8,128)S(1)} %get-tuple-element.15.marginal), custom_call_target="tpu_custom_call" | custom-call | tf_op jit(solution)/shard_map/update/pallas_call | solution.py:438
  (1 shorter events, 0.0 us)
Async XLA Ops:
  0.6 0.7 copy-start.4
  1.3 0.9 %copy-start = (f32[1,6,16,512]{3,2,1,0:T(8,128)S(1)}, f32[1,6,16,512]{3,2,1,0:T(8,128)}, u32[]{:S(2)}) copy-start(f32[1,6,16,512]{3,2,1,0:T(8,128)} %param.5) | copy-start | bytes 589828
  2.2 0.9 %copy-start.2 = (f32[1,6,16,512]{3,2,1,0:T(8,128)S(1)}, f32[1,6,16,512]{3,2,1,0:T(8,128)}, u32[]{:S(2)}) copy-start(f32[1,6,16,512]{3,2,1,0:T(8,128)} %param.4) | copy-start | bytes 589828
  5.2 29.8 %copy-start.1 = (f32[1,6,16,512]{3,2,1,0:T(8,128)S(1)}, f32[1,6,16,512]{3,2,1,0:T(8,128)}, u32[]{:S(2)}) copy-start(f32[1,6,16,512]{3,2,1,0:T(8,128)} %param.5) | copy-start | bytes 589828
  5.2 29.8 %copy-start.3 = (f32[1,6,16,512]{3,2,1,0:T(8,128)S(1)}, f32[1,6,16,512]{3,2,1,0:T(8,128)}, u32[]{:S(2)}) copy-start(f32[1,6,16,512]{3,2,1,0:T(8,128)} %param.4) | copy-start | bytes 589828
  5.2 29.8 %all-to-all-start = ((f32[32,24,128]{2,1,0:T(8,128)}), f32[32,24,128]{2,1,0:T(8,128)S(1)}, u32[]{:S(2)}, u32[]{:S(2)}) async-start(f32[32,24,128]{2,1,0:T(8,128)} %get-tuple-element.13), calls=%async_computation | async-start | bytes 786432 | tf_op jit(solution)/shard_map/all_to_all | solution.py:408
  18.0 16.9 %collective-permute-start = (f32[12,8,512]{2,1,0:T(8,128)S(1)}, f32[12,8,512]{2,1,0:T(8,128)S(1)}, u32[]{:S(2)}, u32[]{:S(2)}) collective-permute-start(f32[12,8,512]{2,1,0:T(8,128)S(1)} %get-tuple-element.11), channel_id=1, source_target_pairs={{0,1},{1,2},{2,3},{3,4},{4,5},{5,6},{6,7},{7,8},{8,9},{9,10},{10,1... | collective-permute-start | bytes 589832 | tf_op jit(solution)/shard_map/ppermute | solution.py:406
  20.2 14.8 %collective-permute-start.1 = (f32[12,8,512]{2,1,0:T(8,128)S(1)}, f32[12,8,512]{2,1,0:T(8,128)S(1)}, u32[]{:S(2)}, u32[]{:S(2)}) collective-permute-start(f32[12,8,512]{2,1,0:T(8,128)S(1)} %get-tuple-element.12), channel_id=1, source_target_pairs={{1,0},{2,1},{3,2},{4,3},{5,4},{6,5},{7,6},{8,7},{9,8},{10,9},{11,1... | collective-permute-start | bytes 589832 | tf_op jit(solution)/shard_map/ppermute | solution.py:407

commit v2 on v1

v2 whole, which is shorter than its diff:
```python
import jax
import jax.numpy as jnp
from jax import lax
from jax.experimental import pallas as pl
from jax.experimental.pallas import tpu as pltpu
from jax.sharding import PartitionSpec as P

KAPPA = 0.24
STEPS = 4
FACES = 6
ROWS = 16
SIDE = 512
HALO = 8
TALL = ROWS + 2 * HALO


def iota(shape, dim):
    return lax.broadcasted_iota(jnp.int32, shape, dim)


def reverse_lanes(x):
    index = 127 - iota((8, 128), 1)
    tiles = [
        jnp.take_along_axis(x[:, at : at + 128], index, axis=1)
        for at in range(0, x.shape[1], 128)
    ]
    return jnp.concatenate(tiles[::-1], axis=1) if len(tiles) > 1 else tiles[0]


def column_strips(first, last):
    strips = None
    for g in range(FACES):
        a, b = first(g), last(g)
        lane = iota(a.shape, 1)
        moved = pltpu.roll(jnp.where(lane >= 64, b, a), 16 * g + 8, 1)
        strips = moved if strips is None else jnp.where(lane >= 16 * g, moved, strips)
    return strips


def spread(block):
    return [pltpu.roll(block, 96 - 32 * b, 1) for b in range(3)]


def unspread(b0, b1, b2):
    lane = iota((8, 128), 1)
    return jnp.where(
        lane < 32, pltpu.roll(b0, 32, 1), jnp.where(lane < 64, pltpu.roll(b1, 64, 1), pltpu.roll(b2, 96, 1))
    )


def pack_kernel(place, seams_at, scaling_at, density_at, up, down, message, seams, scaling, density, arrived):
    p = place[0]
    pairs = ((scaling_at, scaling), (density_at, density), (seams_at, seams))
    copies = [pltpu.make_async_copy(a, b, arrived.at[i]) for i, (a, b) in enumerate(pairs)]
    for copy in copies:
        copy.start()
    for copy in copies:
        copy.wait()
    count = message.shape[0]
    lane = iota((8, 128), 1)
    sub = iota((8, 128), 0)
    for g in range(FACES):
        up[g] = scaling[g, HALO:]
        up[FACES + g] = density[g, HALO:]
        down[g] = scaling[g, :HALO]
        down[FACES + g] = density[g, :HALO]
    vs = column_strips(lambda g: scaling[g, :, :128], lambda g: scaling[g, :, SIDE - 128 :])
    vd = column_strips(lambda g: density[g, :, :128], lambda g: density[g, :, SIDE - 128 :])
    tail = spread(vd[8:])
    head = (vs[:8], vs[8:], vd[:8])
    block = jnp.concatenate([jnp.where(lane < 96, head[b], tail[b]) for b in range(3)], axis=0)
    is_last = p == count - 1
    is_edge = (p == 0) | is_last

    @pl.when(jnp.logical_not(is_edge))
    def _():
        for q in range(count):
            message[q] = block

    @pl.when(is_edge)
    def _():
        message[0] = block
        message[count - 1] = block
        e = is_last.astype(jnp.int32)
        base = pl.multiple_of(e * 8, 8)
        own_s = jnp.where(is_last, vs[:8], vs[8:])
        own_d = jnp.where(is_last, vd[:8], vd[8:])
        far = jnp.where(is_last, pltpu.roll(own_d, 5, 0), pltpu.roll(own_d, 3, 0))
        free = jnp.where(is_last, (sub >= 5).astype(jnp.int32), (sub <= 2).astype(jnp.int32)) == 1
        lane16 = lane % 16
        coded = jnp.where(
            free & (lane16 < 4),
            pltpu.roll(far, 124, 1),
            jnp.where(free & (lane16 >= 12), pltpu.roll(far, 4, 1), own_s),
        )
        extra = spread(coded)
        pieces = []
        for g in range(FACES):
            turned = seams[2, e, g] == 1
            s = scaling[g, pl.ds(base, 8), :]
            d = density[g, pl.ds(base, 8), :]
            pieces.append((jnp.where(turned, reverse_lanes(s), s), jnp.where(turned, reverse_lanes(d), d)))
        sub_wide = iota((8, SIDE), 0)
        lane_wide = iota((8, SIDE), 1) % 128
        blocks = []
        for b in range(3):
            (s0, d0), (s1, d1) = pieces[2 * b], pieces[2 * b + 1]
            low = jnp.where(is_last, pltpu.roll(d0, 4, 0), d0)
            high = jnp.where(is_last, d1, pltpu.roll(d1, 4, 0))
            blocks.append((s0, s1, jnp.where(sub_wide < 4, low, high)))
        for t in range(3):
            tail_t = jnp.concatenate([extra[t]] * 4, axis=1)
            for r in range(8):
                moved = [pltpu.roll(blocks[b][t], (32 * b - 16 * r + 8) % SIDE, 1) for b in range(3)]
                full = jnp.where(
                    lane_wide < 32,
                    moved[0],
                    jnp.where(lane_wide < 64, moved[1], jnp.where(lane_wide < 96, moved[2], tail_t)),
                )
                for a in range(4):
                    q = 8 * a + r
                    if 0 < q < count - 1:
                        message[q, 8 * t : 8 * t + 8, :] = full[:, 128 * a : 128 * a + 128]


def diffuse(x):
    rows, lanes = x.shape
    vertical = pltpu.roll(x, 1, 0) + pltpu.roll(x, rows - 1, 0)
    lateral = pltpu.roll(x, 1, 1) + pltpu.roll(x, lanes - 1, 1)
    return x + KAPPA * ((vertical + lateral) - 4.0 * x)


def diffuse_strip(x, where):
    above = pltpu.roll(x, 1, 0)
    below = pltpu.roll(x, TALL - 1, 0)
    left = pltpu.roll(x, 1, 1)
    right = pltpu.roll(x, 127, 1)
    if where is not None:
        lane = iota((8, 128), 1)
        sub = iota((8, 128), 0)
        at, edge = (0, 8) if where == "first" else (24, 23)
        depth = 7 - sub if where == "first" else sub
        place = lane % 64
        start = lane - place
        line = jnp.broadcast_to(x[edge : edge + 1], (8, 128))
        index = jnp.where(place == 40, start + 39 - depth, jnp.where(place == 23, start + 24 + depth, 0))
        lateral = jnp.take_along_axis(line, index, axis=1)
        index = jnp.where(place >= 32, start + 40, start + 23)
        taken = jnp.take_along_axis(x[at : at + 8], index, axis=1)
        taken = jnp.where((place == 39 - depth) | (place == 24 + depth), taken, 0.0)
        vertical = jnp.sum(taken, axis=0, keepdims=True)
        ghost = (place >= 24) & (place < 40)
        fixed_left = jnp.where(place == 40, lateral, left[at : at + 8])
        fixed_right = jnp.where(place == 23, lateral, right[at : at + 8])
        if where == "first":
            left = jnp.concatenate([fixed_left, left[8:]], axis=0)
            right = jnp.concatenate([fixed_right, right[8:]], axis=0)
            block = jnp.where(ghost & (sub == 0), vertical, above[8:16])
            above = jnp.concatenate([above[:8], block, above[16:]], axis=0)
        else:
            left = jnp.concatenate([left[:24], fixed_left], axis=0)
            right = jnp.concatenate([right[:24], fixed_right], axis=0)
            block = jnp.where(ghost & (sub == 7), vertical, below[16:24])
            below = jnp.concatenate([below[:16], block, below[24:]], axis=0)
    return x + KAPPA * (((above + below) + (left + right)) - 4.0 * x)


def strip_lanes(first, last, h):
    lane = iota(first.shape, 1)
    return jnp.where(
        lane % 64 < 32, pltpu.roll(last, 24 + 64 * h, 1), pltpu.roll(first, 40 + 64 * h, 1)
    )


def swap_depth(x):
    lane = iota((8, 128), 1)
    index = lane + 7 - 2 * (lane % 8)
    return jnp.concatenate(
        [jnp.take_along_axis(x[at : at + 8], index, axis=1) for at in range(0, x.shape[0], 8)], axis=0
    )


def put_weighted(weighted, value, f, i, j):
    per = 48 // weighted.shape[0]
    t = 8 * f + 4 * i + j
    if isinstance(f, int):
        weighted[t // per, 8 * (t % per) : 8 * (t % per) + 8, :] = value
    else:
        at = pl.multiple_of(8 * lax.rem(t, per), 8)
        weighted[lax.div(t, per), pl.ds(at, 8), :] = value


def inner_kernel(weight, scaling, density, up, down, dual, marginal, weighted, strips, own):
    members = weighted.shape[0]
    per = 48 // members
    share = weight[0]
    for k in range(members):
        weighted[k, 8 * per :, :] = jnp.full((8, 128), share, jnp.float32)

    def face(f, carry):
        x = jnp.concatenate([up[f], scaling[f], down[f]], axis=0)
        for _ in range(STEPS):
            x = diffuse(x)
        y = jnp.concatenate([up[FACES + f], density[f], down[FACES + f]], axis=0) / x
        dual[f] = y[HALO : HALO + ROWS]
        for _ in range(STEPS):
            y = diffuse(y)
        m = scaling[f] * y[HALO : HALO + ROWS]
        marginal[f] = m
        scaled = share * jnp.log(m)
        for i in range(2):
            for j in range(4):
                put_weighted(weighted, scaled[8 * i : 8 * i + 8, 128 * j : 128 * j + 128], f, i, j)
        return carry

    lax.fori_loop(0, FACES, face, 0)
    for k, field in enumerate((scaling, density)):

        def ends(g, at):
            columns = slice(at, at + 128)
            return jnp.concatenate(
                [up[FACES * k + g, :, columns], field[g, :, columns], down[FACES * k + g, :, columns]], axis=0
            )

        firsts = [ends(g, 0) for g in range(FACES)]
        lasts = [ends(g, SIDE - 128) for g in range(FACES)]
        lane = iota((TALL, 128), 1)
        for t in range(3):
            strips[k, t] = jnp.where(
                lane < 64,
                strip_lanes(firsts[2 * t], lasts[2 * t], 0),
                strip_lanes(firsts[2 * t + 1], lasts[2 * t + 1], 1),
            )
        own[0, k * TALL : (k + 1) * TALL] = column_strips(lambda g: firsts[g], lambda g: lasts[g])
        own[1, k * TALL : (k + 1) * TALL] = swap_depth(own[0, k * TALL : (k + 1) * TALL])


def seam_kernel(
    place, seams, weight, scaling, density, up, down, message, strips, own, dual_in, marginal_in, weighted_in,
    dual, marginal, weighted, mixed, chunk, table_s, table_d, column_s, column_d, edge, work,
):
    q = place[0]
    count = message.shape[0]
    last = count - 1
    share = weight[0]
    lane = iota((8, 128), 1)
    sub = iota((8, 128), 0)
    is_edge = (q == 0) | (q == last)

    dual[...] = dual_in[...]
    marginal[...] = marginal_in[...]
    weighted[...] = weighted_in[...]

    def far_rows(p):
        return unspread(message[p, :8, :], message[p, 8:16, :], message[p, 16:24, :])

    mirror, upper, lower = last - q, jnp.minimum(last + 1 - q, last), jnp.maximum(last - 1 - q, 0)
    coded = far_rows(jnp.where(q == 1, last, 0))
    near = jnp.where(q == 1, pltpu.roll(coded, 3, 0), pltpu.roll(coded, 5, 0))
    coded_d = jnp.where(lane % 16 < 8, pltpu.roll(near, 4, 1), pltpu.roll(near, 124, 1))
    parts_s = (
        jnp.where(q == last - 1, coded, message[lower, 8:16, :]),
        message[mirror, :8, :],
        message[mirror, 8:16, :],
        jnp.where(q == 1, coded, message[upper, :8, :]),
    )
    parts_d = (
        jnp.where(q == last - 1, coded_d, far_rows(lower)),
        message[mirror, 16:24, :],
        far_rows(mirror),
        jnp.where(q == 1, coded_d, message[upper, 16:24, :]),
    )
    for base, parts in ((0, parts_s), (TALL, parts_d)):
        for block in range(4):
            for i in range(8):
                at = base + TALL - 1 - 8 * block - i
                mixed[2, at : at + 1, :] = parts[block][i : i + 1]

    chunk[:, 96:, :] = jnp.zeros((2, 32, 128), jnp.float32)

    @pl.when(jnp.logical_not(is_edge))
    def _():
        for e in range(2):
            p = e * last
            for g in range(FACES):
                b, h = g // 2, g % 2
                turn = (128 - 32 * b) % 128
                s = message[p, 8 * h : 8 * h + 8, :]
                d = message[p, 16:24, :]
                if turn:
                    s, d = pltpu.roll(s, turn, 1), pltpu.roll(d, turn, 1)
                if h != e:
                    d = pltpu.roll(d, 4, 0)
                at = 48 * e + 8 * g
                chunk[0, at : at + 8, :] = s
                chunk[1, at : at + 8, :] = d

    for is_first in (True, False):

        @pl.when(q == (0 if is_first else last))
        def _():
            e = 0 if is_first else 1

            def gather(p, carry):
                at = pl.multiple_of(16 * p, 16)
                column_s[pl.ds(at, 16), :] = message[p, :16, :]
                column_d[pl.ds(at, 8), :] = message[p, 16:24, :]
                column_d[pl.ds(at + 8, 8), :] = far_rows(p)
                return carry

            lax.fori_loop(0, count, gather, 0, unroll=8)
            for k, (table, columns, field) in enumerate(
                ((table_s, column_s, scaling), (table_d, column_d, density))
            ):
                for a in range(4):
                    rows = slice(128 * a, 128 * a + 128)
                    table[:128, rows] = jnp.transpose(columns[rows, :])
                for e_of in range(2):
                    for g in range(FACES):
                        if is_first:
                            rows = field[g, :HALO] if e_of == 0 else up[FACES * k + g]
                        else:
                            rows = down[FACES * k + g] if e_of == 0 else field[g, HALO:]
                        at = 48 * e_of + 8 * g
                        table[128 + at : 136 + at, :] = rows
                        turned = seams[2, e_of, g] == 1
                        a, b = rows[:, :128], rows[:, SIDE - 128 :]
                        if is_first:
                            piece = pltpu.roll(jnp.where(turned, reverse_lanes(b), a), 8, 1)
                        else:
                            piece = pltpu.roll(jnp.where(turned, reverse_lanes(a), b), 24, 1)
                        chunk[k, at : at + 8, :] = piece
                for f in range(FACES):
                    g, meets = seams[0, e, f], seams[1, e, f]
                    start = jnp.where(
                        meets >= 2, 16 * g + jnp.where(meets == 2, 8, 0), 128 + 48 * meets + 8 * g
                    )
                    rising = (meets % 2) == 0
                    for i in range(8):
                        depth = 7 - i if is_first else i
                        at = start + jnp.where(rising, depth, 7 - depth)
                        edge[k, f, i : i + 1, :] = table[pl.ds(at, 1), :]
                for f in range(FACES):
                    piece = edge[k, f]
                    edge[k, f] = jnp.where(seams[2, e, f] == 1, reverse_lanes(piece), piece)
                at = 0 if is_first else HALO + ROWS
                for t in range(3):
                    pieces = [
                        strip_lanes(edge[k, f, :, :128], edge[k, f, :, SIDE - 128 :], f % 2)
                        for f in (2 * t, 2 * t + 1)
                    ]
                    work[k, t, at : at + 8, :] = jnp.where(lane < 64, pieces[0], pieces[1])

    for k in range(2):
        mixed[4, k * TALL : (k + 1) * TALL, :] = jnp.transpose(chunk[k])[:TALL]
    for v in range(2):
        mixed[v] = own[v]
        if v:
            mixed[2 * v + 1] = swap_depth(mixed[2 * v])
    mixed[5] = swap_depth(mixed[4])

    lane_tall = iota((TALL, 128), 1)
    for k in range(2):
        for t in range(3):
            value = strips[k, t]
            for f in (2 * t, 2 * t + 1):
                for e in (2, 3):
                    g, meets, turned = seams[0, e, f], seams[1, e, f], seams[2, e, f]
                    of_column = meets >= 2
                    rising = (meets % 2) == 0
                    swapped = jnp.where(rising, 1 if e == 2 else 0, 0 if e == 2 else 1)
                    kind = jnp.where(of_column, 2 * turned, 4) + swapped
                    start = jnp.where(of_column, 16 * g + jnp.where(meets == 2, 8, 0), 48 * meets + 8 * g)
                    at = 64 * (f % 2) + (32 if e == 2 else 24)
                    moved = pltpu.roll(
                        mixed[kind, k * TALL : (k + 1) * TALL, :], jnp.bitwise_and(at - start + 128, 127), 1
                    )
                    value = jnp.where((lane_tall >= at) & (lane_tall < at + 8), moved, value)
            rows = [value[:8], value[8:24], value[24:]]
            work[k, t, 8:24, :] = rows[1]

            @pl.when(q != 0)
            def _():
                work[k, t, :8, :] = rows[0]

            @pl.when(q == 0)
            def _():
                work[k, t, :8, :] = jnp.where((lane % 64 >= 24) & (lane % 64 < 40), rows[0], work[k, t, :8, :])

            @pl.when(q != last)
            def _():
                work[k, t, 24:, :] = rows[2]

            @pl.when(q == last)
            def _():
                work[k, t, 24:, :] = jnp.where((lane % 64 >= 24) & (lane % 64 < 40), rows[2], work[k, t, 24:, :])

    for is_first in (True, False):

        @pl.when(q == (0 if is_first else last))
        def _():
            i = 0 if is_first else 1
            near_rows = slice(0, 8) if is_first else slice(8, 16)
            sub_wide = iota((8, SIDE), 0)
            kept = sub_wide >= 4 if is_first else sub_wide < 4

            def stack(ghost, inner):
                return jnp.concatenate([ghost, *inner] if is_first else [*inner, ghost], axis=0)

            def face(f, carry):
                x = stack(edge[0, f], [scaling[f, near_rows, :]])
                for _ in range(STEPS):
                    x = diffuse(x)
                y = stack(edge[1, f], [density[f, near_rows, :]]) / x
                old = dual_in[f]
                ghost, mine = (y[:8], y[8:]) if is_first else (y[8:], y[:8])
                mine = jnp.where(kept, old[near_rows], mine)
                dual[f, near_rows, :] = mine
                y = stack(ghost, [mine, old[8:]] if is_first else [old[:8], mine])
                for _ in range(STEPS):
                    y = diffuse(y)
                m = scaling[f, near_rows, :] * y[8:16]
                marginal[f, near_rows, :] = m
                scaled = share * jnp.log(m)
                for j in range(4):
                    put_weighted(weighted, scaled[:, 128 * j : 128 * j + 128], f, i, j)
                return carry

            lax.fori_loop(0, FACES, face, 0)

    def run(where):
        x = [work[0, t] for t in range(3)]
        for _ in range(STEPS):
            x = [diffuse_strip(v, where) for v in x]
        y = [work[1, t] / x[t] for t in range(3)]
        first = [v[HALO : HALO + ROWS] for v in y]
        for _ in range(STEPS):
            y = [diffuse_strip(v, where) for v in y]
        lane = iota((ROWS, 128), 1)
        per = 48 // weighted.shape[0]
        for t in range(3):
            m = work[0, t, HALO : HALO + ROWS, :] * y[t][HALO : HALO + ROWS]
            scaled = share * jnp.log(m)
            for h in range(2):
                f = 2 * t + h
                for j, turn, mask in ((0, 88 - 64 * h, lane < 8), (3, 104 - 64 * h, lane >= 120)):
                    columns = slice(128 * j, 128 * j + 128)
                    for ref, value in ((dual, first[t]), (marginal, m)):
                        ref[f, :, columns] = jnp.where(mask, pltpu.roll(value, turn, 1), ref[f, :, columns])
                    moved = pltpu.roll(scaled, turn, 1)
                    for i in range(2):
                        at = 8 * f + 4 * i + j
                        rows = slice(8 * (at % per), 8 * (at % per) + 8)
                        weighted[at // per, rows, :] = jnp.where(
                            mask[:8], moved[8 * i : 8 * i + 8], weighted[at // per, rows, :]
                        )

    @pl.when(q == 0)
    def _():
        run("first")

    @pl.when(q == last)
    def _():
        run("last")

    @pl.when(jnp.logical_not(is_edge))
    def _():
        run(None)


def mean_kernel(parts, result):
    members, rows = result.shape[0], result.shape[1]
    total = parts[0]
    for k in range(1, members):
        total = total + parts[k]
    mean = total[:rows] / total[rows : rows + 1]
    value = jnp.exp(mean)
    for k in range(members):
        result[k] = value


def update_kernel(parts, scaling, marginal, fresh, barycenter):
    members = parts.shape[0]
    per = 48 // members
    for f in range(FACES):
        for i in range(2):
            for j in range(4):
                t = 8 * f + 4 * i + j
                at = 8 * (t % per)
                value = parts[t // per, at : at + 8, :]
                rows, columns = slice(8 * i, 8 * i + 8), slice(128 * j, 128 * j + 128)
                barycenter[f, rows, columns] = value
                fresh[f, rows, columns] = scaling[f, rows, columns] * value / marginal[f, rows, columns]


def body(density, scaling, member_weights, seams):
    tiles = lax.axis_size("tile")
    members = lax.axis_size("member")
    scaling = scaling[0]
    density = density[0]
    place = lax.axis_index("tile").astype(jnp.int32).reshape(1)
    f32 = jnp.float32
    vmem = pl.BlockSpec(memory_space=pltpu.VMEM)
    smem = pl.BlockSpec(memory_space=pltpu.SMEM)
    field = jax.ShapeDtypeStruct((FACES, ROWS, SIDE), f32)
    edge_rows = jax.ShapeDtypeStruct((2 * FACES, HALO, SIDE), f32)
    params = pltpu.CompilerParams(vmem_limit_bytes=24 * 1024 * 1024)
    up, down, message = pl.pallas_call(
        pack_kernel,
        out_shape=(edge_rows, edge_rows, jax.ShapeDtypeStruct((tiles, 24, 128), f32)),
        in_specs=[smem] + [pl.BlockSpec(memory_space=pltpu.HBM)] * 3,
        out_specs=(vmem, vmem, vmem),
        scratch_shapes=[
            pltpu.SMEM(seams.shape, jnp.int32),
            pltpu.VMEM(scaling.shape, f32),
            pltpu.VMEM(density.shape, f32),
            pltpu.SemaphoreType.DMA((3,)),
        ],
        compiler_params=params,
        name="pack",
    )(place, seams, scaling, density)
    onward = [(i, (i + 1) % tiles) for i in range(tiles)]
    back = [(b, a) for a, b in onward]
    up = lax.ppermute(up, "tile", onward)
    down = lax.ppermute(down, "tile", back)
    message = lax.all_to_all(message, "tile", 0, 0)
    rows = 384 // members
    sums = jax.ShapeDtypeStruct((members, rows + 8, 128), f32)
    dual, marginal, weighted, strips, own = pl.pallas_call(
        inner_kernel,
        out_shape=(
            field, field, sums,
            jax.ShapeDtypeStruct((2, 3, TALL, 128), f32),
            jax.ShapeDtypeStruct((2, 2 * TALL, 128), f32),
        ),
        in_specs=[smem] + [vmem] * 4,
        out_specs=(vmem,) * 5,
        compiler_params=params,
        name="inner",
    )(member_weights, scaling, density, up, down)
    dual, marginal, weighted = pl.pallas_call(
        seam_kernel,
        out_shape=(field, field, sums),
        in_specs=[smem, smem, smem] + [vmem] * 10,
        out_specs=(vmem, vmem, vmem),
        scratch_shapes=[
            pltpu.VMEM((6, 2 * TALL, 128), f32),
            pltpu.VMEM((2, 128, 128), f32),
            pltpu.VMEM((224, SIDE), f32),
            pltpu.VMEM((224, SIDE), f32),
            pltpu.VMEM((SIDE, 128), f32),
            pltpu.VMEM((SIDE, 128), f32),
            pltpu.VMEM((2, FACES, HALO, SIDE), f32),
            pltpu.VMEM((2, 3, TALL, 128), f32),
        ],
        compiler_params=params,
        name="seam",
    )(place, seams, member_weights, scaling, density, up, down, message, strips, own, dual, marginal, weighted)
    weighted = lax.all_to_all(weighted, "member", 0, 0)
    means = pl.pallas_call(
        mean_kernel,
        out_shape=jax.ShapeDtypeStruct((members, rows, 128), f32),
        in_specs=[vmem],
        out_specs=vmem,
        compiler_params=params,
        name="mean",
    )(weighted)
    means = lax.all_to_all(means, "member", 0, 0)
    fresh, barycenter = pl.pallas_call(
        update_kernel,
        out_shape=(field, field),
        in_specs=[vmem] * 3,
        out_specs=(vmem, vmem),
        compiler_params=params,
        name="update",
    )(means, scaling, marginal)
    return (fresh[None], dual[None], barycenter)


def solution(mesh):
    return jax.shard_map(
        body,
        mesh=mesh,
        in_specs=(
            P("member", None, "tile", None),
            P("member", None, "tile", None),
            P("member"),
            P(),
        ),
        out_specs=(
            P("member", None, "tile", None),
            P("member", None, "tile", None),
            P(None, "tile", None),
        ),
        check_vma=False,
    )
```

time: 76.6 us -> 78 us (1.018)
  Pallas kernels: 14.2 us -> 15.6 us
    pallas_call x1 -> x2, Pallas kernels: 11.4 us -> 12.3 us  [the longest x1 8.03 us: body(): pl.pallas_call(seam_kernel, out_shape=(field, field, sums), in_specs=[sme...]
  transfers between devices with their start and end apart: 3 -> 3, of which waited for: 1 -> 1; matrix products, arithmetic and copies ran while one was open for 0% -> 0% of each run, Pallas kernels for 0% -> 5%
where the time goes in v2:
time: 78 us; the launch traced here: 77.6 us
  blocking collectives  28.9 us (37%)
  starting transfers between devices  22 us (28%)
  Pallas kernels  15.6 us (20%)
  waiting for transfers between devices  7.1 us (9%)
  local copies, waits for them, and re-layouts  2.55 us (3%)
  between operations  1.35 us (2%)
    all_to_all x1, blocking collectives, body(): weighted = lax.all_to_all(weighted, 'member', 0, 0)  16.4 us
    all_to_all x1, starting transfers between devices, body(): message = lax.all_to_all(message, 'tile', 0, 0)  12.9 us
    all_to_all x1, blocking collectives, body(): means = lax.all_to_all(means, 'member', 0, 0)  12.5 us
    pallas_call x1, Pallas kernels, body(): pl.pallas_call(seam_kernel, out_shape=(field, field, sums), in_specs=[sme...  8.03 us
    ppermute x1, waiting for transfers between devices, body(): up = lax.ppermute(up, 'tile', onward)  7.1 us
    ppermute x1, starting transfers between devices, body(): down = lax.ppermute(down, 'tile', back)  6.99 us
    pallas_call x1, Pallas kernels, body(): pl.pallas_call(inner_kernel, out_shape=(field, field, sums, jax.ShapeDtyp...  4.25 us
    unnamed x10, local copies, waits for them, and re-layouts  2.55 us
  transfers between devices with their start and end apart: 3, of which 1 were waited for; matrix products, arithmetic and copies ran while one was open for 0% of the time, Pallas kernels for 5%

profile of v2, /device:TPU:8, one launch (start us, length us, event | category | flops | bytes accessed | tf_op | source)
XLA Modules:
  0.0 77.6 jit_solution(14685260764286804362)
XLA Ops:
  0.6 0.0 copy-start.4
  0.6 0.7 copy-done.4
  1.3 0.0 copy-start
  1.3 0.9 %copy-done = f32[1,6,16,512]{3,2,1,0:T(8,128)S(1)} copy-done((f32[1,6,16,512]{3,2,1,0:T(8,128)S(1)}, f32[1,6,16,512]{3,2,1,0:T(8,128)}, u32[]{:S(2)}) %copy-start) | copy-done | bytes 196632
  2.2 0.0 copy-start.2
  2.3 0.9 %copy-done.2 = f32[1,6,16,512]{3,2,1,0:T(8,128)S(1)} copy-done((f32[1,6,16,512]{3,2,1,0:T(8,128)S(1)}, f32[1,6,16,512]{3,2,1,0:T(8,128)}, u32[]{:S(2)}) %copy-start.2) | copy-done | bytes 196632
  3.2 2.5 %pack.1 = (f32[12,8,512]{2,1,0:T(8,128)S(1)}, f32[12,8,512]{2,1,0:T(8,128)S(1)}, f32[32,24,128]{2,1,0:T(8,128)}) custom-call(s32[1]{0:T(128)} %bitcast.place, s32[3,4,6]{2,1,0:T(4,128)S(1)} %copy-done.4, f32[6,16,512]{2,1,0:T(8,128)S(1)} %bitcast.5, f32[6,16,512]{2,1,0:T(8,128)S(1)} %bitcast.9), custom_call_target="tpu_custom_call" | custom-call | tf_op jit(solution)/shard_map/pack/pallas_call | solution.py:508
  5.7 0.0 copy-start.1
  5.7 0.0 copy-start.3
  5.7 12.9 %all-to-all-start = ((f32[32,24,128]{2,1,0:T(8,128)}), f32[32,24,128]{2,1,0:T(8,128)S(1)}, u32[]{:S(2)}, u32[]{:S(2)}) async-start(f32[32,24,128]{2,1,0:T(8,128)} %get-tuple-element.18), calls=%async_computation | async-start | bytes 786432 | tf_op jit(solution)/shard_map/all_to_all | solution.py:526
  18.6 2.2 %collective-permute-start = (f32[12,8,512]{2,1,0:T(8,128)S(1)}, f32[12,8,512]{2,1,0:T(8,128)S(1)}, u32[]{:S(2)}, u32[]{:S(2)}) collective-permute-start(f32[12,8,512]{2,1,0:T(8,128)S(1)} %get-tuple-element.16), channel_id=1, source_target_pairs={{0,1},{1,2},{2,3},{3,4},{4,5},{5,6},{6,7},{7,8},{8,9},{9,10},{10,1... | collective-permute-start | bytes 589832 | tf_op jit(solution)/shard_map/ppermute | solution.py:524
  20.8 7.0 %collective-permute-start.1 = (f32[12,8,512]{2,1,0:T(8,128)S(1)}, f32[12,8,512]{2,1,0:T(8,128)S(1)}, u32[]{:S(2)}, u32[]{:S(2)}) collective-permute-start(f32[12,8,512]{2,1,0:T(8,128)S(1)} %get-tuple-element.17), channel_id=1, source_target_pairs={{1,0},{2,1},{3,2},{4,3},{5,4},{6,5},{7,6},{8,7},{9,8},{10,9},{11,1... | collective-permute-start | bytes 589832 | tf_op jit(solution)/shard_map/ppermute | solution.py:525
  28.4 7.1 %collective-permute-done.up = f32[12,8,512]{2,1,0:T(8,128)S(1)} collective-permute-done((f32[12,8,512]{2,1,0:T(8,128)S(1)}, f32[12,8,512]{2,1,0:T(8,128)S(1)}, u32[]{:S(2)}, u32[]{:S(2)}) %collective-permute-start) | collective-permute-done | bytes 196640 | tf_op jit(solution)/shard_map/ppermute | solution.py:524
  35.5 0.0 collective-permute-done.1.down
  35.5 0.0 copy-done.1
  35.5 0.0 copy-done.3
  35.5 4.2 %inner.1 = (f32[6,16,512]{2,1,0:T(8,128)S(1)}, f32[6,16,512]{2,1,0:T(8,128)S(1)}, f32[16,32,128]{2,1,0:T(8,128)S(1)}, f32[2,3,32,128]{3,2,1,0:T(8,128)S(1)}, f32[2,64,128]{2,1,0:T(8,128)S(1)}) custom-call(f32[1]{0:T(128)S(6)} %copy.7.weight, f32[6,16,512]{2,1,0:T(8,128)S(1)} %bitcast.6, f32[6,16,512]{2,1,0:T(8,128)S(1)} %bitcast.10, ...), custom_call_target="tpu_custom_call" | custom-call | tf_op jit(solution)/shard_map/inner/pallas_call | solution.py:529
  39.8 0.0 all-to-all-done.message
  39.8 8.0 %seam.1 = (f32[6,16,512]{2,1,0:T(8,128)}, f32[6,16,512]{2,1,0:T(8,128)S(1)}, f32[16,32,128]{2,1,0:T(8,128)S(1)}) custom-call(s32[1]{0:T(128)} %bitcast.place, s32[3,4,6]{2,1,0:T(4,128)S(1)} %copy-done.4, f32[1]{0:T(128)S(6)} %copy.7.weight, f32[6,16,512]{2,1,0:T(8,128)S(1)} %bitcast.7, f32[6,16,512]{2,1,0:T(8,128)S(1)} %bitcast.11, ...), custom_call_target="tpu_custom_call" | custom-call | tf_op jit(solution)/shard_map/seam/pallas_call | solution.py:541
  47.8 16.4 %all_to_all.15.parts = f32[16,32,128]{2,1,0:T(8,128)S(1)} all-to-all(f32[16,32,128]{2,1,0:T(8,128)S(1)} %get-tuple-element.24), channel_id=1, replica_groups=mesh['member'=16,'tile'=32] {'member'}, dimensions={0} | all-to-all | bytes 524288 | tf_op jit(solution)/shard_map/all_to_all | solution.py:559
  64.3 12.5 %all_to_all.16.parts = f32[16,24,128]{2,1,0:T(8,128)S(1)} all-to-all(f32[16,24,128]{2,1,0:T(8,128)S(1)} %mean.1), channel_id=1, replica_groups=mesh['member'=16,'tile'=32] {'member'}, dimensions={0} | all-to-all | bytes 393216 | tf_op jit(solution)/shard_map/all_to_all | solution.py:568
  76.8 0.8 update.1
  (1 shorter events, 0.0 us)
Async XLA Ops:
  0.6 0.7 copy-start.4
  1.3 0.9 %copy-start = (f32[1,6,16,512]{3,2,1,0:T(8,128)S(1)}, f32[1,6,16,512]{3,2,1,0:T(8,128)}, u32[]{:S(2)}) copy-start(f32[1,6,16,512]{3,2,1,0:T(8,128)} %param.5) | copy-start | bytes 589828
  2.2 0.9 %copy-start.2 = (f32[1,6,16,512]{3,2,1,0:T(8,128)S(1)}, f32[1,6,16,512]{3,2,1,0:T(8,128)}, u32[]{:S(2)}) copy-start(f32[1,6,16,512]{3,2,1,0:T(8,128)} %param.4) | copy-start | bytes 589828
  5.7 29.8 %copy-start.1 = (f32[1,6,16,512]{3,2,1,0:T(8,128)S(1)}, f32[1,6,16,512]{3,2,1,0:T(8,128)}, u32[]{:S(2)}) copy-start(f32[1,6,16,512]{3,2,1,0:T(8,128)} %param.5) | copy-start | bytes 589828
  5.7 29.8 %copy-start.3 = (f32[1,6,16,512]{3,2,1,0:T(8,128)S(1)}, f32[1,6,16,512]{3,2,1,0:T(8,128)}, u32[]{:S(2)}) copy-start(f32[1,6,16,512]{3,2,1,0:T(8,128)} %param.4) | copy-start | bytes 589828
  5.7 34.1 %all-to-all-start = ((f32[32,24,128]{2,1,0:T(8,128)}), f32[32,24,128]{2,1,0:T(8,128)S(1)}, u32[]{:S(2)}, u32[]{:S(2)}) async-start(f32[32,24,128]{2,1,0:T(8,128)} %get-tuple-element.18), calls=%async_computation | async-start | bytes 786432 | tf_op jit(solution)/shard_map/all_to_all | solution.py:526
  18.6 16.9 %collective-permute-start = (f32[12,8,512]{2,1,0:T(8,128)S(1)}, f32[12,8,512]{2,1,0:T(8,128)S(1)}, u32[]{:S(2)}, u32[]{:S(2)}) collective-permute-start(f32[12,8,512]{2,1,0:T(8,128)S(1)} %get-tuple-element.16), channel_id=1, source_target_pairs={{0,1},{1,2},{2,3},{3,4},{4,5},{5,6},{6,7},{7,8},{8,9},{9,10},{10,1... | collective-permute-start | bytes 589832 | tf_op jit(solution)/shard_map/ppermute | solution.py:524
  20.8 14.8 %collective-permute-start.1 = (f32[12,8,512]{2,1,0:T(8,128)S(1)}, f32[12,8,512]{2,1,0:T(8,128)S(1)}, u32[]{:S(2)}, u32[]{:S(2)}) collective-permute-start(f32[12,8,512]{2,1,0:T(8,128)S(1)} %get-tuple-element.17), channel_id=1, source_target_pairs={{1,0},{2,1},{3,2},{4,3},{5,4},{6,5},{7,6},{8,7},{9,8},{10,9},{11,1... | collective-permute-start | bytes 589832 | tf_op jit(solution)/shard_map/ppermute | solution.py:525

commit v3 on v2

--- a/solution.py
+++ b/solution.py
@@ -12,6 +12,9 @@
 SIDE = 512
 HALO = 8
 TALL = ROWS + 2 * HALO
+
+
+LONG = pl.CostEstimate(flops=10**10, bytes_accessed=10**10, transcendentals=0)
 
 
 def iota(shape, dim):
@@ -48,22 +51,23 @@
     )
 
 
-def pack_kernel(place, seams_at, scaling_at, density_at, up, down, message, seams, scaling, density, arrived):
-    p = place[0]
-    pairs = ((scaling_at, scaling), (density_at, density), (seams_at, seams))
-    copies = [pltpu.make_async_copy(a, b, arrived.at[i]) for i, (a, b) in enumerate(pairs)]
+def rows_kernel(scaling, density, up, down, arrived):
+    copies = []
+    for i, (field, at) in enumerate(((scaling, 0), (density, FACES))):
+        faces = pl.ds(at, FACES)
+        copies.append(pltpu.make_async_copy(field.at[:, pl.ds(HALO, HALO)], up.at[faces], arrived.at[2 * i]))
+        copies.append(pltpu.make_async_copy(field.at[:, pl.ds(0, HALO)], down.at[faces], arrived.at[2 * i + 1]))
     for copy in copies:
         copy.start()
     for copy in copies:
         copy.wait()
+
+
+def pack_kernel(place, seams, scaling, density, message):
+    p = place[0]
     count = message.shape[0]
     lane = iota((8, 128), 1)
     sub = iota((8, 128), 0)
-    for g in range(FACES):
-        up[g] = scaling[g, HALO:]
-        up[FACES + g] = density[g, HALO:]
-        down[g] = scaling[g, :HALO]
-        down[FACES + g] = density[g, :HALO]
     vs = column_strips(lambda g: scaling[g, :, :128], lambda g: scaling[g, :, SIDE - 128 :])
     vd = column_strips(lambda g: density[g, :, :128], lambda g: density[g, :, SIDE - 128 :])
     tail = spread(vd[8:])
@@ -505,24 +509,28 @@
     field = jax.ShapeDtypeStruct((FACES, ROWS, SIDE), f32)
     edge_rows = jax.ShapeDtypeStruct((2 * FACES, HALO, SIDE), f32)
     params = pltpu.CompilerParams(vmem_limit_bytes=24 * 1024 * 1024)
-    up, down, message = pl.pallas_call(
-        pack_kernel,
-        out_shape=(edge_rows, edge_rows, jax.ShapeDtypeStruct((tiles, 24, 128), f32)),
-        in_specs=[smem] + [pl.BlockSpec(memory_space=pltpu.HBM)] * 3,
-        out_specs=(vmem, vmem, vmem),
-        scratch_shapes=[
-            pltpu.SMEM(seams.shape, jnp.int32),
-            pltpu.VMEM(scaling.shape, f32),
-            pltpu.VMEM(density.shape, f32),
-            pltpu.SemaphoreType.DMA((3,)),
-        ],
-        compiler_params=params,
-        name="pack",
-    )(place, seams, scaling, density)
+    anywhere = pl.BlockSpec(memory_space=pl.ANY)
+    up, down = pl.pallas_call(
+        rows_kernel,
+        out_shape=(edge_rows, edge_rows),
+        in_specs=[anywhere, anywhere],
+        out_specs=(anywhere, anywhere),
+        scratch_shapes=[pltpu.SemaphoreType.DMA((4,))],
+        name="rows",
+    )(scaling, density)
     onward = [(i, (i + 1) % tiles) for i in range(tiles)]
     back = [(b, a) for a, b in onward]
     up = lax.ppermute(up, "tile", onward)
     down = lax.ppermute(down, "tile", back)
+    message = pl.pallas_call(
+        pack_kernel,
+        out_shape=jax.ShapeDtypeStruct((tiles, 24, 128), f32),
+        in_specs=[smem, smem, vmem, vmem],
+        out_specs=vmem,
+        compiler_params=params,
+        cost_estimate=LONG,
+        name="pack",
+    )(place, seams, scaling, density)
     message = lax.all_to_all(message, "tile", 0, 0)
     rows = 384 // members
     sums = jax.ShapeDtypeStruct((members, rows + 8, 128), f32)
@@ -536,6 +544,7 @@
         in_specs=[smem] + [vmem] * 4,
         out_specs=(vmem,) * 5,
         compiler_params=params,
+        cost_estimate=LONG,
         name="inner",
     )(member_weights, scaling, density, up, down)
     dual, marginal, weighted = pl.pallas_call(

time: 78 us -> 89.6 us (1.15)
  Pallas kernels: 15.6 us -> 28.1 us
  waiting for transfers between devices: 7.1 us -> 10.4 us
  local copies, waits for them, and re-layouts: 2.55 us -> 0.01 us
  starting transfers between devices: 22 us -> 19.8 us
    pallas_call x1 -> x2, Pallas kernels: 2.5 us -> 15.1 us  [the longest x1 13 us: body(): pl.pallas_call(rows_kernel, out_shape=(edge_rows, edge_rows), in_specs=[a...]
    all_to_all x1, waiting for transfers between devices: 0.01 us -> 10.4 us  [body(): message = lax.all_to_all(message, 'tile', 0, 0)]
    all_to_all x1, starting transfers between devices: 12.9 us -> 5.02 us  [body(): message = lax.all_to_all(message, 'tile', 0, 0)]
    ppermute x1, waiting for transfers between devices: 7.1 us -> 0.01 us  [body(): up = lax.ppermute(up, 'tile', onward)]
    ppermute x1, starting transfers between devices: 6.99 us -> 12.8 us  [body(): down = lax.ppermute(down, 'tile', back)]
    unnamed x10 -> x6, local copies, waits for them, and re-layouts: 2.55 us -> 0.01 us
  transfers between devices with their start and end apart: 3 -> 3, of which waited for: 1 -> 1; matrix products, arithmetic and copies ran while one was open for 0% -> 0% of each run, Pallas kernels for 5% -> 7%
where the time goes in v3:
time: 89.6 us; the launch traced here: 89.2 us
  blocking collectives  29.5 us (33%)
  Pallas kernels  28.1 us (31%)
  starting transfers between devices  19.8 us (22%)
  waiting for transfers between devices  10.4 us (12%)
  between operations  1.39 us (2%)
    all_to_all x1, blocking collectives, body(): weighted = lax.all_to_all(weighted, 'member', 0, 0)  17 us
    pallas_call x1, Pallas kernels, body(): pl.pallas_call(rows_kernel, out_shape=(edge_rows, edge_rows), in_specs=[a...  13 us
    ppermute x1, starting transfers between devices, body(): down = lax.ppermute(down, 'tile', back)  12.8 us
    all_to_all x1, blocking collectives, body(): means = lax.all_to_all(means, 'member', 0, 0)  12.5 us
    all_to_all x1, waiting for transfers between devices, body(): message = lax.all_to_all(message, 'tile', 0, 0)  10.4 us
    pallas_call x1, Pallas kernels, body(): pl.pallas_call(seam_kernel, out_shape=(field, field, sums), in_specs=[sme...  8.02 us
    all_to_all x1, starting transfers between devices, body(): message = lax.all_to_all(message, 'tile', 0, 0)  5.02 us
    pallas_call x1, Pallas kernels, body(): pl.pallas_call(inner_kernel, out_shape=(field, field, sums, jax.ShapeDtyp...  4.25 us
  transfers between devices with their start and end apart: 3, of which 1 were waited for; matrix products, arithmetic and copies ran while one was open for 0% of the time, Pallas kernels for 7%

profile of v3, /device:TPU:8, one launch (start us, length us, event | category | flops | bytes accessed | tf_op | source)
XLA Modules:
  0.0 89.2 jit_solution(18350947570658094387)
XLA Ops:
  0.6 0.0 copy-start
  0.6 0.0 copy-start.1
  0.6 13.0 %rows.1 = (f32[12,8,512]{2,1,0:T(8,128)}, f32[12,8,512]{2,1,0:T(8,128)}) custom-call(f32[6,16,512]{2,1,0:T(8,128)} %bitcast.5, f32[6,16,512]{2,1,0:T(8,128)} %bitcast.10), custom_call_target="tpu_custom_call" | custom-call | tf_op jit(solution)/shard_map/rows/pallas_call | solution.py:513
  13.7 0.0 copy-start.2
  13.7 1.9 %collective-permute-start = (f32[12,8,512]{2,1,0:T(8,128)}, f32[12,8,512]{2,1,0:T(8,128)S(1)}, u32[]{:S(2)}, u32[]{:S(2)}) collective-permute-start(f32[12,8,512]{2,1,0:T(8,128)} %get-tuple-element.15), channel_id=1, source_target_pairs={{0,1},{1,2},{2,3},{3,4},{4,5},{5,6},{6,7},{7,8},{8,9},{9,10},{10,1... | collective-permute-start | bytes 589832 | tf_op jit(solution)/shard_map/ppermute | solution.py:523
  15.6 12.8 %collective-permute-start.1 = (f32[12,8,512]{2,1,0:T(8,128)}, f32[12,8,512]{2,1,0:T(8,128)S(1)}, u32[]{:S(2)}, u32[]{:S(2)}) collective-permute-start(f32[12,8,512]{2,1,0:T(8,128)} %get-tuple-element.16), channel_id=1, source_target_pairs={{1,0},{2,1},{3,2},{4,3},{5,4},{6,5},{7,6},{8,7},{9,8},{10,9},{11,1... | collective-permute-start | bytes 589832 | tf_op jit(solution)/shard_map/ppermute | solution.py:524
  28.5 0.0 copy-done
  28.5 0.0 copy-done.1
  28.5 0.0 copy-done.2
  28.5 2.0 %pack.1 = f32[32,24,128]{2,1,0:T(8,128)} custom-call(s32[1]{0:T(128)} %bitcast.place, s32[3,4,6]{2,1,0:T(4,128)S(1)} %copy-done.2, f32[6,16,512]{2,1,0:T(8,128)S(1)} %bitcast.6, f32[6,16,512]{2,1,0:T(8,128)S(1)} %bitcast.11), custom_call_target="tpu_custom_call" | custom-call | flops 10000000000 | bytes 10000000000 | tf_op jit(solution)/shard_map/pack/pallas_call | solution.py:525
  30.5 5.0 %all-to-all-start = ((f32[32,24,128]{2,1,0:T(8,128)}), f32[32,24,128]{2,1,0:T(8,128)S(1)}, u32[]{:S(2)}, u32[]{:S(2)}) async-start(f32[32,24,128]{2,1,0:T(8,128)} %pack.1), calls=%async_computation | async-start | bytes 786432 | tf_op jit(solution)/shard_map/all_to_all | solution.py:534
  36.2 0.0 collective-permute-done.up
  36.2 0.0 collective-permute-done.1.down
  36.2 4.2 %inner.1 = (f32[6,16,512]{2,1,0:T(8,128)S(1)}, f32[6,16,512]{2,1,0:T(8,128)S(1)}, f32[16,32,128]{2,1,0:T(8,128)S(1)}, f32[2,3,32,128]{3,2,1,0:T(8,128)S(1)}, f32[2,64,128]{2,1,0:T(8,128)S(1)}) custom-call(f32[1]{0:T(128)S(6)} %copy.7.weight, f32[6,16,512]{2,1,0:T(8,128)S(1)} %bitcast.7, f32[6,16,512]{2,1,0:T(8,128)S(1)} %bitcast.12, ...), custom_call_target="tpu_custom_call" | custom-call | flops 10000000000 | bytes 10000000000 | tf_op jit(solution)/shard_map/inner/pallas_call | solution.py:537
  40.5 10.4 %all-to-all-done.message = f32[32,24,128]{2,1,0:T(8,128)S(1)} async-done(((f32[32,24,128]{2,1,0:T(8,128)}), f32[32,24,128]{2,1,0:T(8,128)S(1)}, u32[]{:S(2)}, u32[]{:S(2)}) %all-to-all-start) | async-done | bytes 393248 | tf_op jit(solution)/shard_map/all_to_all | solution.py:534
  50.9 8.0 %seam.1 = (f32[6,16,512]{2,1,0:T(8,128)}, f32[6,16,512]{2,1,0:T(8,128)S(1)}, f32[16,32,128]{2,1,0:T(8,128)S(1)}) custom-call(s32[1]{0:T(128)} %bitcast.place, s32[3,4,6]{2,1,0:T(4,128)S(1)} %copy-done.2, f32[1]{0:T(128)S(6)} %copy.7.weight, f32[6,16,512]{2,1,0:T(8,128)S(1)} %bitcast.8, f32[6,16,512]{2,1,0:T(8,128)S(1)} %bitcast.13, ...), custom_call_target="tpu_custom_call" | custom-call | tf_op jit(solution)/shard_map/seam/pallas_call | solution.py:550
  58.9 17.0 %all_to_all.15.parts = f32[16,32,128]{2,1,0:T(8,128)S(1)} all-to-all(f32[16,32,128]{2,1,0:T(8,128)S(1)} %get-tuple-element.22), channel_id=1, replica_groups=mesh['member'=16,'tile'=32] {'member'}, dimensions={0} | all-to-all | bytes 524288 | tf_op jit(solution)/shard_map/all_to_all | solution.py:568
  75.9 12.5 %all_to_all.16.parts = f32[16,24,128]{2,1,0:T(8,128)S(1)} all-to-all(f32[16,24,128]{2,1,0:T(8,128)S(1)} %mean.1), channel_id=1, replica_groups=mesh['member'=16,'tile'=32] {'member'}, dimensions={0} | all-to-all | bytes 393216 | tf_op jit(solution)/shard_map/all_to_all | solution.py:577
  88.4 0.8 update.1
  (1 shorter events, 0.0 us)
Async XLA Ops:
  0.6 27.9 %copy-start = (f32[1,6,16,512]{3,2,1,0:T(8,128)S(1)}, f32[1,6,16,512]{3,2,1,0:T(8,128)}, u32[]{:S(2)}) copy-start(f32[1,6,16,512]{3,2,1,0:T(8,128)} %param.5) | copy-start | bytes 589828
  0.6 27.9 %copy-start.1 = (f32[1,6,16,512]{3,2,1,0:T(8,128)S(1)}, f32[1,6,16,512]{3,2,1,0:T(8,128)}, u32[]{:S(2)}) copy-start(f32[1,6,16,512]{3,2,1,0:T(8,128)} %param.4) | copy-start | bytes 589828
  13.7 14.8 %copy-start.2 = (s32[3,4,6]{2,1,0:T(4,128)S(1)}, s32[3,4,6]{2,1,0:T(4,128)}, u32[]{:S(2)}) copy-start(s32[3,4,6]{2,1,0:T(4,128)} %seams.3) | copy-start | bytes 868
  13.7 22.5 %collective-permute-start = (f32[12,8,512]{2,1,0:T(8,128)}, f32[12,8,512]{2,1,0:T(8,128)S(1)}, u32[]{:S(2)}, u32[]{:S(2)}) collective-permute-start(f32[12,8,512]{2,1,0:T(8,128)} %get-tuple-element.15), channel_id=1, source_target_pairs={{0,1},{1,2},{2,3},{3,4},{4,5},{5,6},{6,7},{7,8},{8,9},{9,10},{10,1... | collective-permute-start | bytes 589832 | tf_op jit(solution)/shard_map/ppermute | solution.py:523
  15.6 20.6 %collective-permute-start.1 = (f32[12,8,512]{2,1,0:T(8,128)}, f32[12,8,512]{2,1,0:T(8,128)S(1)}, u32[]{:S(2)}, u32[]{:S(2)}) collective-permute-start(f32[12,8,512]{2,1,0:T(8,128)} %get-tuple-element.16), channel_id=1, source_target_pairs={{1,0},{2,1},{3,2},{4,3},{5,4},{6,5},{7,6},{8,7},{9,8},{10,9},{11,1... | collective-permute-start | bytes 589832 | tf_op jit(solution)/shard_map/ppermute | solution.py:524
  30.5 20.4 %all-to-all-start = ((f32[32,24,128]{2,1,0:T(8,128)}), f32[32,24,128]{2,1,0:T(8,128)S(1)}, u32[]{:S(2)}, u32[]{:S(2)}) async-start(f32[32,24,128]{2,1,0:T(8,128)} %pack.1), calls=%async_computation | async-start | bytes 786432 | tf_op jit(solution)/shard_map/all_to_all | solution.py:534

commit v4 on v2

--- a/solution.py
+++ b/solution.py
@@ -48,22 +48,32 @@
     )
 
 
-def pack_kernel(place, seams_at, scaling_at, density_at, up, down, message, seams, scaling, density, arrived):
+def join_halves(low, high):
+    return jnp.where(iota(low.shape, 0) < 4, low, high)
+
+
+def halo_rows(rows, k, g, is_up):
+    if k == 0:
+        return rows[g]
+    block = rows[FACES + g // 2]
+    return pltpu.roll(block, 4, 0) if (g % 2 == 0) == is_up else block
+
+
+def pack_kernel(place, seams, scaling, density, up, down, message):
     p = place[0]
-    pairs = ((scaling_at, scaling), (density_at, density), (seams_at, seams))
-    copies = [pltpu.make_async_copy(a, b, arrived.at[i]) for i, (a, b) in enumerate(pairs)]
-    for copy in copies:
-        copy.start()
-    for copy in copies:
-        copy.wait()
     count = message.shape[0]
     lane = iota((8, 128), 1)
     sub = iota((8, 128), 0)
     for g in range(FACES):
         up[g] = scaling[g, HALO:]
-        up[FACES + g] = density[g, HALO:]
         down[g] = scaling[g, :HALO]
-        down[FACES + g] = density[g, :HALO]
+    for b in range(3):
+        up[FACES + b] = join_halves(
+            pltpu.roll(density[2 * b, HALO:], 4, 0), density[2 * b + 1, HALO:]
+        )
+        down[FACES + b] = join_halves(
+            density[2 * b, :HALO], pltpu.roll(density[2 * b + 1, :HALO], 4, 0)
+        )
     vs = column_strips(lambda g: scaling[g, :, :128], lambda g: scaling[g, :, SIDE - 128 :])
     vd = column_strips(lambda g: density[g, :, :128], lambda g: density[g, :, SIDE - 128 :])
     tail = spread(vd[8:])
@@ -190,53 +200,8 @@
         weighted[lax.div(t, per), pl.ds(at, 8), :] = value
 
 
-def inner_kernel(weight, scaling, density, up, down, dual, marginal, weighted, strips, own):
-    members = weighted.shape[0]
-    per = 48 // members
-    share = weight[0]
-    for k in range(members):
-        weighted[k, 8 * per :, :] = jnp.full((8, 128), share, jnp.float32)
-
-    def face(f, carry):
-        x = jnp.concatenate([up[f], scaling[f], down[f]], axis=0)
-        for _ in range(STEPS):
-            x = diffuse(x)
-        y = jnp.concatenate([up[FACES + f], density[f], down[FACES + f]], axis=0) / x
-        dual[f] = y[HALO : HALO + ROWS]
-        for _ in range(STEPS):
-            y = diffuse(y)
-        m = scaling[f] * y[HALO : HALO + ROWS]
-        marginal[f] = m
-        scaled = share * jnp.log(m)
-        for i in range(2):
-            for j in range(4):
-                put_weighted(weighted, scaled[8 * i : 8 * i + 8, 128 * j : 128 * j + 128], f, i, j)
-        return carry
-
-    lax.fori_loop(0, FACES, face, 0)
-    for k, field in enumerate((scaling, density)):
-
-        def ends(g, at):
-            columns = slice(at, at + 128)
-            return jnp.concatenate(
-                [up[FACES * k + g, :, columns], field[g, :, columns], down[FACES * k + g, :, columns]], axis=0
-            )
-
-        firsts = [ends(g, 0) for g in range(FACES)]
-        lasts = [ends(g, SIDE - 128) for g in range(FACES)]
-        lane = iota((TALL, 128), 1)
-        for t in range(3):
-            strips[k, t] = jnp.where(
-                lane < 64,
-                strip_lanes(firsts[2 * t], lasts[2 * t], 0),
-                strip_lanes(firsts[2 * t + 1], lasts[2 * t + 1], 1),
-            )
-        own[0, k * TALL : (k + 1) * TALL] = column_strips(lambda g: firsts[g], lambda g: lasts[g])
-        own[1, k * TALL : (k + 1) * TALL] = swap_depth(own[0, k * TALL : (k + 1) * TALL])
-
-
-def seam_kernel(
-    place, seams, weight, scaling, density, up, down, message, strips, own, dual_in, marginal_in, weighted_in,
+def heat_kernel(
+    place, seams, weight, scaling, density, up, down, message,
     dual, marginal, weighted, mixed, chunk, table_s, table_d, column_s, column_d, edge, work,
 ):
     q = place[0]
@@ -247,9 +212,9 @@
     sub = iota((8, 128), 0)
     is_edge = (q == 0) | (q == last)
 
-    dual[...] = dual_in[...]
-    marginal[...] = marginal_in[...]
-    weighted[...] = weighted_in[...]
+    per = 48 // weighted.shape[0]
+    for k in range(weighted.shape[0]):
+        weighted[k, 8 * per :, :] = jnp.full((8, 128), share, jnp.float32)
 
     def far_rows(p):
         return unspread(message[p, :8, :], message[p, 8:16, :], message[p, 16:24, :])
@@ -318,9 +283,9 @@
                 for e_of in range(2):
                     for g in range(FACES):
                         if is_first:
-                            rows = field[g, :HALO] if e_of == 0 else up[FACES * k + g]
+                            rows = field[g, :HALO] if e_of == 0 else halo_rows(up, k, g, True)
                         else:
-                            rows = down[FACES * k + g] if e_of == 0 else field[g, HALO:]
+                            rows = halo_rows(down, k, g, False) if e_of == 0 else field[g, HALO:]
                         at = 48 * e_of + 8 * g
                         table[128 + at : 136 + at, :] = rows
                         turned = seams[2, e_of, g] == 1
@@ -353,16 +318,35 @@
 
     for k in range(2):
         mixed[4, k * TALL : (k + 1) * TALL, :] = jnp.transpose(chunk[k])[:TALL]
-    for v in range(2):
-        mixed[v] = own[v]
-        if v:
-            mixed[2 * v + 1] = swap_depth(mixed[2 * v])
-    mixed[5] = swap_depth(mixed[4])
-
     lane_tall = iota((TALL, 128), 1)
+    strips = []
+    for k, field in enumerate((scaling, density)):
+
+        def ends(g, at):
+            columns = slice(at, at + 128)
+            above = up.at[:, :, columns]
+            below = down.at[:, :, columns]
+            return jnp.concatenate(
+                [halo_rows(above, k, g, True), field[g, :, columns], halo_rows(below, k, g, False)], axis=0
+            )
+
+        firsts = [ends(g, 0) for g in range(FACES)]
+        lasts = [ends(g, SIDE - 128) for g in range(FACES)]
+        strips.append([
+            jnp.where(
+                lane_tall < 64,
+                strip_lanes(firsts[2 * t], lasts[2 * t], 0),
+                strip_lanes(firsts[2 * t + 1], lasts[2 * t + 1], 1),
+            )
+            for t in range(3)
+        ])
+        mixed[0, k * TALL : (k + 1) * TALL, :] = column_strips(lambda g: firsts[g], lambda g: lasts[g])
+    for v in (0, 2, 4):
+        mixed[v + 1] = swap_depth(mixed[v])
+
     for k in range(2):
         for t in range(3):
-            value = strips[k, t]
+            value = strips[k][t]
             for f in (2 * t, 2 * t + 1):
                 for e in (2, 3):
                     g, meets, turned = seams[0, e, f], seams[1, e, f], seams[2, e, f]
@@ -395,40 +379,23 @@
             def _():
                 work[k, t, 24:, :] = jnp.where((lane % 64 >= 24) & (lane % 64 < 40), rows[2], work[k, t, 24:, :])
 
-    for is_first in (True, False):
-
-        @pl.when(q == (0 if is_first else last))
-        def _():
-            i = 0 if is_first else 1
-            near_rows = slice(0, 8) if is_first else slice(8, 16)
-            sub_wide = iota((8, SIDE), 0)
-            kept = sub_wide >= 4 if is_first else sub_wide < 4
-
-            def stack(ghost, inner):
-                return jnp.concatenate([ghost, *inner] if is_first else [*inner, ghost], axis=0)
-
-            def face(f, carry):
-                x = stack(edge[0, f], [scaling[f, near_rows, :]])
-                for _ in range(STEPS):
-                    x = diffuse(x)
-                y = stack(edge[1, f], [density[f, near_rows, :]]) / x
-                old = dual_in[f]
-                ghost, mine = (y[:8], y[8:]) if is_first else (y[8:], y[:8])
-                mine = jnp.where(kept, old[near_rows], mine)
-                dual[f, near_rows, :] = mine
-                y = stack(ghost, [mine, old[8:]] if is_first else [old[:8], mine])
-                for _ in range(STEPS):
-                    y = diffuse(y)
-                m = scaling[f, near_rows, :] * y[8:16]
-                marginal[f, near_rows, :] = m
-                scaled = share * jnp.log(m)
+    def run(where):
+        for f in range(FACES):
+            above = [edge[k, f] if where == "first" else halo_rows(up, k, f, True) for k in range(2)]
+            below = [edge[k, f] if where == "last" else halo_rows(down, k, f, False) for k in range(2)]
+            x = jnp.concatenate([above[0], scaling[f], below[0]], axis=0)
+            for _ in range(STEPS):
+                x = diffuse(x)
+            y = jnp.concatenate([above[1], density[f], below[1]], axis=0) / x
+            dual[f] = y[HALO : HALO + ROWS]
+            for _ in range(STEPS):
+                y = diffuse(y)
+            m = scaling[f] * y[HALO : HALO + ROWS]
+            marginal[f] = m
+            scaled = share * jnp.log(m)
+            for i in range(2):
                 for j in range(4):
-                    put_weighted(weighted, scaled[:, 128 * j : 128 * j + 128], f, i, j)
-                return carry
-
-            lax.fori_loop(0, FACES, face, 0)
-
-    def run(where):
+                    put_weighted(weighted, scaled[8 * i : 8 * i + 8, 128 * j : 128 * j + 128], f, i, j)
         x = [work[0, t] for t in range(3)]
         for _ in range(STEPS):
             x = [diffuse_strip(v, where) for v in x]
@@ -437,7 +404,6 @@
         for _ in range(STEPS):
             y = [diffuse_strip(v, where) for v in y]
         lane = iota((ROWS, 128), 1)
-        per = 48 // weighted.shape[0]
         for t in range(3):
             m = work[0, t, HALO : HALO + ROWS, :] * y[t][HALO : HALO + ROWS]
             scaled = share * jnp.log(m)
@@ -503,19 +469,13 @@
     vmem = pl.BlockSpec(memory_space=pltpu.VMEM)
     smem = pl.BlockSpec(memory_space=pltpu.SMEM)
     field = jax.ShapeDtypeStruct((FACES, ROWS, SIDE), f32)
-    edge_rows = jax.ShapeDtypeStruct((2 * FACES, HALO, SIDE), f32)
+    edge_rows = jax.ShapeDtypeStruct((FACES + FACES // 2, HALO, SIDE), f32)
     params = pltpu.CompilerParams(vmem_limit_bytes=24 * 1024 * 1024)
     up, down, message = pl.pallas_call(
         pack_kernel,
         out_shape=(edge_rows, edge_rows, jax.ShapeDtypeStruct((tiles, 24, 128), f32)),
-        in_specs=[smem] + [pl.BlockSpec(memory_space=pltpu.HBM)] * 3,
+        in_specs=[smem, smem, vmem, vmem],
         out_specs=(vmem, vmem, vmem),
-        scratch_shapes=[
-            pltpu.SMEM(seams.shape, jnp.int32),
-            pltpu.VMEM(scaling.shape, f32),
-            pltpu.VMEM(density.shape, f32),
-            pltpu.SemaphoreType.DMA((3,)),
-        ],
         compiler_params=params,
         name="pack",
     )(place, seams, scaling, density)
@@ -526,22 +486,10 @@
     message = lax.all_to_all(message, "tile", 0, 0)
     rows = 384 // members
     sums = jax.ShapeDtypeStruct((members, rows + 8, 128), f32)
-    dual, marginal, weighted, strips, own = pl.pallas_call(
-        inner_kernel,
-        out_shape=(
-            field, field, sums,
-            jax.ShapeDtypeStruct((2, 3, TALL, 128), f32),
-            jax.ShapeDtypeStruct((2, 2 * TALL, 128), f32),
-        ),
-        in_specs=[smem] + [vmem] * 4,
-        out_specs=(vmem,) * 5,
-        compiler_params=params,
-        name="inner",
-    )(member_weights, scaling, density, up, down)
     dual, marginal, weighted = pl.pallas_call(
-        seam_kernel,
+        heat_kernel,
         out_shape=(field, field, sums),
-        in_specs=[smem, smem, smem] + [vmem] * 10,
+        in_specs=[smem, smem, smem] + [vmem] * 5,
         out_specs=(vmem, vmem, vmem),
         scratch_shapes=[
             pltpu.VMEM((6, 2 * TALL, 128), f32),
@@ -554,8 +502,8 @@
             pltpu.VMEM((2, 3, TALL, 128), f32),
         ],
         compiler_params=params,
-        name="seam",
-    )(place, seams, member_weights, scaling, density, up, down, message, strips, own, dual, marginal, weighted)
+        name="heat",
+    )(place, seams, member_weights, scaling, density, up, down, message)
     weighted = lax.all_to_all(weighted, "member", 0, 0)
     means = pl.pallas_call(
         mean_kernel,

time: 78 us -> 72.5 us (0.929)
  Pallas kernels: 15.6 us -> 10.8 us
    pallas_call x2 -> x1, Pallas kernels: 12.3 us -> 7.97 us  [body(): pl.pallas_call(heat_kernel, out_shape=(field, field, sums), in_specs=[sme...]
  transfers between devices with their start and end apart: 3 -> 3, of which waited for: 1 -> 1; matrix products, arithmetic and copies ran while one was open for 0% -> 0% of each run, Pallas kernels for 5% -> 0%
where the time goes in v4:
time: 72.5 us; the launch traced here: 72.1 us
  blocking collectives  28.9 us (40%)
  starting transfers between devices  22 us (30%)
  Pallas kernels  10.8 us (15%)
  waiting for transfers between devices  6.49 us (9%)
  local copies, waits for them, and re-layouts  2.54 us (4%)
  between operations  1.34 us (2%)
    all_to_all x1, blocking collectives, body(): weighted = lax.all_to_all(weighted, 'member', 0, 0)  16.4 us
    all_to_all x1, starting transfers between devices, body(): message = lax.all_to_all(message, 'tile', 0, 0)  12.9 us
    all_to_all x1, blocking collectives, body(): means = lax.all_to_all(means, 'member', 0, 0)  12.5 us
    pallas_call x1, Pallas kernels, body(): pl.pallas_call(heat_kernel, out_shape=(field, field, sums), in_specs=[sme...  7.97 us
    ppermute x1, starting transfers between devices, body(): down = lax.ppermute(down, 'tile', back)  6.99 us
    ppermute x1, waiting for transfers between devices, body(): up = lax.ppermute(up, 'tile', onward)  6.49 us
    unnamed x10, local copies, waits for them, and re-layouts  2.54 us
    ppermute x1, starting transfers between devices, body(): up = lax.ppermute(up, 'tile', onward)  2.18 us
  transfers between devices with their start and end apart: 3, of which 1 were waited for; matrix products, arithmetic and copies ran while one was open for 0% of the time, Pallas kernels for 0%

profile of v4, /device:TPU:8, one launch (start us, length us, event | category | flops | bytes accessed | tf_op | source)
XLA Modules:
  0.0 72.1 jit_solution(18355999401138769511)
XLA Ops:
  0.6 0.0 copy-start.4
  0.6 0.7 copy-done.4
  1.3 0.0 copy-start
  1.3 0.9 %copy-done = f32[1,6,16,512]{3,2,1,0:T(8,128)S(1)} copy-done((f32[1,6,16,512]{3,2,1,0:T(8,128)S(1)}, f32[1,6,16,512]{3,2,1,0:T(8,128)}, u32[]{:S(2)}) %copy-start) | copy-done | bytes 196632
  2.2 0.0 copy-start.2
  2.3 0.9 %copy-done.2 = f32[1,6,16,512]{3,2,1,0:T(8,128)S(1)} copy-done((f32[1,6,16,512]{3,2,1,0:T(8,128)S(1)}, f32[1,6,16,512]{3,2,1,0:T(8,128)}, u32[]{:S(2)}) %copy-start.2) | copy-done | bytes 196632
  3.2 2.0 %pack.1 = (f32[9,8,512]{2,1,0:T(8,128)S(1)}, f32[9,8,512]{2,1,0:T(8,128)S(1)}, f32[32,24,128]{2,1,0:T(8,128)}) custom-call(s32[1]{0:T(128)} %bitcast.place, s32[3,4,6]{2,1,0:T(4,128)S(1)} %copy-done.4, f32[6,16,512]{2,1,0:T(8,128)S(1)} %bitcast.5, f32[6,16,512]{2,1,0:T(8,128)S(1)} %bitcast.8), custom_call_target="tpu_custom_call" | custom-call | tf_op jit(solution)/shard_map/pack/pallas_call | solution.py:474
  5.2 0.0 copy-start.1
  5.2 0.0 copy-start.3
  5.2 12.9 %all-to-all-start = ((f32[32,24,128]{2,1,0:T(8,128)}), f32[32,24,128]{2,1,0:T(8,128)S(1)}, u32[]{:S(2)}, u32[]{:S(2)}) async-start(f32[32,24,128]{2,1,0:T(8,128)} %get-tuple-element.13), calls=%async_computation | async-start | bytes 786432 | tf_op jit(solution)/shard_map/all_to_all | solution.py:486
  18.0 2.2 %collective-permute-start = (f32[9,8,512]{2,1,0:T(8,128)S(1)}, f32[9,8,512]{2,1,0:T(8,128)S(1)}, u32[]{:S(2)}, u32[]{:S(2)}) collective-permute-start(f32[9,8,512]{2,1,0:T(8,128)S(1)} %get-tuple-element.11), channel_id=1, source_target_pairs={{0,1},{1,2},{2,3},{3,4},{4,5},{5,6},{6,7},{7,8},{8,9},{9,10},{10,1... | collective-permute-start | bytes 442376 | tf_op jit(solution)/shard_map/ppermute | solution.py:484
  20.2 7.0 %collective-permute-start.1 = (f32[9,8,512]{2,1,0:T(8,128)S(1)}, f32[9,8,512]{2,1,0:T(8,128)S(1)}, u32[]{:S(2)}, u32[]{:S(2)}) collective-permute-start(f32[9,8,512]{2,1,0:T(8,128)S(1)} %get-tuple-element.12), channel_id=1, source_target_pairs={{1,0},{2,1},{3,2},{4,3},{5,4},{6,5},{7,6},{8,7},{9,8},{10,9},{11,1... | collective-permute-start | bytes 442376 | tf_op jit(solution)/shard_map/ppermute | solution.py:485
  27.9 6.5 %collective-permute-done.up = f32[9,8,512]{2,1,0:T(8,128)S(1)} collective-permute-done((f32[9,8,512]{2,1,0:T(8,128)S(1)}, f32[9,8,512]{2,1,0:T(8,128)S(1)}, u32[]{:S(2)}, u32[]{:S(2)}) %collective-permute-start) | collective-permute-done | bytes 147488 | tf_op jit(solution)/shard_map/ppermute | solution.py:484
  34.4 0.0 collective-permute-done.1.down
  34.4 0.0 all-to-all-done.message
  34.4 0.0 copy-done.1
  34.4 0.0 copy-done.3
  34.4 8.0 %heat.1 = (f32[6,16,512]{2,1,0:T(8,128)}, f32[6,16,512]{2,1,0:T(8,128)S(1)}, f32[16,32,128]{2,1,0:T(8,128)S(1)}) custom-call(s32[1]{0:T(128)} %bitcast.place, s32[3,4,6]{2,1,0:T(4,128)S(1)} %copy-done.4, f32[1]{0:T(128)S(6)} %copy.7.weight, f32[6,16,512]{2,1,0:T(8,128)S(1)} %bitcast.6, f32[6,16,512]{2,1,0:T(8,128)S(1)} %bitcast.9, ...), custom_call_target="tpu_custom_call" | custom-call | tf_op jit(solution)/shard_map/heat/pallas_call | solution.py:489
  42.4 16.4 %all_to_all.15.parts = f32[16,32,128]{2,1,0:T(8,128)S(1)} all-to-all(f32[16,32,128]{2,1,0:T(8,128)S(1)} %get-tuple-element.14), channel_id=1, replica_groups=mesh['member'=16,'tile'=32] {'member'}, dimensions={0} | all-to-all | bytes 524288 | tf_op jit(solution)/shard_map/all_to_all | solution.py:507
  58.8 12.5 %all_to_all.16.parts = f32[16,24,128]{2,1,0:T(8,128)S(1)} all-to-all(f32[16,24,128]{2,1,0:T(8,128)S(1)} %mean.1), channel_id=1, replica_groups=mesh['member'=16,'tile'=32] {'member'}, dimensions={0} | all-to-all | bytes 393216 | tf_op jit(solution)/shard_map/all_to_all | solution.py:516
  71.3 0.8 %update.1 = (f32[6,16,512]{2,1,0:T(8,128)}, f32[6,16,512]{2,1,0:T(8,128)}) custom-call(f32[16,24,128]{2,1,0:T(8,128)S(1)} %all_to_all.16.parts, f32[6,16,512]{2,1,0:T(8,128)S(1)} %bitcast.7, f32[6,16,512]{2,1,0:T(8,128)S(1)} %get-tuple-element.15.marginal), custom_call_target="tpu_custom_call" | custom-call | tf_op jit(solution)/shard_map/update/pallas_call | solution.py:517
  (1 shorter events, 0.0 us)
Async XLA Ops:
  0.6 0.7 copy-start.4
  1.3 0.9 %copy-start = (f32[1,6,16,512]{3,2,1,0:T(8,128)S(1)}, f32[1,6,16,512]{3,2,1,0:T(8,128)}, u32[]{:S(2)}) copy-start(f32[1,6,16,512]{3,2,1,0:T(8,128)} %param.5) | copy-start | bytes 589828
  2.2 0.9 %copy-start.2 = (f32[1,6,16,512]{3,2,1,0:T(8,128)S(1)}, f32[1,6,16,512]{3,2,1,0:T(8,128)}, u32[]{:S(2)}) copy-start(f32[1,6,16,512]{3,2,1,0:T(8,128)} %param.4) | copy-start | bytes 589828
  5.2 29.2 %copy-start.1 = (f32[1,6,16,512]{3,2,1,0:T(8,128)S(1)}, f32[1,6,16,512]{3,2,1,0:T(8,128)}, u32[]{:S(2)}) copy-start(f32[1,6,16,512]{3,2,1,0:T(8,128)} %param.5) | copy-start | bytes 589828
  5.2 29.2 %copy-start.3 = (f32[1,6,16,512]{3,2,1,0:T(8,128)S(1)}, f32[1,6,16,512]{3,2,1,0:T(8,128)}, u32[]{:S(2)}) copy-start(f32[1,6,16,512]{3,2,1,0:T(8,128)} %param.4) | copy-start | bytes 589828
  5.2 29.2 %all-to-all-start = ((f32[32,24,128]{2,1,0:T(8,128)}), f32[32,24,128]{2,1,0:T(8,128)S(1)}, u32[]{:S(2)}, u32[]{:S(2)}) async-start(f32[32,24,128]{2,1,0:T(8,128)} %get-tuple-element.13), calls=%async_computation | async-start | bytes 786432 | tf_op jit(solution)/shard_map/all_to_all | solution.py:486
  18.0 16.3 %collective-permute-start = (f32[9,8,512]{2,1,0:T(8,128)S(1)}, f32[9,8,512]{2,1,0:T(8,128)S(1)}, u32[]{:S(2)}, u32[]{:S(2)}) collective-permute-start(f32[9,8,512]{2,1,0:T(8,128)S(1)} %get-tuple-element.11), channel_id=1, source_target_pairs={{0,1},{1,2},{2,3},{3,4},{4,5},{5,6},{6,7},{7,8},{8,9},{9,10},{10,1... | collective-permute-start | bytes 442376 | tf_op jit(solution)/shard_map/ppermute | solution.py:484
  20.2 14.1 %collective-permute-start.1 = (f32[9,8,512]{2,1,0:T(8,128)S(1)}, f32[9,8,512]{2,1,0:T(8,128)S(1)}, u32[]{:S(2)}, u32[]{:S(2)}) collective-permute-start(f32[9,8,512]{2,1,0:T(8,128)S(1)} %get-tuple-element.12), channel_id=1, source_target_pairs={{1,0},{2,1},{3,2},{4,3},{5,4},{6,5},{7,6},{8,7},{9,8},{10,9},{11,1... | collective-permute-start | bytes 442376 | tf_op jit(solution)/shard_map/ppermute | solution.py:485

commit v5 on v4

--- a/solution.py
+++ b/solution.py
@@ -59,21 +59,27 @@
     return pltpu.roll(block, 4, 0) if (g % 2 == 0) == is_up else block
 
 
-def pack_kernel(place, seams, scaling, density, up, down, message):
+def pack_kernel(place, seams_at, scaling_at, density_at, beside, across, message, seams, scaling, density, arrived):
     p = place[0]
+    pairs = ((scaling_at, scaling), (density_at, density), (seams_at, seams))
+    copies = [pltpu.make_async_copy(a, b, arrived.at[i]) for i, (a, b) in enumerate(pairs)]
+    for copy in copies:
+        copy.start()
+    for copy in copies:
+        copy.wait()
+    is_even = lax.rem(p, 2) == 0
     count = message.shape[0]
     lane = iota((8, 128), 1)
     sub = iota((8, 128), 0)
-    for g in range(FACES):
-        up[g] = scaling[g, HALO:]
-        down[g] = scaling[g, :HALO]
+    ups = [scaling[g, HALO:] for g in range(FACES)]
+    downs = [scaling[g, :HALO] for g in range(FACES)]
     for b in range(3):
-        up[FACES + b] = join_halves(
-            pltpu.roll(density[2 * b, HALO:], 4, 0), density[2 * b + 1, HALO:]
-        )
-        down[FACES + b] = join_halves(
-            density[2 * b, :HALO], pltpu.roll(density[2 * b + 1, :HALO], 4, 0)
-        )
+        d0, d1 = density[2 * b], density[2 * b + 1]
+        ups.append(join_halves(pltpu.roll(d0[HALO:], 4, 0), d1[HALO:]))
+        downs.append(join_halves(d0[:HALO], pltpu.roll(d1[:HALO], 4, 0)))
+    for b, (u, d) in enumerate(zip(ups, downs)):
+        beside[b] = jnp.where(is_even, u, d)
+        across[b] = jnp.where(is_even, d, u)
     vs = column_strips(lambda g: scaling[g, :, :128], lambda g: scaling[g, :, SIDE - 128 :])
     vd = column_strips(lambda g: density[g, :, :128], lambda g: density[g, :, SIDE - 128 :])
     tail = spread(vd[8:])
@@ -201,12 +207,16 @@
 
 
 def heat_kernel(
-    place, seams, weight, scaling, density, up, down, message,
-    dual, marginal, weighted, mixed, chunk, table_s, table_d, column_s, column_d, edge, work,
+    place, seams, weight, scaling, density, beside, across, message,
+    dual, marginal, weighted, up, down, mixed, chunk, table_s, table_d, column_s, column_d, edge, work,
 ):
     q = place[0]
     count = message.shape[0]
     last = count - 1
+    is_even = lax.rem(q, 2) == 0
+    for b in range(FACES + FACES // 2):
+        up[b] = jnp.where(is_even, across[b], beside[b])
+        down[b] = jnp.where(is_even, beside[b], across[b])
     share = weight[0]
     lane = iota((8, 128), 1)
     sub = iota((8, 128), 0)
@@ -471,18 +481,21 @@
     field = jax.ShapeDtypeStruct((FACES, ROWS, SIDE), f32)
     edge_rows = jax.ShapeDtypeStruct((FACES + FACES // 2, HALO, SIDE), f32)
     params = pltpu.CompilerParams(vmem_limit_bytes=24 * 1024 * 1024)
-    up, down, message = pl.pallas_call(
+    beside, across, message = pl.pallas_call(
         pack_kernel,
         out_shape=(edge_rows, edge_rows, jax.ShapeDtypeStruct((tiles, 24, 128), f32)),
-        in_specs=[smem, smem, vmem, vmem],
+        in_specs=[smem] + [pl.BlockSpec(memory_space=pl.ANY)] * 3,
         out_specs=(vmem, vmem, vmem),
-        compiler_params=params,
+        scratch_shapes=[
+            pltpu.SMEM(seams.shape, jnp.int32),
+            pltpu.VMEM(scaling.shape, f32),
+            pltpu.VMEM(density.shape, f32),
+            pltpu.SemaphoreType.DMA((3,)),
+        ],
         name="pack",
     )(place, seams, scaling, density)
-    onward = [(i, (i + 1) % tiles) for i in range(tiles)]
-    back = [(b, a) for a, b in onward]
-    up = lax.ppermute(up, "tile", onward)
-    down = lax.ppermute(down, "tile", back)
+    beside = lax.ppermute(beside, "tile", [(i, i ^ 1) for i in range(tiles)])
+    across = lax.ppermute(across, "tile", [(i, (i + 1 if i % 2 else i - 1) % tiles) for i in range(tiles)])
     message = lax.all_to_all(message, "tile", 0, 0)
     rows = 384 // members
     sums = jax.ShapeDtypeStruct((members, rows + 8, 128), f32)
@@ -492,6 +505,8 @@
         in_specs=[smem, smem, smem] + [vmem] * 5,
         out_specs=(vmem, vmem, vmem),
         scratch_shapes=[
+            pltpu.VMEM(edge_rows.shape, f32),
+            pltpu.VMEM(edge_rows.shape, f32),
             pltpu.VMEM((6, 2 * TALL, 128), f32),
             pltpu.VMEM((2, 128, 128), f32),
             pltpu.VMEM((224, SIDE), f32),
@@ -503,7 +518,7 @@
         ],
         compiler_params=params,
         name="heat",
-    )(place, seams, member_weights, scaling, density, up, down, message)
+    )(place, seams, member_weights, scaling, density, beside, across, message)
     weighted = lax.all_to_all(weighted, "member", 0, 0)
     means = pl.pallas_call(
         mean_kernel,

time: 72.5 us -> 70.5 us (0.972)
  local copies, waits for them, and re-layouts: 2.54 us -> 0.03 us
    unnamed x10, local copies, waits for them, and re-layouts: 2.54 us -> 0.03 us
where the time goes in v5:
time: 70.5 us; the launch traced here: 70.2 us
  blocking collectives  28.9 us (41%)
  starting transfers between devices  22.3 us (32%)
  Pallas kernels  11.3 us (16%)
  waiting for transfers between devices  6.22 us (9%)
  between operations  1.4 us (2%)
    all_to_all x1, blocking collectives, body(): weighted = lax.all_to_all(weighted, 'member', 0, 0)  16.4 us
    all_to_all x1, starting transfers between devices, body(): message = lax.all_to_all(message, 'tile', 0, 0)  12.9 us
    all_to_all x1, blocking collectives, body(): means = lax.all_to_all(means, 'member', 0, 0)  12.5 us
    pallas_call x1, Pallas kernels, body(): pl.pallas_call(heat_kernel, out_shape=(field, field, sums), in_specs=[sme...  7.96 us
    ppermute x1, starting transfers between devices, body(): lax.ppermute(across, 'tile', [(i, (i + 1 if i % 2 else i - 1) % tiles) fo...  7.24 us
    ppermute x1, waiting for transfers between devices, body(): lax.ppermute(across, 'tile', [(i, (i + 1 if i % 2 else i - 1) % tiles) fo...  6.21 us
    pallas_call x1, Pallas kernels, body(): pl.pallas_call(pack_kernel, out_shape=(edge_rows, edge_rows, jax.ShapeDty...  2.54 us
    ppermute x1, starting transfers between devices, body(): beside = lax.ppermute(beside, 'tile', [(i, i ^ 1) for i in range(tiles)])  2.18 us
  transfers between devices with their start and end apart: 3, of which 1 were waited for; matrix products, arithmetic and copies ran while one was open for 0% of the time, Pallas kernels for 0%

profile of v5, /device:TPU:8, one launch (start us, length us, event | category | flops | bytes accessed | tf_op | source)
XLA Modules:
  0.0 70.2 jit_solution(10639165572310720258)
XLA Ops:
  0.6 2.5 %pack.1 = (f32[9,8,512]{2,1,0:T(8,128)}, f32[9,8,512]{2,1,0:T(8,128)}, f32[32,24,128]{2,1,0:T(8,128)}) custom-call(s32[1]{0:T(128)} %bitcast.place, s32[3,4,6]{2,1,0:T(4,128)} %seams.1, f32[6,16,512]{2,1,0:T(8,128)} %bitcast.5, f32[6,16,512]{2,1,0:T(8,128)} %bitcast.8), custom_call_target="tpu_custom_call" | custom-call | tf_op jit(solution)/shard_map/pack/pallas_call | solution.py:484
  3.2 0.0 copy-start.4
  3.2 0.0 copy-start.3
  3.2 0.0 copy-start
  3.2 0.0 copy-start.1
  3.2 0.0 copy-start.2
  3.2 12.9 %all-to-all-start = ((f32[32,24,128]{2,1,0:T(8,128)}), f32[32,24,128]{2,1,0:T(8,128)S(1)}, u32[]{:S(2)}, u32[]{:S(2)}) async-start(f32[32,24,128]{2,1,0:T(8,128)} %get-tuple-element.13), calls=%async_computation | async-start | bytes 786432 | tf_op jit(solution)/shard_map/all_to_all | solution.py:499
  16.1 0.0 copy-done.4
  16.1 2.2 %collective-permute-start = (f32[9,8,512]{2,1,0:T(8,128)S(1)}, f32[9,8,512]{2,1,0:T(8,128)S(1)}, u32[]{:S(2)}, u32[]{:S(2)}) collective-permute-start(f32[9,8,512]{2,1,0:T(8,128)S(1)} %copy-done.4), channel_id=1, source_target_pairs={{0,1},{1,0},{2,3},{3,2},{4,5},{5,4},{6,7},{7,6},{8,9},{9,8},{10,11... | collective-permute-start | bytes 442376 | tf_op jit(solution)/shard_map/ppermute | solution.py:497
  18.3 0.0 copy-done.3
  18.3 7.2 %collective-permute-start.1 = (f32[9,8,512]{2,1,0:T(8,128)S(1)}, f32[9,8,512]{2,1,0:T(8,128)S(1)}, u32[]{:S(2)}, u32[]{:S(2)}) collective-permute-start(f32[9,8,512]{2,1,0:T(8,128)S(1)} %copy-done.3), channel_id=1, source_target_pairs={{0,31},{1,2},{2,1},{3,4},{4,3},{5,6},{6,5},{7,8},{8,7},{9,10},{10,... | collective-permute-start | bytes 442376 | tf_op jit(solution)/shard_map/ppermute | solution.py:498
  26.2 0.0 collective-permute-done.beside
  26.2 6.2 %collective-permute-done.1.across = f32[9,8,512]{2,1,0:T(8,128)S(1)} collective-permute-done((f32[9,8,512]{2,1,0:T(8,128)S(1)}, f32[9,8,512]{2,1,0:T(8,128)S(1)}, u32[]{:S(2)}, u32[]{:S(2)}) %collective-permute-start.1) | collective-permute-done | bytes 147488 | tf_op jit(solution)/shard_map/ppermute | solution.py:498
  32.4 0.0 all-to-all-done.message
  32.4 0.0 copy-done
  32.4 0.0 copy-done.1
  32.4 0.0 copy-done.2
  32.5 8.0 %heat.1 = (f32[6,16,512]{2,1,0:T(8,128)}, f32[6,16,512]{2,1,0:T(8,128)S(1)}, f32[16,32,128]{2,1,0:T(8,128)S(1)}) custom-call(s32[1]{0:T(128)} %bitcast.place, s32[3,4,6]{2,1,0:T(4,128)S(1)} %copy-done.2, f32[1]{0:T(128)S(6)} %copy.7.weight, f32[6,16,512]{2,1,0:T(8,128)S(1)} %bitcast.6, f32[6,16,512]{2,1,0:T(8,128)S(1)} %bitcast.9, ...), custom_call_target="tpu_custom_call" | custom-call | tf_op jit(solution)/shard_map/heat/pallas_call | solution.py:502
  40.4 16.4 %all_to_all.15.parts = f32[16,32,128]{2,1,0:T(8,128)S(1)} all-to-all(f32[16,32,128]{2,1,0:T(8,128)S(1)} %get-tuple-element.14), channel_id=1, replica_groups=mesh['member'=16,'tile'=32] {'member'}, dimensions={0} | all-to-all | bytes 524288 | tf_op jit(solution)/shard_map/all_to_all | solution.py:522
  56.9 12.5 %all_to_all.16.parts = f32[16,24,128]{2,1,0:T(8,128)S(1)} all-to-all(f32[16,24,128]{2,1,0:T(8,128)S(1)} %mean.1), channel_id=1, replica_groups=mesh['member'=16,'tile'=32] {'member'}, dimensions={0} | all-to-all | bytes 393216 | tf_op jit(solution)/shard_map/all_to_all | solution.py:531
  69.4 0.8 %update.1 = (f32[6,16,512]{2,1,0:T(8,128)}, f32[6,16,512]{2,1,0:T(8,128)}) custom-call(f32[16,24,128]{2,1,0:T(8,128)S(1)} %all_to_all.16.parts, f32[6,16,512]{2,1,0:T(8,128)S(1)} %bitcast.7, f32[6,16,512]{2,1,0:T(8,128)S(1)} %get-tuple-element.15.marginal), custom_call_target="tpu_custom_call" | custom-call | tf_op jit(solution)/shard_map/update/pallas_call | solution.py:532
  (1 shorter events, 0.0 us)
Async XLA Ops:
  3.2 12.9 %copy-start.4 = (f32[9,8,512]{2,1,0:T(8,128)S(1)}, f32[9,8,512]{2,1,0:T(8,128)}, u32[]{:S(2)}) copy-start(f32[9,8,512]{2,1,0:T(8,128)} %get-tuple-element.11) | copy-start | bytes 442372
  3.2 15.1 %copy-start.3 = (f32[9,8,512]{2,1,0:T(8,128)S(1)}, f32[9,8,512]{2,1,0:T(8,128)}, u32[]{:S(2)}) copy-start(f32[9,8,512]{2,1,0:T(8,128)} %get-tuple-element.12) | copy-start | bytes 442372
  3.2 29.2 %copy-start = (f32[1,6,16,512]{3,2,1,0:T(8,128)S(1)}, f32[1,6,16,512]{3,2,1,0:T(8,128)}, u32[]{:S(2)}) copy-start(f32[1,6,16,512]{3,2,1,0:T(8,128)} %param.5) | copy-start | bytes 589828
  3.2 29.2 %copy-start.1 = (f32[1,6,16,512]{3,2,1,0:T(8,128)S(1)}, f32[1,6,16,512]{3,2,1,0:T(8,128)}, u32[]{:S(2)}) copy-start(f32[1,6,16,512]{3,2,1,0:T(8,128)} %param.4) | copy-start | bytes 589828
  3.2 29.2 %copy-start.2 = (s32[3,4,6]{2,1,0:T(4,128)S(1)}, s32[3,4,6]{2,1,0:T(4,128)}, u32[]{:S(2)}) copy-start(s32[3,4,6]{2,1,0:T(4,128)} %seams.1) | copy-start | bytes 868
  3.2 29.2 %all-to-all-start = ((f32[32,24,128]{2,1,0:T(8,128)}), f32[32,24,128]{2,1,0:T(8,128)S(1)}, u32[]{:S(2)}, u32[]{:S(2)}) async-start(f32[32,24,128]{2,1,0:T(8,128)} %get-tuple-element.13), calls=%async_computation | async-start | bytes 786432 | tf_op jit(solution)/shard_map/all_to_all | solution.py:499
  16.1 10.1 %collective-permute-start = (f32[9,8,512]{2,1,0:T(8,128)S(1)}, f32[9,8,512]{2,1,0:T(8,128)S(1)}, u32[]{:S(2)}, u32[]{:S(2)}) collective-permute-start(f32[9,8,512]{2,1,0:T(8,128)S(1)} %copy-done.4), channel_id=1, source_target_pairs={{0,1},{1,0},{2,3},{3,2},{4,5},{5,4},{6,7},{7,6},{8,9},{9,8},{10,11... | collective-permute-start | bytes 442376 | tf_op jit(solution)/shard_map/ppermute | solution.py:497
  18.3 14.1 %collective-permute-start.1 = (f32[9,8,512]{2,1,0:T(8,128)S(1)}, f32[9,8,512]{2,1,0:T(8,128)S(1)}, u32[]{:S(2)}, u32[]{:S(2)}) collective-permute-start(f32[9,8,512]{2,1,0:T(8,128)S(1)} %copy-done.3), channel_id=1, source_target_pairs={{0,31},{1,2},{2,1},{3,4},{4,3},{5,6},{6,5},{7,8},{8,7},{9,10},{10,... | collective-permute-start | bytes 442376 | tf_op jit(solution)/shard_map/ppermute | solution.py:498

commit v6 on v5

--- a/solution.py
+++ b/solution.py
@@ -59,7 +59,7 @@
     return pltpu.roll(block, 4, 0) if (g % 2 == 0) == is_up else block
 
 
-def pack_kernel(place, seams_at, scaling_at, density_at, beside, across, message, seams, scaling, density, arrived):
+def pack_kernel(place, seams_at, scaling_at, density_at, across, beside, message, seams, scaling, density, arrived):
     p = place[0]
     pairs = ((scaling_at, scaling), (density_at, density), (seams_at, seams))
     copies = [pltpu.make_async_copy(a, b, arrived.at[i]) for i, (a, b) in enumerate(pairs)]
@@ -207,7 +207,7 @@
 
 
 def heat_kernel(
-    place, seams, weight, scaling, density, beside, across, message,
+    place, seams, weight, scaling, density, across, beside, message,
     dual, marginal, weighted, up, down, mixed, chunk, table_s, table_d, column_s, column_d, edge, work,
 ):
     q = place[0]
@@ -481,7 +481,7 @@
     field = jax.ShapeDtypeStruct((FACES, ROWS, SIDE), f32)
     edge_rows = jax.ShapeDtypeStruct((FACES + FACES // 2, HALO, SIDE), f32)
     params = pltpu.CompilerParams(vmem_limit_bytes=24 * 1024 * 1024)
-    beside, across, message = pl.pallas_call(
+    across, beside, message = pl.pallas_call(
         pack_kernel,
         out_shape=(edge_rows, edge_rows, jax.ShapeDtypeStruct((tiles, 24, 128), f32)),
         in_specs=[smem] + [pl.BlockSpec(memory_space=pl.ANY)] * 3,
@@ -494,8 +494,8 @@
         ],
         name="pack",
     )(place, seams, scaling, density)
+    across = lax.ppermute(across, "tile", [(i, (i + 1 if i % 2 else i - 1) % tiles) for i in range(tiles)])
     beside = lax.ppermute(beside, "tile", [(i, i ^ 1) for i in range(tiles)])
-    across = lax.ppermute(across, "tile", [(i, (i + 1 if i % 2 else i - 1) % tiles) for i in range(tiles)])
     message = lax.all_to_all(message, "tile", 0, 0)
     rows = 384 // members
     sums = jax.ShapeDtypeStruct((members, rows + 8, 128), f32)
@@ -518,7 +518,7 @@
         ],
         compiler_params=params,
         name="heat",
-    )(place, seams, member_weights, scaling, density, beside, across, message)
+    )(place, seams, member_weights, scaling, density, across, beside, message)
     weighted = lax.all_to_all(weighted, "member", 0, 0)
     means = pl.pallas_call(
         mean_kernel,

time: 70.5 us -> 70.5 us (level)
  no operation moved by 1% of the time
where the time goes in v6:
time: 70.5 us; the launch traced here: 70.2 us
  blocking collectives  28.9 us (41%)
  starting transfers between devices  21.9 us (31%)
  Pallas kernels  11.3 us (16%)
  waiting for transfers between devices  6.58 us (9%)
  between operations  1.4 us (2%)
    all_to_all x1, blocking collectives, body(): weighted = lax.all_to_all(weighted, 'member', 0, 0)  16.4 us
    all_to_all x1, starting transfers between devices, body(): message = lax.all_to_all(message, 'tile', 0, 0)  12.9 us
    all_to_all x1, blocking collectives, body(): means = lax.all_to_all(means, 'member', 0, 0)  12.5 us
    pallas_call x1, Pallas kernels, body(): pl.pallas_call(heat_kernel, out_shape=(field, field, sums), in_specs=[sme...  7.96 us
    ppermute x1, starting transfers between devices, body(): lax.ppermute(across, 'tile', [(i, (i + 1 if i % 2 else i - 1) % tiles) fo...  7.15 us
    ppermute x1, waiting for transfers between devices, body(): lax.ppermute(across, 'tile', [(i, (i + 1 if i % 2 else i - 1) % tiles) fo...  6.57 us
    pallas_call x1, Pallas kernels, body(): pl.pallas_call(pack_kernel, out_shape=(edge_rows, edge_rows, jax.ShapeDty...  2.54 us
    ppermute x1, starting transfers between devices, body(): beside = lax.ppermute(beside, 'tile', [(i, i ^ 1) for i in range(tiles)])  1.92 us
  transfers between devices with their start and end apart: 3, of which 1 were waited for; matrix products, arithmetic and copies ran while one was open for 0% of the time, Pallas kernels for 0%

profile of v6, /device:TPU:8, one launch (start us, length us, event | category | flops | bytes accessed | tf_op | source)
XLA Modules:
  0.0 70.2 jit_solution(12299153161911695261)
XLA Ops:
  0.6 2.5 %pack.1 = (f32[9,8,512]{2,1,0:T(8,128)}, f32[9,8,512]{2,1,0:T(8,128)}, f32[32,24,128]{2,1,0:T(8,128)}) custom-call(s32[1]{0:T(128)} %bitcast.place, s32[3,4,6]{2,1,0:T(4,128)} %seams.1, f32[6,16,512]{2,1,0:T(8,128)} %bitcast.5, f32[6,16,512]{2,1,0:T(8,128)} %bitcast.8), custom_call_target="tpu_custom_call" | custom-call | tf_op jit(solution)/shard_map/pack/pallas_call | solution.py:484
  3.2 0.0 copy-start.4
  3.2 0.0 copy-start.3
  3.2 0.0 copy-start
  3.2 0.0 copy-start.1
  3.2 0.0 copy-start.2
  3.2 12.9 %all-to-all-start = ((f32[32,24,128]{2,1,0:T(8,128)}), f32[32,24,128]{2,1,0:T(8,128)S(1)}, u32[]{:S(2)}, u32[]{:S(2)}) async-start(f32[32,24,128]{2,1,0:T(8,128)} %get-tuple-element.13), calls=%async_computation | async-start | bytes 786432 | tf_op jit(solution)/shard_map/all_to_all | solution.py:499
  16.1 0.0 copy-done.4
  16.1 7.2 %collective-permute-start = (f32[9,8,512]{2,1,0:T(8,128)S(1)}, f32[9,8,512]{2,1,0:T(8,128)S(1)}, u32[]{:S(2)}, u32[]{:S(2)}) collective-permute-start(f32[9,8,512]{2,1,0:T(8,128)S(1)} %copy-done.4), channel_id=1, source_target_pairs={{0,31},{1,2},{2,1},{3,4},{4,3},{5,6},{6,5},{7,8},{8,7},{9,10},{10,... | collective-permute-start | bytes 442376 | tf_op jit(solution)/shard_map/ppermute | solution.py:497
  23.3 0.0 copy-done.3
  23.3 1.9 %collective-permute-start.1 = (f32[9,8,512]{2,1,0:T(8,128)S(1)}, f32[9,8,512]{2,1,0:T(8,128)S(1)}, u32[]{:S(2)}, u32[]{:S(2)}) collective-permute-start(f32[9,8,512]{2,1,0:T(8,128)S(1)} %copy-done.3), channel_id=1, source_target_pairs={{0,1},{1,0},{2,3},{3,2},{4,5},{5,4},{6,7},{7,6},{8,9},{9,8},{10,11... | collective-permute-start | bytes 442376 | tf_op jit(solution)/shard_map/ppermute | solution.py:498
  25.9 6.6 %collective-permute-done.across = f32[9,8,512]{2,1,0:T(8,128)S(1)} collective-permute-done((f32[9,8,512]{2,1,0:T(8,128)S(1)}, f32[9,8,512]{2,1,0:T(8,128)S(1)}, u32[]{:S(2)}, u32[]{:S(2)}) %collective-permute-start) | collective-permute-done | bytes 147488 | tf_op jit(solution)/shard_map/ppermute | solution.py:497
  32.4 0.0 collective-permute-done.1.beside
  32.4 0.0 all-to-all-done.message
  32.4 0.0 copy-done
  32.4 0.0 copy-done.1
  32.5 0.0 copy-done.2
  32.5 8.0 %heat.1 = (f32[6,16,512]{2,1,0:T(8,128)}, f32[6,16,512]{2,1,0:T(8,128)S(1)}, f32[16,32,128]{2,1,0:T(8,128)S(1)}) custom-call(s32[1]{0:T(128)} %bitcast.place, s32[3,4,6]{2,1,0:T(4,128)S(1)} %copy-done.2, f32[1]{0:T(128)S(6)} %copy.7.weight, f32[6,16,512]{2,1,0:T(8,128)S(1)} %bitcast.6, f32[6,16,512]{2,1,0:T(8,128)S(1)} %bitcast.9, ...), custom_call_target="tpu_custom_call" | custom-call | tf_op jit(solution)/shard_map/heat/pallas_call | solution.py:502
  40.4 16.4 %all_to_all.15.parts = f32[16,32,128]{2,1,0:T(8,128)S(1)} all-to-all(f32[16,32,128]{2,1,0:T(8,128)S(1)} %get-tuple-element.14), channel_id=1, replica_groups=mesh['member'=16,'tile'=32] {'member'}, dimensions={0} | all-to-all | bytes 524288 | tf_op jit(solution)/shard_map/all_to_all | solution.py:522
  56.9 12.5 %all_to_all.16.parts = f32[16,24,128]{2,1,0:T(8,128)S(1)} all-to-all(f32[16,24,128]{2,1,0:T(8,128)S(1)} %mean.1), channel_id=1, replica_groups=mesh['member'=16,'tile'=32] {'member'}, dimensions={0} | all-to-all | bytes 393216 | tf_op jit(solution)/shard_map/all_to_all | solution.py:531
  69.4 0.8 %update.1 = (f32[6,16,512]{2,1,0:T(8,128)}, f32[6,16,512]{2,1,0:T(8,128)}) custom-call(f32[16,24,128]{2,1,0:T(8,128)S(1)} %all_to_all.16.parts, f32[6,16,512]{2,1,0:T(8,128)S(1)} %bitcast.7, f32[6,16,512]{2,1,0:T(8,128)S(1)} %get-tuple-element.15.marginal), custom_call_target="tpu_custom_call" | custom-call | tf_op jit(solution)/shard_map/update/pallas_call | solution.py:532
  (1 shorter events, 0.0 us)
Async XLA Ops:
  3.2 12.9 %copy-start.4 = (f32[9,8,512]{2,1,0:T(8,128)S(1)}, f32[9,8,512]{2,1,0:T(8,128)}, u32[]{:S(2)}) copy-start(f32[9,8,512]{2,1,0:T(8,128)} %get-tuple-element.11) | copy-start | bytes 442372
  3.2 20.1 %copy-start.3 = (f32[9,8,512]{2,1,0:T(8,128)S(1)}, f32[9,8,512]{2,1,0:T(8,128)}, u32[]{:S(2)}) copy-start(f32[9,8,512]{2,1,0:T(8,128)} %get-tuple-element.12) | copy-start | bytes 442372
  3.2 29.2 %copy-start = (f32[1,6,16,512]{3,2,1,0:T(8,128)S(1)}, f32[1,6,16,512]{3,2,1,0:T(8,128)}, u32[]{:S(2)}) copy-start(f32[1,6,16,512]{3,2,1,0:T(8,128)} %param.5) | copy-start | bytes 589828
  3.2 29.2 %copy-start.1 = (f32[1,6,16,512]{3,2,1,0:T(8,128)S(1)}, f32[1,6,16,512]{3,2,1,0:T(8,128)}, u32[]{:S(2)}) copy-start(f32[1,6,16,512]{3,2,1,0:T(8,128)} %param.4) | copy-start | bytes 589828
  3.2 29.2 %copy-start.2 = (s32[3,4,6]{2,1,0:T(4,128)S(1)}, s32[3,4,6]{2,1,0:T(4,128)}, u32[]{:S(2)}) copy-start(s32[3,4,6]{2,1,0:T(4,128)} %seams.1) | copy-start | bytes 868
  3.2 29.2 %all-to-all-start = ((f32[32,24,128]{2,1,0:T(8,128)}), f32[32,24,128]{2,1,0:T(8,128)S(1)}, u32[]{:S(2)}, u32[]{:S(2)}) async-start(f32[32,24,128]{2,1,0:T(8,128)} %get-tuple-element.13), calls=%async_computation | async-start | bytes 786432 | tf_op jit(solution)/shard_map/all_to_all | solution.py:499
  16.1 16.3 %collective-permute-start = (f32[9,8,512]{2,1,0:T(8,128)S(1)}, f32[9,8,512]{2,1,0:T(8,128)S(1)}, u32[]{:S(2)}, u32[]{:S(2)}) collective-permute-start(f32[9,8,512]{2,1,0:T(8,128)S(1)} %copy-done.4), channel_id=1, source_target_pairs={{0,31},{1,2},{2,1},{3,4},{4,3},{5,6},{6,5},{7,8},{8,7},{9,10},{10,... | collective-permute-start | bytes 442376 | tf_op jit(solution)/shard_map/ppermute | solution.py:497
  23.3 9.1 %collective-permute-start.1 = (f32[9,8,512]{2,1,0:T(8,128)S(1)}, f32[9,8,512]{2,1,0:T(8,128)S(1)}, u32[]{:S(2)}, u32[]{:S(2)}) collective-permute-start(f32[9,8,512]{2,1,0:T(8,128)S(1)} %copy-done.3), channel_id=1, source_target_pairs={{0,1},{1,0},{2,3},{3,2},{4,5},{5,4},{6,7},{7,6},{8,9},{9,8},{10,11... | collective-permute-start | bytes 442376 | tf_op jit(solution)/shard_map/ppermute | solution.py:498

commit v7 on v6

--- a/solution.py
+++ b/solution.py
@@ -139,11 +139,22 @@
                         message[q, 8 * t : 8 * t + 8, :] = full[:, 128 * a : 128 * a + 128]
 
 
-def diffuse(x):
-    rows, lanes = x.shape
-    vertical = pltpu.roll(x, 1, 0) + pltpu.roll(x, rows - 1, 0)
-    lateral = pltpu.roll(x, 1, 1) + pltpu.roll(x, lanes - 1, 1)
-    return x + KAPPA * ((vertical + lateral) - 4.0 * x)
+def diffuse(blocks):
+    lane = iota((8, 128), 1)
+    sub = iota((8, 128), 0)
+    high, wide = len(blocks), len(blocks[0])
+    result = []
+    for i in range(high):
+        line = []
+        for j in range(wide):
+            x = blocks[i][j]
+            above = pltpu.roll(jnp.where(sub == 7, blocks[i - 1][j], x), 1, 0)
+            below = pltpu.roll(jnp.where(sub == 0, blocks[(i + 1) % high][j], x), 7, 0)
+            left = pltpu.roll(jnp.where(lane == 127, blocks[i][j - 1], x), 1, 1)
+            right = pltpu.roll(jnp.where(lane == 0, blocks[i][(j + 1) % wide], x), 127, 1)
+            line.append((1.0 - 4.0 * KAPPA) * x + KAPPA * ((above + below) + (left + right)))
+        result.append(line)
+    return result
 
 
 def diffuse_strip(x, where):
@@ -390,22 +401,34 @@
                 work[k, t, 24:, :] = jnp.where((lane % 64 >= 24) & (lane % 64 < 40), rows[2], work[k, t, 24:, :])
 
     def run(where):
-        for f in range(FACES):
-            above = [edge[k, f] if where == "first" else halo_rows(up, k, f, True) for k in range(2)]
-            below = [edge[k, f] if where == "last" else halo_rows(down, k, f, False) for k in range(2)]
-            x = jnp.concatenate([above[0], scaling[f], below[0]], axis=0)
+        def tall(k, f):
+            field = (scaling, density)[k]
+            above = edge[k, f] if where == "first" else halo_rows(up, k, f, True)
+            below = edge[k, f] if where == "last" else halo_rows(down, k, f, False)
+            lines = (above, field[f, :HALO], field[f, HALO:], below)
+            return [[line[:, at : at + 128] for at in range(0, SIDE, 128)] for line in lines]
+
+        for some in (range(0, 3), range(3, FACES)):
+            x = [tall(0, f) for f in some]
             for _ in range(STEPS):
-                x = diffuse(x)
-            y = jnp.concatenate([above[1], density[f], below[1]], axis=0) / x
-            dual[f] = y[HALO : HALO + ROWS]
+                x = [diffuse(v) for v in x]
+            y = [
+                [[d / h for d, h in zip(*lines)] for lines in zip(tall(1, f), v)]
+                for f, v in zip(some, x)
+            ]
+            for f, v in zip(some, y):
+                for i in range(2):
+                    for j in range(4):
+                        dual[f, 8 * i : 8 * i + 8, 128 * j : 128 * j + 128] = v[i + 1][j]
             for _ in range(STEPS):
-                y = diffuse(y)
-            m = scaling[f] * y[HALO : HALO + ROWS]
-            marginal[f] = m
-            scaled = share * jnp.log(m)
-            for i in range(2):
-                for j in range(4):
-                    put_weighted(weighted, scaled[8 * i : 8 * i + 8, 128 * j : 128 * j + 128], f, i, j)
+                y = [diffuse(v) for v in y]
+            for f, v in zip(some, y):
+                for i in range(2):
+                    for j in range(4):
+                        at = (f, slice(8 * i, 8 * i + 8), slice(128 * j, 128 * j + 128))
+                        m = scaling[at] * v[i + 1][j]
+                        marginal[at] = m
+                        put_weighted(weighted, share * jnp.log(m), f, i, j)
         x = [work[0, t] for t in range(3)]
         for _ in range(STEPS):
             x = [diffuse_strip(v, where) for v in x]

time: 70.5 us -> 68.4 us (0.970)
  Pallas kernels: 11.3 us -> 9.19 us
    pallas_call x1, Pallas kernels: 7.96 us -> 5.83 us  [body(): pl.pallas_call(heat_kernel, out_shape=(field, field, sums), in_specs=[sme...]
where the time goes in v7:
time: 68.4 us; the launch traced here: 68.1 us
  blocking collectives  28.9 us (42%)
  starting transfers between devices  21.9 us (32%)
  Pallas kernels  9.19 us (13%)
  waiting for transfers between devices  6.58 us (10%)
  between operations  1.4 us (2%)
    all_to_all x1, blocking collectives, body(): weighted = lax.all_to_all(weighted, 'member', 0, 0)  16.4 us
    all_to_all x1, starting transfers between devices, body(): message = lax.all_to_all(message, 'tile', 0, 0)  12.9 us
    all_to_all x1, blocking collectives, body(): means = lax.all_to_all(means, 'member', 0, 0)  12.5 us
    ppermute x1, starting transfers between devices, body(): lax.ppermute(across, 'tile', [(i, (i + 1 if i % 2 else i - 1) % tiles) fo...  7.15 us
    ppermute x1, waiting for transfers between devices, body(): lax.ppermute(across, 'tile', [(i, (i + 1 if i % 2 else i - 1) % tiles) fo...  6.57 us
    pallas_call x1, Pallas kernels, body(): pl.pallas_call(heat_kernel, out_shape=(field, field, sums), in_specs=[sme...  5.83 us
    pallas_call x1, Pallas kernels, body(): pl.pallas_call(pack_kernel, out_shape=(edge_rows, edge_rows, jax.ShapeDty...  2.54 us
    ppermute x1, starting transfers between devices, body(): beside = lax.ppermute(beside, 'tile', [(i, i ^ 1) for i in range(tiles)])  1.92 us
  transfers between devices with their start and end apart: 3, of which 1 were waited for; matrix products, arithmetic and copies ran while one was open for 0% of the time, Pallas kernels for 0%

profile of v7, /device:TPU:8, one launch (start us, length us, event | category | flops | bytes accessed | tf_op | source)
XLA Modules:
  0.0 68.1 jit_solution(8749803140212942224)
XLA Ops:
  0.6 2.5 %pack.1 = (f32[9,8,512]{2,1,0:T(8,128)}, f32[9,8,512]{2,1,0:T(8,128)}, f32[32,24,128]{2,1,0:T(8,128)}) custom-call(s32[1]{0:T(128)} %bitcast.place, s32[3,4,6]{2,1,0:T(4,128)} %seams.1, f32[6,16,512]{2,1,0:T(8,128)} %bitcast.5, f32[6,16,512]{2,1,0:T(8,128)} %bitcast.8), custom_call_target="tpu_custom_call" | custom-call | tf_op jit(solution)/shard_map/pack/pallas_call | solution.py:507
  3.2 0.0 copy-start.4
  3.2 0.0 copy-start.3
  3.2 0.0 copy-start
  3.2 0.0 copy-start.1
  3.2 0.0 copy-start.2
  3.2 12.9 %all-to-all-start = ((f32[32,24,128]{2,1,0:T(8,128)}), f32[32,24,128]{2,1,0:T(8,128)S(1)}, u32[]{:S(2)}, u32[]{:S(2)}) async-start(f32[32,24,128]{2,1,0:T(8,128)} %get-tuple-element.13), calls=%async_computation | async-start | bytes 786432 | tf_op jit(solution)/shard_map/all_to_all | solution.py:522
  16.1 0.0 copy-done.4
  16.1 7.2 %collective-permute-start = (f32[9,8,512]{2,1,0:T(8,128)S(1)}, f32[9,8,512]{2,1,0:T(8,128)S(1)}, u32[]{:S(2)}, u32[]{:S(2)}) collective-permute-start(f32[9,8,512]{2,1,0:T(8,128)S(1)} %copy-done.4), channel_id=1, source_target_pairs={{0,31},{1,2},{2,1},{3,4},{4,3},{5,6},{6,5},{7,8},{8,7},{9,10},{10,... | collective-permute-start | bytes 442376 | tf_op jit(solution)/shard_map/ppermute | solution.py:520
  23.3 0.0 copy-done.3
  23.3 1.9 %collective-permute-start.1 = (f32[9,8,512]{2,1,0:T(8,128)S(1)}, f32[9,8,512]{2,1,0:T(8,128)S(1)}, u32[]{:S(2)}, u32[]{:S(2)}) collective-permute-start(f32[9,8,512]{2,1,0:T(8,128)S(1)} %copy-done.3), channel_id=1, source_target_pairs={{0,1},{1,0},{2,3},{3,2},{4,5},{5,4},{6,7},{7,6},{8,9},{9,8},{10,11... | collective-permute-start | bytes 442376 | tf_op jit(solution)/shard_map/ppermute | solution.py:521
  25.9 6.6 %collective-permute-done.across = f32[9,8,512]{2,1,0:T(8,128)S(1)} collective-permute-done((f32[9,8,512]{2,1,0:T(8,128)S(1)}, f32[9,8,512]{2,1,0:T(8,128)S(1)}, u32[]{:S(2)}, u32[]{:S(2)}) %collective-permute-start) | collective-permute-done | bytes 147488 | tf_op jit(solution)/shard_map/ppermute | solution.py:520
  32.4 0.0 collective-permute-done.1.beside
  32.4 0.0 all-to-all-done.message
  32.4 0.0 copy-done
  32.4 0.0 copy-done.1
  32.5 0.0 copy-done.2
  32.5 5.8 %heat.1 = (f32[6,16,512]{2,1,0:T(8,128)}, f32[6,16,512]{2,1,0:T(8,128)S(1)}, f32[16,32,128]{2,1,0:T(8,128)S(1)}) custom-call(s32[1]{0:T(128)} %bitcast.place, s32[3,4,6]{2,1,0:T(4,128)S(1)} %copy-done.2, f32[1]{0:T(128)S(6)} %copy.7.weight, f32[6,16,512]{2,1,0:T(8,128)S(1)} %bitcast.6, f32[6,16,512]{2,1,0:T(8,128)S(1)} %bitcast.9, ...), custom_call_target="tpu_custom_call" | custom-call | tf_op jit(solution)/shard_map/heat/pallas_call | solution.py:525
  38.3 16.4 %all_to_all.15.parts = f32[16,32,128]{2,1,0:T(8,128)S(1)} all-to-all(f32[16,32,128]{2,1,0:T(8,128)S(1)} %get-tuple-element.14), channel_id=1, replica_groups=mesh['member'=16,'tile'=32] {'member'}, dimensions={0} | all-to-all | bytes 524288 | tf_op jit(solution)/shard_map/all_to_all | solution.py:545
  54.8 12.5 %all_to_all.16.parts = f32[16,24,128]{2,1,0:T(8,128)S(1)} all-to-all(f32[16,24,128]{2,1,0:T(8,128)S(1)} %mean.1), channel_id=1, replica_groups=mesh['member'=16,'tile'=32] {'member'}, dimensions={0} | all-to-all | bytes 393216 | tf_op jit(solution)/shard_map/all_to_all | solution.py:554
  67.3 0.8 %update.1 = (f32[6,16,512]{2,1,0:T(8,128)}, f32[6,16,512]{2,1,0:T(8,128)}) custom-call(f32[16,24,128]{2,1,0:T(8,128)S(1)} %all_to_all.16.parts, f32[6,16,512]{2,1,0:T(8,128)S(1)} %bitcast.7, f32[6,16,512]{2,1,0:T(8,128)S(1)} %get-tuple-element.15.marginal), custom_call_target="tpu_custom_call" | custom-call | tf_op jit(solution)/shard_map/update/pallas_call | solution.py:555
  (1 shorter events, 0.0 us)
Async XLA Ops:
  3.2 12.9 %copy-start.4 = (f32[9,8,512]{2,1,0:T(8,128)S(1)}, f32[9,8,512]{2,1,0:T(8,128)}, u32[]{:S(2)}) copy-start(f32[9,8,512]{2,1,0:T(8,128)} %get-tuple-element.11) | copy-start | bytes 442372
  3.2 20.1 %copy-start.3 = (f32[9,8,512]{2,1,0:T(8,128)S(1)}, f32[9,8,512]{2,1,0:T(8,128)}, u32[]{:S(2)}) copy-start(f32[9,8,512]{2,1,0:T(8,128)} %get-tuple-element.12) | copy-start | bytes 442372
  3.2 29.2 %copy-start = (f32[1,6,16,512]{3,2,1,0:T(8,128)S(1)}, f32[1,6,16,512]{3,2,1,0:T(8,128)}, u32[]{:S(2)}) copy-start(f32[1,6,16,512]{3,2,1,0:T(8,128)} %param.5) | copy-start | bytes 589828
  3.2 29.2 %copy-start.1 = (f32[1,6,16,512]{3,2,1,0:T(8,128)S(1)}, f32[1,6,16,512]{3,2,1,0:T(8,128)}, u32[]{:S(2)}) copy-start(f32[1,6,16,512]{3,2,1,0:T(8,128)} %param.4) | copy-start | bytes 589828
  3.2 29.2 %copy-start.2 = (s32[3,4,6]{2,1,0:T(4,128)S(1)}, s32[3,4,6]{2,1,0:T(4,128)}, u32[]{:S(2)}) copy-start(s32[3,4,6]{2,1,0:T(4,128)} %seams.1) | copy-start | bytes 868
  3.2 29.2 %all-to-all-start = ((f32[32,24,128]{2,1,0:T(8,128)}), f32[32,24,128]{2,1,0:T(8,128)S(1)}, u32[]{:S(2)}, u32[]{:S(2)}) async-start(f32[32,24,128]{2,1,0:T(8,128)} %get-tuple-element.13), calls=%async_computation | async-start | bytes 786432 | tf_op jit(solution)/shard_map/all_to_all | solution.py:522
  16.1 16.3 %collective-permute-start = (f32[9,8,512]{2,1,0:T(8,128)S(1)}, f32[9,8,512]{2,1,0:T(8,128)S(1)}, u32[]{:S(2)}, u32[]{:S(2)}) collective-permute-start(f32[9,8,512]{2,1,0:T(8,128)S(1)} %copy-done.4), channel_id=1, source_target_pairs={{0,31},{1,2},{2,1},{3,4},{4,3},{5,6},{6,5},{7,8},{8,7},{9,10},{10,... | collective-permute-start | bytes 442376 | tf_op jit(solution)/shard_map/ppermute | solution.py:520
  23.3 9.1 %collective-permute-start.1 = (f32[9,8,512]{2,1,0:T(8,128)S(1)}, f32[9,8,512]{2,1,0:T(8,128)S(1)}, u32[]{:S(2)}, u32[]{:S(2)}) collective-permute-start(f32[9,8,512]{2,1,0:T(8,128)S(1)} %copy-done.3), channel_id=1, source_target_pairs={{0,1},{1,0},{2,3},{3,2},{4,5},{5,4},{6,7},{7,6},{8,9},{9,8},{10,11... | collective-permute-start | bytes 442376 | tf_op jit(solution)/shard_map/ppermute | solution.py:521

commit v8 on v7

--- a/solution.py
+++ b/solution.py
@@ -37,15 +37,42 @@
     return strips
 
 
-def spread(block):
-    return [pltpu.roll(block, 96 - 32 * b, 1) for b in range(3)]
-
-
-def unspread(b0, b1, b2):
+PIECE = 18
+
+
+def put_message(message, q, t0, t1, t2):
     lane = iota((8, 128), 1)
-    return jnp.where(
-        lane < 32, pltpu.roll(b0, 32, 1), jnp.where(lane < 64, pltpu.roll(b1, 64, 1), pltpu.roll(b2, 96, 1))
-    )
+    sub = iota((8, 128), 0)
+    at = PIECE * q
+    message[at : at + 8, :] = jnp.where(lane < 96, t0, pltpu.roll(t2, 96, 1))
+    message[at + 8 : at + 16, :] = jnp.where(lane < 96, t1, pltpu.roll(t2, 64, 1))
+    rest = jnp.take_along_axis(t2, 64 + lane % 32, axis=1)
+    rest = jnp.where(lane // 32 == sub % 4, rest, 0.0)
+    message[at + 16 : at + 17, :] = jnp.sum(rest[:4], axis=0, keepdims=True)
+    message[at + 17 : at + 18, :] = jnp.sum(rest[4:], axis=0, keepdims=True)
+
+
+def get_message(message, p):
+    lane = iota((8, 128), 1)
+    sub = iota((8, 128), 0)
+    at = PIECE * p
+    t0 = message[pl.ds(at, 8), :]
+    t1 = message[pl.ds(at + 8, 8), :]
+    rest = jnp.where(sub < 4, message[pl.ds(at + 16, 1), :], message[pl.ds(at + 17, 1), :])
+    rest = jnp.take_along_axis(rest, (lane + 64 + 32 * (sub % 4)) % 128, axis=1)
+    t2 = jnp.where(lane < 32, pltpu.roll(t0, 32, 1), jnp.where(lane < 64, pltpu.roll(t1, 64, 1), rest))
+    return t0, t1, t2
+
+
+def join_density(near, far):
+    lane = iota((8, 128), 1) % 16
+    moved = jnp.where(lane < 8, pltpu.roll(far, 124, 1), pltpu.roll(far, 4, 1))
+    return jnp.where((lane >= 4) & (lane < 12), near, moved)
+
+
+def far_density(block):
+    lane = iota((8, 128), 1) % 16
+    return jnp.where(lane < 8, pltpu.roll(block, 4, 1), pltpu.roll(block, 124, 1))
 
 
 def join_halves(low, high):
@@ -68,7 +95,7 @@
     for copy in copies:
         copy.wait()
     is_even = lax.rem(p, 2) == 0
-    count = message.shape[0]
+    count = message.shape[0] // PIECE
     lane = iota((8, 128), 1)
     sub = iota((8, 128), 0)
     ups = [scaling[g, HALO:] for g in range(FACES)]
@@ -82,34 +109,37 @@
         across[b] = jnp.where(is_even, d, u)
     vs = column_strips(lambda g: scaling[g, :, :128], lambda g: scaling[g, :, SIDE - 128 :])
     vd = column_strips(lambda g: density[g, :, :128], lambda g: density[g, :, SIDE - 128 :])
-    tail = spread(vd[8:])
-    head = (vs[:8], vs[8:], vd[:8])
-    block = jnp.concatenate([jnp.where(lane < 96, head[b], tail[b]) for b in range(3)], axis=0)
+    columns = (vs[:8], vs[8:], join_density(vd[:8], vd[8:]))
     is_last = p == count - 1
     is_edge = (p == 0) | is_last
 
     @pl.when(jnp.logical_not(is_edge))
     def _():
         for q in range(count):
-            message[q] = block
+            put_message(message, q, *columns)
 
     @pl.when(is_edge)
     def _():
-        message[0] = block
-        message[count - 1] = block
+        put_message(message, 0, *columns)
+        put_message(message, count - 1, *columns)
         e = is_last.astype(jnp.int32)
         base = pl.multiple_of(e * 8, 8)
         own_s = jnp.where(is_last, vs[:8], vs[8:])
         own_d = jnp.where(is_last, vd[:8], vd[8:])
-        far = jnp.where(is_last, pltpu.roll(own_d, 5, 0), pltpu.roll(own_d, 3, 0))
-        free = jnp.where(is_last, (sub >= 5).astype(jnp.int32), (sub <= 2).astype(jnp.int32)) == 1
-        lane16 = lane % 16
-        coded = jnp.where(
-            free & (lane16 < 4),
-            pltpu.roll(far, 124, 1),
-            jnp.where(free & (lane16 >= 12), pltpu.roll(far, 4, 1), own_s),
+        turned_d = pltpu.roll(own_d, 4, 0)
+        even_d, odd_d = jnp.where(is_last, own_d, turned_d), jnp.where(is_last, turned_d, own_d)
+        lane32 = lane % 32
+
+        def coded(v, h):
+            return jnp.where(lane32 < 8, pltpu.roll(v, 120 - 16 * h, 1), pltpu.roll(v, 24 - 16 * h, 1))
+
+        room = jnp.where(is_last, 7 - sub, sub)
+        free = (lane32 <= room) | (lane32 >= 31 - room)
+        extra = (
+            (free, coded(own_s, 0)),
+            (free, coded(own_s, 1)),
+            ((lane32 < 4) | (lane32 >= 28), jnp.where(sub < 4, coded(even_d, 0), coded(odd_d, 1))),
         )
-        extra = spread(coded)
         pieces = []
         for g in range(FACES):
             turned = seams[2, e, g] == 1
@@ -124,19 +154,20 @@
             low = jnp.where(is_last, pltpu.roll(d0, 4, 0), d0)
             high = jnp.where(is_last, d1, pltpu.roll(d1, 4, 0))
             blocks.append((s0, s1, jnp.where(sub_wide < 4, low, high)))
-        for t in range(3):
-            tail_t = jnp.concatenate([extra[t]] * 4, axis=1)
-            for r in range(8):
+        for r in range(8):
+            full = []
+            for t in range(3):
                 moved = [pltpu.roll(blocks[b][t], (32 * b - 16 * r + 8) % SIDE, 1) for b in range(3)]
-                full = jnp.where(
-                    lane_wide < 32,
-                    moved[0],
-                    jnp.where(lane_wide < 64, moved[1], jnp.where(lane_wide < 96, moved[2], tail_t)),
+                full.append(
+                    jnp.where(lane_wide < 32, moved[0], jnp.where(lane_wide < 64, moved[1], moved[2]))
                 )
-                for a in range(4):
-                    q = 8 * a + r
-                    if 0 < q < count - 1:
-                        message[q, 8 * t : 8 * t + 8, :] = full[:, 128 * a : 128 * a + 128]
+            for a in range(4):
+                q = 8 * a + r
+                tiles = [x[:, 128 * a : 128 * a + 128] for x in full]
+                if q in (1, count - 2):
+                    tiles = [jnp.where(mask, other, tile) for (mask, other), tile in zip(extra, tiles)]
+                if 0 < q < count - 1:
+                    put_message(message, q, *tiles)
 
 
 def diffuse(blocks):
@@ -222,7 +253,7 @@
     dual, marginal, weighted, up, down, mixed, chunk, table_s, table_d, column_s, column_d, edge, work,
 ):
     q = place[0]
-    count = message.shape[0]
+    count = message.shape[0] // PIECE
     last = count - 1
     is_even = lax.rem(q, 2) == 0
     for b in range(FACES + FACES // 2):
@@ -237,24 +268,35 @@
     for k in range(weighted.shape[0]):
         weighted[k, 8 * per :, :] = jnp.full((8, 128), share, jnp.float32)
 
-    def far_rows(p):
-        return unspread(message[p, :8, :], message[p, 8:16, :], message[p, 16:24, :])
-
-    mirror, upper, lower = last - q, jnp.minimum(last + 1 - q, last), jnp.maximum(last - 1 - q, 0)
-    coded = far_rows(jnp.where(q == 1, last, 0))
-    near = jnp.where(q == 1, pltpu.roll(coded, 3, 0), pltpu.roll(coded, 5, 0))
-    coded_d = jnp.where(lane % 16 < 8, pltpu.roll(near, 4, 1), pltpu.roll(near, 124, 1))
+    lane32 = lane % 32
+    tiles = get_message(message, jnp.where(q == 1, last, 0))
+    turned_d = pltpu.roll(tiles[2], 4, 0)
+    even_d, odd_d = jnp.where(q == 1, tiles[2], turned_d), jnp.where(q == 1, turned_d, tiles[2])
+
+    def decoded(even, odd):
+        is_right = lane % 16 < 8
+        return jnp.where(
+            lane32 < 16,
+            jnp.where(is_right, pltpu.roll(even, 104, 1), pltpu.roll(even, 8, 1)),
+            jnp.where(is_right, pltpu.roll(odd, 120, 1), pltpu.roll(odd, 24, 1)),
+        )
+
+    coded_s = decoded(tiles[0], tiles[1])
+    coded_d = decoded(even_d, odd_d)
+    mirror = get_message(message, last - q)
+    upper = get_message(message, jnp.minimum(last + 1 - q, last))
+    lower = get_message(message, jnp.maximum(last - 1 - q, 0))
     parts_s = (
-        jnp.where(q == last - 1, coded, message[lower, 8:16, :]),
-        message[mirror, :8, :],
-        message[mirror, 8:16, :],
-        jnp.where(q == 1, coded, message[upper, :8, :]),
+        jnp.where(q == last - 1, coded_s, lower[1]),
+        mirror[0],
+        mirror[1],
+        jnp.where(q == 1, coded_s, upper[0]),
     )
     parts_d = (
-        jnp.where(q == last - 1, coded_d, far_rows(lower)),
-        message[mirror, 16:24, :],
-        far_rows(mirror),
-        jnp.where(q == 1, coded_d, message[upper, 16:24, :]),
+        jnp.where(q == last - 1, coded_d, far_density(lower[2])),
+        mirror[2],
+        far_density(mirror[2]),
+        jnp.where(q == 1, coded_d, upper[2]),
     )
     for base, parts in ((0, parts_s), (TALL, parts_d)):
         for block in range(4):
@@ -267,12 +309,11 @@
     @pl.when(jnp.logical_not(is_edge))
     def _():
         for e in range(2):
-            p = e * last
+            tiles = get_message(message, e * last)
             for g in range(FACES):
                 b, h = g // 2, g % 2
                 turn = (128 - 32 * b) % 128
-                s = message[p, 8 * h : 8 * h + 8, :]
-                d = message[p, 16:24, :]
+                s, d = tiles[h], tiles[2]
                 if turn:
                     s, d = pltpu.roll(s, turn, 1), pltpu.roll(d, turn, 1)
                 if h != e:
@@ -289,9 +330,11 @@
 
             def gather(p, carry):
                 at = pl.multiple_of(16 * p, 16)
-                column_s[pl.ds(at, 16), :] = message[p, :16, :]
-                column_d[pl.ds(at, 8), :] = message[p, 16:24, :]
-                column_d[pl.ds(at + 8, 8), :] = far_rows(p)
+                t0, t1, t2 = get_message(message, p)
+                column_s[pl.ds(at, 8), :] = t0
+                column_s[pl.ds(at + 8, 8), :] = t1
+                column_d[pl.ds(at, 8), :] = t2
+                column_d[pl.ds(at + 8, 8), :] = far_density(t2)
                 return carry
 
             lax.fori_loop(0, count, gather, 0, unroll=8)
@@ -506,7 +549,7 @@
     params = pltpu.CompilerParams(vmem_limit_bytes=24 * 1024 * 1024)
     across, beside, message = pl.pallas_call(
         pack_kernel,
-        out_shape=(edge_rows, edge_rows, jax.ShapeDtypeStruct((tiles, 24, 128), f32)),
+        out_shape=(edge_rows, edge_rows, jax.ShapeDtypeStruct((PIECE * tiles, 128), f32)),
         in_specs=[smem] + [pl.BlockSpec(memory_space=pl.ANY)] * 3,
         out_specs=(vmem, vmem, vmem),
         scratch_shapes=[
@@ -519,7 +562,8 @@
     )(place, seams, scaling, density)
     across = lax.ppermute(across, "tile", [(i, (i + 1 if i % 2 else i - 1) % tiles) for i in range(tiles)])
     beside = lax.ppermute(beside, "tile", [(i, i ^ 1) for i in range(tiles)])
-    message = lax.all_to_all(message, "tile", 0, 0)
+    message = lax.all_to_all(message.reshape(tiles, PIECE * 128), "tile", 0, 0, tiled=True)
+    message = message.reshape(PIECE * tiles, 128)
     rows = 384 // members
     sums = jax.ShapeDtypeStruct((members, rows + 8, 128), f32)
     dual, marginal, weighted = pl.pallas_call(

time: 68.4 us -> 67.1 us (0.981)
  waiting for transfers between devices: 6.58 us -> 4.53 us
  Pallas kernels: 9.19 us -> 10 us
    ppermute x1, waiting for transfers between devices: 6.57 us -> 4.53 us  [body(): lax.ppermute(across, 'tile', [(i, (i + 1 if i % 2 else i - 1) % tiles) fo...]
where the time goes in v8:
time: 67.1 us; the launch traced here: 66.7 us
  blocking collectives  28.9 us (43%)
  starting transfers between devices  21.8 us (32%)
  Pallas kernels  10 us (15%)
  waiting for transfers between devices  4.53 us (7%)
  between operations  1.38 us (2%)
    all_to_all x1, blocking collectives, body(): weighted = lax.all_to_all(weighted, 'member', 0, 0)  16.4 us
    all_to_all x1, starting transfers between devices, body(): lax.all_to_all(message.reshape(tiles, PIECE * 128), 'tile', 0, 0, tiled=T...  12.7 us
    all_to_all x1, blocking collectives, body(): means = lax.all_to_all(means, 'member', 0, 0)  12.5 us
    ppermute x1, starting transfers between devices, body(): lax.ppermute(across, 'tile', [(i, (i + 1 if i % 2 else i - 1) % tiles) fo...  7.15 us
    pallas_call x1, Pallas kernels, body(): pl.pallas_call(heat_kernel, out_shape=(field, field, sums), in_specs=[sme...  6.14 us
    ppermute x1, waiting for transfers between devices, body(): lax.ppermute(across, 'tile', [(i, (i + 1 if i % 2 else i - 1) % tiles) fo...  4.53 us
    pallas_call x1, Pallas kernels, body(): pl.pallas_call(pack_kernel, out_shape=(edge_rows, edge_rows, jax.ShapeDty...  3.04 us
    ppermute x1, starting transfers between devices, body(): beside = lax.ppermute(beside, 'tile', [(i, i ^ 1) for i in range(tiles)])  1.92 us
  transfers between devices with their start and end apart: 3, of which 1 were waited for; matrix products, arithmetic and copies ran while one was open for 0% of the time, Pallas kernels for 0%

profile of v8, /device:TPU:8, one launch (start us, length us, event | category | flops | bytes accessed | tf_op | source)
XLA Modules:
  0.0 66.7 jit_solution(13009890938688466953)
XLA Ops:
  0.6 3.0 %pack.1 = (f32[9,8,512]{2,1,0:T(8,128)}, f32[9,8,512]{2,1,0:T(8,128)}, f32[576,128]{1,0:T(8,128)}) custom-call(s32[1]{0:T(128)} %bitcast.place, s32[3,4,6]{2,1,0:T(4,128)} %seams.1, f32[6,16,512]{2,1,0:T(8,128)} %bitcast.7, f32[6,16,512]{2,1,0:T(8,128)} %bitcast.11), custom_call_target="tpu_custom_call" | custom-call | tf_op jit(solution)/shard_map/pack/pallas_call | solution.py:550
  3.7 0.0 copy-start.3
  3.7 0.0 copy-start
  3.7 0.0 copy-start.1
  3.7 12.7 %all-to-all-start = ((f32[32,1,2304]{2,1,0:T(1,128)}), f32[32,1,2304]{2,1,0:T(1,128)S(1)}, u32[]{:S(2)}, u32[]{:S(2)}) async-start(f32[32,1,2304]{2,1,0:T(1,128)} %bitcast.13), calls=%async_computation | async-start | bytes 589824 | tf_op jit(solution)/shard_map/all_to_all | solution.py:565
  16.5 0.0 copy-start.2
  16.5 7.2 %collective-permute-start = (f32[9,8,512]{2,1,0:T(8,128)}, f32[9,8,512]{2,1,0:T(8,128)S(1)}, u32[]{:S(2)}, u32[]{:S(2)}) collective-permute-start(f32[9,8,512]{2,1,0:T(8,128)} %get-tuple-element.11), channel_id=1, source_target_pairs={{0,31},{1,2},{2,1},{3,4},{4,3},{5,6},{6,5},{7,8},{8,7},{9,10},{10,... | collective-permute-start | bytes 442376 | tf_op jit(solution)/shard_map/ppermute | solution.py:563
  23.6 0.0 copy-done.3
  23.7 1.9 %collective-permute-start.1 = (f32[9,8,512]{2,1,0:T(8,128)S(1)}, f32[9,8,512]{2,1,0:T(8,128)S(1)}, u32[]{:S(2)}, u32[]{:S(2)}) collective-permute-start(f32[9,8,512]{2,1,0:T(8,128)S(1)} %copy-done.3), channel_id=1, source_target_pairs={{0,1},{1,0},{2,3},{3,2},{4,5},{5,4},{6,7},{7,6},{8,9},{9,8},{10,11... | collective-permute-start | bytes 442376 | tf_op jit(solution)/shard_map/ppermute | solution.py:564
  26.2 4.5 %collective-permute-done.across = f32[9,8,512]{2,1,0:T(8,128)S(1)} collective-permute-done((f32[9,8,512]{2,1,0:T(8,128)}, f32[9,8,512]{2,1,0:T(8,128)S(1)}, u32[]{:S(2)}, u32[]{:S(2)}) %collective-permute-start) | collective-permute-done | bytes 147488 | tf_op jit(solution)/shard_map/ppermute | solution.py:563
  30.8 0.0 collective-permute-done.1.beside
  30.8 0.0 all-to-all-done
  30.8 0.0 copy-done
  30.8 0.0 copy-done.1
  30.8 0.0 copy-done.2
  30.8 6.1 %heat.1 = (f32[6,16,512]{2,1,0:T(8,128)}, f32[6,16,512]{2,1,0:T(8,128)S(1)}, f32[16,32,128]{2,1,0:T(8,128)S(1)}) custom-call(s32[1]{0:T(128)} %bitcast.place, s32[3,4,6]{2,1,0:T(4,128)S(1)} %copy-done.2, f32[1]{0:T(128)S(6)} %copy.8.weight, f32[6,16,512]{2,1,0:T(8,128)S(1)} %bitcast.8, f32[6,16,512]{2,1,0:T(8,128)S(1)} %bitcast.12, ...), custom_call_target="tpu_custom_call" | custom-call | tf_op jit(solution)/shard_map/heat/pallas_call | solution.py:569
  36.9 16.4 %all_to_all.19.parts = f32[16,32,128]{2,1,0:T(8,128)S(1)} all-to-all(f32[16,32,128]{2,1,0:T(8,128)S(1)} %get-tuple-element.14), channel_id=1, replica_groups=mesh['member'=16,'tile'=32] {'member'}, dimensions={0} | all-to-all | bytes 524288 | tf_op jit(solution)/shard_map/all_to_all | solution.py:589
  53.4 12.5 %all_to_all.20.parts = f32[16,24,128]{2,1,0:T(8,128)S(1)} all-to-all(f32[16,24,128]{2,1,0:T(8,128)S(1)} %mean.1), channel_id=1, replica_groups=mesh['member'=16,'tile'=32] {'member'}, dimensions={0} | all-to-all | bytes 393216 | tf_op jit(solution)/shard_map/all_to_all | solution.py:598
  65.9 0.8 %update.1 = (f32[6,16,512]{2,1,0:T(8,128)}, f32[6,16,512]{2,1,0:T(8,128)}) custom-call(f32[16,24,128]{2,1,0:T(8,128)S(1)} %all_to_all.20.parts, f32[6,16,512]{2,1,0:T(8,128)S(1)} %bitcast.9, f32[6,16,512]{2,1,0:T(8,128)S(1)} %get-tuple-element.15.marginal), custom_call_target="tpu_custom_call" | custom-call | tf_op jit(solution)/shard_map/update/pallas_call | solution.py:599
  (1 shorter events, 0.0 us)
Async XLA Ops:
  3.7 20.0 %copy-start.3 = (f32[9,8,512]{2,1,0:T(8,128)S(1)}, f32[9,8,512]{2,1,0:T(8,128)}, u32[]{:S(2)}) copy-start(f32[9,8,512]{2,1,0:T(8,128)} %get-tuple-element.12) | copy-start | bytes 442372
  3.7 27.1 %copy-start = (f32[1,6,16,512]{3,2,1,0:T(8,128)S(1)}, f32[1,6,16,512]{3,2,1,0:T(8,128)}, u32[]{:S(2)}) copy-start(f32[1,6,16,512]{3,2,1,0:T(8,128)} %param.5) | copy-start | bytes 589828
  3.7 27.1 %copy-start.1 = (f32[1,6,16,512]{3,2,1,0:T(8,128)S(1)}, f32[1,6,16,512]{3,2,1,0:T(8,128)}, u32[]{:S(2)}) copy-start(f32[1,6,16,512]{3,2,1,0:T(8,128)} %param.4) | copy-start | bytes 589828
  3.7 27.0 %all-to-all-start = ((f32[32,1,2304]{2,1,0:T(1,128)}), f32[32,1,2304]{2,1,0:T(1,128)S(1)}, u32[]{:S(2)}, u32[]{:S(2)}) async-start(f32[32,1,2304]{2,1,0:T(1,128)} %bitcast.13), calls=%async_computation | async-start | bytes 589824 | tf_op jit(solution)/shard_map/all_to_all | solution.py:565
  16.5 14.3 %copy-start.2 = (s32[3,4,6]{2,1,0:T(4,128)S(1)}, s32[3,4,6]{2,1,0:T(4,128)}, u32[]{:S(2)}) copy-start(s32[3,4,6]{2,1,0:T(4,128)} %seams.1) | copy-start | bytes 868
  16.5 14.3 %collective-permute-start = (f32[9,8,512]{2,1,0:T(8,128)}, f32[9,8,512]{2,1,0:T(8,128)S(1)}, u32[]{:S(2)}, u32[]{:S(2)}) collective-permute-start(f32[9,8,512]{2,1,0:T(8,128)} %get-tuple-element.11), channel_id=1, source_target_pairs={{0,31},{1,2},{2,1},{3,4},{4,3},{5,6},{6,5},{7,8},{8,7},{9,10},{10,... | collective-permute-start | bytes 442376 | tf_op jit(solution)/shard_map/ppermute | solution.py:563
  23.7 7.1 %collective-permute-start.1 = (f32[9,8,512]{2,1,0:T(8,128)S(1)}, f32[9,8,512]{2,1,0:T(8,128)S(1)}, u32[]{:S(2)}, u32[]{:S(2)}) collective-permute-start(f32[9,8,512]{2,1,0:T(8,128)S(1)} %copy-done.3), channel_id=1, source_target_pairs={{0,1},{1,0},{2,3},{3,2},{4,5},{5,4},{6,7},{7,6},{8,9},{9,8},{10,11... | collective-permute-start | bytes 442376 | tf_op jit(solution)/shard_map/ppermute | solution.py:564

commit v9 on v8

--- a/solution.py
+++ b/solution.py
@@ -48,8 +48,10 @@
     message[at + 8 : at + 16, :] = jnp.where(lane < 96, t1, pltpu.roll(t2, 64, 1))
     rest = jnp.take_along_axis(t2, 64 + lane % 32, axis=1)
     rest = jnp.where(lane // 32 == sub % 4, rest, 0.0)
-    message[at + 16 : at + 17, :] = jnp.sum(rest[:4], axis=0, keepdims=True)
-    message[at + 17 : at + 18, :] = jnp.sum(rest[4:], axis=0, keepdims=True)
+    rest = rest + pltpu.roll(rest, 1, 0)
+    rest = rest + pltpu.roll(rest, 2, 0)
+    message[at + 16 : at + 17, :] = rest[3:4]
+    message[at + 17 : at + 18, :] = rest[7:8]
 
 
 def get_message(message, p):
@@ -238,14 +240,14 @@
     )
 
 
-def put_weighted(weighted, value, f, i, j):
-    per = 48 // weighted.shape[0]
-    t = 8 * f + 4 * i + j
-    if isinstance(f, int):
-        weighted[t // per, 8 * (t % per) : 8 * (t % per) + 8, :] = value
-    else:
-        at = pl.multiple_of(8 * lax.rem(t, per), 8)
-        weighted[lax.div(t, per), pl.ds(at, 8), :] = value
+CELLS = FACES * ROWS * SIDE // 128
+
+
+def weighted_rows(weighted, f, i, j):
+    share = CELLS // ((weighted.shape[0] - CELLS))
+    t = 8 * (8 * f + 4 * i + j)
+    at = t // share * (share + 1) + t % share
+    return slice(at, at + 8)
 
 
 def heat_kernel(
@@ -264,9 +266,10 @@
     sub = iota((8, 128), 0)
     is_edge = (q == 0) | (q == last)
 
-    per = 48 // weighted.shape[0]
-    for k in range(weighted.shape[0]):
-        weighted[k, 8 * per :, :] = jnp.full((8, 128), share, jnp.float32)
+    members = weighted.shape[0] - CELLS
+    for k in range(1, members + 1):
+        at = k * (CELLS // members + 1) - 1
+        weighted[at : at + 1, :] = jnp.full((1, 128), share, jnp.float32)
 
     lane32 = lane % 32
     tiles = get_message(message, jnp.where(q == 1, last, 0))
@@ -471,7 +474,7 @@
                         at = (f, slice(8 * i, 8 * i + 8), slice(128 * j, 128 * j + 128))
                         m = scaling[at] * v[i + 1][j]
                         marginal[at] = m
-                        put_weighted(weighted, share * jnp.log(m), f, i, j)
+                        weighted[weighted_rows(weighted, f, i, j), :] = share * jnp.log(m)
         x = [work[0, t] for t in range(3)]
         for _ in range(STEPS):
             x = [diffuse_strip(v, where) for v in x]
@@ -491,11 +494,8 @@
                         ref[f, :, columns] = jnp.where(mask, pltpu.roll(value, turn, 1), ref[f, :, columns])
                     moved = pltpu.roll(scaled, turn, 1)
                     for i in range(2):
-                        at = 8 * f + 4 * i + j
-                        rows = slice(8 * (at % per), 8 * (at % per) + 8)
-                        weighted[at // per, rows, :] = jnp.where(
-                            mask[:8], moved[8 * i : 8 * i + 8], weighted[at // per, rows, :]
-                        )
+                        rows = weighted_rows(weighted, f, i, j)
+                        weighted[rows, :] = jnp.where(mask[:8], moved[8 * i : 8 * i + 8], weighted[rows, :])
 
     @pl.when(q == 0)
     def _():
@@ -512,9 +512,9 @@
 
 def mean_kernel(parts, result):
     members, rows = result.shape[0], result.shape[1]
-    total = parts[0]
+    total = parts[: rows + 1, :]
     for k in range(1, members):
-        total = total + parts[k]
+        total = total + parts[k * (rows + 1) : (k + 1) * (rows + 1), :]
     mean = total[:rows] / total[rows : rows + 1]
     value = jnp.exp(mean)
     for k in range(members):
@@ -565,7 +565,7 @@
     message = lax.all_to_all(message.reshape(tiles, PIECE * 128), "tile", 0, 0, tiled=True)
     message = message.reshape(PIECE * tiles, 128)
     rows = 384 // members
-    sums = jax.ShapeDtypeStruct((members, rows + 8, 128), f32)
+    sums = jax.ShapeDtypeStruct((CELLS + members, 128), f32)
     dual, marginal, weighted = pl.pallas_call(
         heat_kernel,
         out_shape=(field, field, sums),
@@ -586,7 +586,8 @@
         compiler_params=params,
         name="heat",
     )(place, seams, member_weights, scaling, density, across, beside, message)
-    weighted = lax.all_to_all(weighted, "member", 0, 0)
+    weighted = lax.all_to_all(weighted.reshape(members, (rows + 1) * 128), "member", 0, 0, tiled=True)
+    weighted = weighted.reshape(CELLS + members, 128)
     means = pl.pallas_call(
         mean_kernel,
         out_shape=jax.ShapeDtypeStruct((members, rows, 128), f32),

time: 67.1 us -> 66.4 us (0.990)
  no operation moved by 1% of the time
where the time goes in v9:
time: 66.4 us; the launch traced here: 66.1 us
  blocking collectives  28.3 us (43%)
  starting transfers between devices  21.8 us (33%)
  Pallas kernels  9.99 us (15%)
  waiting for transfers between devices  4.53 us (7%)
  between operations  1.38 us (2%)
    all_to_all x1, blocking collectives, body(): lax.all_to_all(weighted.reshape(members, (rows + 1) * 128), 'member', 0,...  16 us
    all_to_all x1, starting transfers between devices, body(): lax.all_to_all(message.reshape(tiles, PIECE * 128), 'tile', 0, 0, tiled=T...  12.7 us
    all_to_all x1, blocking collectives, body(): means = lax.all_to_all(means, 'member', 0, 0)  12.4 us
    ppermute x1, starting transfers between devices, body(): lax.ppermute(across, 'tile', [(i, (i + 1 if i % 2 else i - 1) % tiles) fo...  7.15 us
    pallas_call x1, Pallas kernels, body(): pl.pallas_call(heat_kernel, out_shape=(field, field, sums), in_specs=[sme...  6.14 us
    ppermute x1, waiting for transfers between devices, body(): lax.ppermute(across, 'tile', [(i, (i + 1 if i % 2 else i - 1) % tiles) fo...  4.53 us
    pallas_call x1, Pallas kernels, body(): pl.pallas_call(pack_kernel, out_shape=(edge_rows, edge_rows, jax.ShapeDty...  3.04 us
    ppermute x1, starting transfers between devices, body(): beside = lax.ppermute(beside, 'tile', [(i, i ^ 1) for i in range(tiles)])  1.92 us
  transfers between devices with their start and end apart: 3, of which 1 were waited for; matrix products, arithmetic and copies ran while one was open for 0% of the time, Pallas kernels for 0%

profile of v9, /device:TPU:8, one launch (start us, length us, event | category | flops | bytes accessed | tf_op | source)
XLA Modules:
  0.0 66.1 jit_solution(14001834269850856706)
XLA Ops:
  0.6 3.0 %pack.1 = (f32[9,8,512]{2,1,0:T(8,128)}, f32[9,8,512]{2,1,0:T(8,128)}, f32[576,128]{1,0:T(8,128)}) custom-call(s32[1]{0:T(128)} %bitcast.place, s32[3,4,6]{2,1,0:T(4,128)} %seams.1, f32[6,16,512]{2,1,0:T(8,128)} %bitcast.9, f32[6,16,512]{2,1,0:T(8,128)} %bitcast.14), custom_call_target="tpu_custom_call" | custom-call | tf_op jit(solution)/shard_map/pack/pallas_call | solution.py:550
  3.7 0.0 copy-start.3
  3.7 0.0 copy-start
  3.7 0.0 copy-start.1
  3.7 12.7 %all-to-all-start = ((f32[32,1,2304]{2,1,0:T(1,128)}), f32[32,1,2304]{2,1,0:T(1,128)S(1)}, u32[]{:S(2)}, u32[]{:S(2)}) async-start(f32[32,1,2304]{2,1,0:T(1,128)} %bitcast.17), calls=%async_computation | async-start | bytes 589824 | tf_op jit(solution)/shard_map/all_to_all | solution.py:565
  16.5 0.0 copy-start.2
  16.5 7.2 %collective-permute-start = (f32[9,8,512]{2,1,0:T(8,128)}, f32[9,8,512]{2,1,0:T(8,128)S(1)}, u32[]{:S(2)}, u32[]{:S(2)}) collective-permute-start(f32[9,8,512]{2,1,0:T(8,128)} %get-tuple-element.11), channel_id=1, source_target_pairs={{0,31},{1,2},{2,1},{3,4},{4,3},{5,6},{6,5},{7,8},{8,7},{9,10},{10,... | collective-permute-start | bytes 442376 | tf_op jit(solution)/shard_map/ppermute | solution.py:563
  23.6 0.0 copy-done.3
  23.7 1.9 %collective-permute-start.1 = (f32[9,8,512]{2,1,0:T(8,128)S(1)}, f32[9,8,512]{2,1,0:T(8,128)S(1)}, u32[]{:S(2)}, u32[]{:S(2)}) collective-permute-start(f32[9,8,512]{2,1,0:T(8,128)S(1)} %copy-done.3), channel_id=1, source_target_pairs={{0,1},{1,0},{2,3},{3,2},{4,5},{5,4},{6,7},{7,6},{8,9},{9,8},{10,11... | collective-permute-start | bytes 442376 | tf_op jit(solution)/shard_map/ppermute | solution.py:564
  26.2 4.5 %collective-permute-done.across = f32[9,8,512]{2,1,0:T(8,128)S(1)} collective-permute-done((f32[9,8,512]{2,1,0:T(8,128)}, f32[9,8,512]{2,1,0:T(8,128)S(1)}, u32[]{:S(2)}, u32[]{:S(2)}) %collective-permute-start) | collective-permute-done | bytes 147488 | tf_op jit(solution)/shard_map/ppermute | solution.py:563
  30.8 0.0 collective-permute-done.1.beside
  30.8 0.0 all-to-all-done
  30.8 0.0 copy-done
  30.8 0.0 copy-done.1
  30.8 0.0 copy-done.2
  30.8 6.1 %heat.1 = (f32[6,16,512]{2,1,0:T(8,128)}, f32[6,16,512]{2,1,0:T(8,128)S(1)}, f32[400,128]{1,0:T(8,128)S(1)}) custom-call(s32[1]{0:T(128)} %bitcast.place, s32[3,4,6]{2,1,0:T(4,128)S(1)} %copy-done.2, f32[1]{0:T(128)S(6)} %copy.9.weight, f32[6,16,512]{2,1,0:T(8,128)S(1)} %bitcast.10, f32[6,16,512]{2,1,0:T(8,128)S(1)} %bitcast.15, ...), custom_call_target="tpu_custom_call" | custom-call | tf_op jit(solution)/shard_map/heat/pallas_call | solution.py:569
  36.9 16.0 %all_to_all.23 = f32[16,1,3200]{2,1,0:T(1,128)S(1)} all-to-all(f32[16,1,3200]{2,1,0:T(1,128)S(1)} %bitcast.16), channel_id=1, replica_groups=mesh['member'=16,'tile'=32] {'member'}, dimensions={0} | all-to-all | bytes 409600 | tf_op jit(solution)/shard_map/all_to_all | solution.py:589
  52.9 12.4 %all_to_all.24.parts = f32[16,24,128]{2,1,0:T(8,128)S(1)} all-to-all(f32[16,24,128]{2,1,0:T(8,128)S(1)} %mean.1), channel_id=1, replica_groups=mesh['member'=16,'tile'=32] {'member'}, dimensions={0} | all-to-all | bytes 393216 | tf_op jit(solution)/shard_map/all_to_all | solution.py:599
  65.3 0.8 %update.1 = (f32[6,16,512]{2,1,0:T(8,128)}, f32[6,16,512]{2,1,0:T(8,128)}) custom-call(f32[16,24,128]{2,1,0:T(8,128)S(1)} %all_to_all.24.parts, f32[6,16,512]{2,1,0:T(8,128)S(1)} %bitcast.11, f32[6,16,512]{2,1,0:T(8,128)S(1)} %get-tuple-element.15.marginal), custom_call_target="tpu_custom_call" | custom-call | tf_op jit(solution)/shard_map/update/pallas_call | solution.py:600
  (1 shorter events, 0.0 us)
Async XLA Ops:
  3.7 20.0 %copy-start.3 = (f32[9,8,512]{2,1,0:T(8,128)S(1)}, f32[9,8,512]{2,1,0:T(8,128)}, u32[]{:S(2)}) copy-start(f32[9,8,512]{2,1,0:T(8,128)} %get-tuple-element.12) | copy-start | bytes 442372
  3.7 27.1 %copy-start = (f32[1,6,16,512]{3,2,1,0:T(8,128)S(1)}, f32[1,6,16,512]{3,2,1,0:T(8,128)}, u32[]{:S(2)}) copy-start(f32[1,6,16,512]{3,2,1,0:T(8,128)} %param.5) | copy-start | bytes 589828
  3.7 27.1 %copy-start.1 = (f32[1,6,16,512]{3,2,1,0:T(8,128)S(1)}, f32[1,6,16,512]{3,2,1,0:T(8,128)}, u32[]{:S(2)}) copy-start(f32[1,6,16,512]{3,2,1,0:T(8,128)} %param.4) | copy-start | bytes 589828
  3.7 27.0 %all-to-all-start = ((f32[32,1,2304]{2,1,0:T(1,128)}), f32[32,1,2304]{2,1,0:T(1,128)S(1)}, u32[]{:S(2)}, u32[]{:S(2)}) async-start(f32[32,1,2304]{2,1,0:T(1,128)} %bitcast.17), calls=%async_computation | async-start | bytes 589824 | tf_op jit(solution)/shard_map/all_to_all | solution.py:565
  16.5 14.3 %copy-start.2 = (s32[3,4,6]{2,1,0:T(4,128)S(1)}, s32[3,4,6]{2,1,0:T(4,128)}, u32[]{:S(2)}) copy-start(s32[3,4,6]{2,1,0:T(4,128)} %seams.1) | copy-start | bytes 868
  16.5 14.3 %collective-permute-start = (f32[9,8,512]{2,1,0:T(8,128)}, f32[9,8,512]{2,1,0:T(8,128)S(1)}, u32[]{:S(2)}, u32[]{:S(2)}) collective-permute-start(f32[9,8,512]{2,1,0:T(8,128)} %get-tuple-element.11), channel_id=1, source_target_pairs={{0,31},{1,2},{2,1},{3,4},{4,3},{5,6},{6,5},{7,8},{8,7},{9,10},{10,... | collective-permute-start | bytes 442376 | tf_op jit(solution)/shard_map/ppermute | solution.py:563
  23.7 7.1 %collective-permute-start.1 = (f32[9,8,512]{2,1,0:T(8,128)S(1)}, f32[9,8,512]{2,1,0:T(8,128)S(1)}, u32[]{:S(2)}, u32[]{:S(2)}) collective-permute-start(f32[9,8,512]{2,1,0:T(8,128)S(1)} %copy-done.3), channel_id=1, source_target_pairs={{0,1},{1,0},{2,3},{3,2},{4,5},{5,4},{6,7},{7,6},{8,9},{9,8},{10,11... | collective-permute-start | bytes 442376 | tf_op jit(solution)/shard_map/ppermute | solution.py:564
